TPU v7x, 32 devices: a whole 2x2x4 slice. The times are simulated.
32 devices in a mesh: batch: 4 (over x, core), seq: 8 (over z, y).
Axes of the slice: x: 2, y: 2, z: 4, core: 2. Of those that a mesh axis runs over, the one named last changes fastest.
Arguments:
- block_input: bfloat16 [8, 1024, 1024], P('batch', 'seq'), may hold values from -6 to 6
- doc_lengths: int32 [8, 8], P('batch'), may hold values from 0 to 1024, as said below
- out_grad: bfloat16 [8, 1024, 1024], P('batch', 'seq'), may hold values from -6 to 6
- joined_weight: bfloat16 [1024, 3072], replicated, may hold values from -0.1875 to 0.1875
- proj_weight: bfloat16 [1024, 1024], replicated, may hold values from -0.75 to 0.75
- expand_weight: bfloat16 [1024, 4096], replicated, may hold values from -0.1875 to 0.1875
- shrink_weight: bfloat16 [4096, 1024], replicated, may hold values from -0.09375 to 0.09375
- joined_left: bfloat16 [1024, 128], replicated, may hold values from -0.1875 to 0.1875
- joined_right: bfloat16 [128, 3072], replicated, may hold values from -0.5 to 0.5
- proj_left: bfloat16 [1024, 128], replicated, may hold values from -0.75 to 0.75
- proj_right: bfloat16 [128, 1024], replicated, may hold values from -0.5 to 0.5
- expand_left: bfloat16 [1024, 128], replicated, may hold values from -0.1875 to 0.1875
- expand_right: bfloat16 [128, 4096], replicated, may hold values from -0.5 to 0.5
- shrink_left: bfloat16 [4096, 128], replicated, may hold values from -0.09375 to 0.09375
- shrink_right: bfloat16 [128, 1024], replicated, may hold values from -0.5 to 0.5
- mixer_gain: float32 [1024], replicated, may hold values from 0.5 to 1.5
- mixer_shift: float32 [1024], replicated, may hold values from -3 to 3
- feed_gain: float32 [1024], replicated, may hold values from 0.5 to 1.5
- feed_shift: float32 [1024], replicated, may hold values from -3 to 3
Outputs:
- output: bfloat16 [8, 1024, 1024], P('batch', 'seq')
- input_grad: bfloat16 [8, 1024, 1024], P('batch', 'seq')
- grad_joined_left: float32 [1024, 128], replicated
- grad_joined_right: float32 [128, 3072], replicated
- grad_proj_left: float32 [1024, 128], replicated
- grad_proj_right: float32 [128, 1024], replicated
- grad_expand_left: float32 [1024, 128], replicated
- grad_expand_right: float32 [128, 4096], replicated
- grad_shrink_left: float32 [4096, 128], replicated
- grad_shrink_right: float32 [128, 1024], replicated
- grad_mixer_gain: float32 [1024], replicated
- grad_mixer_shift: float32 [1024], replicated
- grad_feed_gain: float32 [1024], replicated
- grad_feed_shift: float32 [1024], replicated
Inputs may be any that keep to these rules, and one draw needn't show every extreme that they name: `doc_lengths`: each row's lengths add up to 1024; zero entries are empty documents. In every aligned group of 2 rows, one row holds a document that begins before slot 128 and ends after slot 896.
All inputs are finite; a program needn't handle non-finite values.
Results may differ from a plain program's by a relative error of at most 0.029.
Values may be sent and summed in bfloat16 or wider, within the bound.
No kernel may reach another device: no remote copies, remote signals or barrier semaphores. Data moves between devices by JAX's collectives and lax.ppermute only.
A program may use at most 320 MiB of HBM per device.

v0:
```python
from functools import partial

import jax
import jax.numpy as jnp
from jax import lax
from jax.sharding import PartitionSpec as P

D = 1024
HEADS = 16
HEAD_DIM = 64
ROT_DIM = 16


EPSILON = 1e-05
SCALING = 0.25
NEGATIVE = -1e30


def layer_norm(values, gain_vector, shift_vector):
    average = jnp.mean(values, axis=-1, keepdims=True)
    centred = values - average
    spread = jnp.mean(centred * centred, axis=-1, keepdims=True)
    return centred * lax.rsqrt(spread + EPSILON) * gain_vector + shift_vector


def times_transposed(left_side, right_side):
    return lax.dot_general(
        left_side, right_side, (((1,), (1,)), ((), ())), preferred_element_type=jnp.float32
    )


def transposed_times(left_side, right_side):
    return lax.dot_general(
        left_side, right_side, (((0,), (0,)), ((), ())), preferred_element_type=jnp.float32
    )


def adapted(inputs, frozen, left_factor, right_factor):
    low_rank = jnp.dot(inputs, left_factor, preferred_element_type=jnp.float32).astype(jnp.bfloat16)
    result = jnp.dot(inputs, frozen, preferred_element_type=jnp.float32)
    result = result + SCALING * jnp.dot(low_rank, right_factor, preferred_element_type=jnp.float32)
    return (result, low_rank)


def adapted_back(inputs, low_rank, incoming, frozen, left_factor, right_factor):
    rank_grad = (SCALING * times_transposed(incoming, right_factor)).astype(jnp.bfloat16)
    grad_right = SCALING * transposed_times(low_rank, incoming)
    grad_left = transposed_times(inputs, rank_grad)
    grad_inputs = times_transposed(incoming, frozen) + times_transposed(rank_grad, left_factor)
    return (grad_inputs, grad_left, grad_right)


def document_info(doc_lengths, places):
    endings = jnp.cumsum(doc_lengths, axis=1)
    passed = places[:, :, None] >= endings[:, None, :]
    segment = jnp.sum(passed.astype(jnp.int32), axis=2)
    begins = jnp.sum(jnp.where(passed, doc_lengths[:, None, :], 0), axis=2)
    return (segment, places - begins)


def rotate(head_values, offsets, direction):
    halfway = ROT_DIM // 2
    frequency = 10000.0 ** (-2.0 * jnp.arange(halfway, dtype=jnp.float32) / ROT_DIM)
    angles = offsets.astype(jnp.float32)[..., None] * frequency
    cosine = jnp.cos(angles)[..., None, :]
    sine_part = direction * jnp.sin(angles)[..., None, :]
    former = head_values[..., :halfway]
    latter = head_values[..., halfway:ROT_DIM]
    return jnp.concatenate(
        [
            former * cosine - latter * sine_part,
            latter * cosine + former * sine_part,
            head_values[..., ROT_DIM:],
        ],
        axis=-1,
    )


def per_device(
    block_input,
    doc_lengths,
    out_grad,
    joined_weight,
    proj_weight,
    expand_weight,
    shrink_weight,
    joined_left,
    joined_right,
    proj_left,
    proj_right,
    expand_left,
    expand_right,
    shrink_left,
    shrink_right,
    mixer_gain,
    mixer_shift,
    feed_gain,
    feed_shift,
):
    row_count, slot_count = (block_input.shape[0], block_input.shape[1])
    tokens = row_count * slot_count
    inputs = block_input.astype(jnp.float32).reshape(tokens, D)
    mixer_in, mixer_pull = jax.vjp(layer_norm, inputs, mixer_gain, mixer_shift)
    feed_in, feed_pull = jax.vjp(layer_norm, inputs, feed_gain, feed_shift)
    mixer_low = mixer_in.astype(jnp.bfloat16)
    feed_low = feed_in.astype(jnp.bfloat16)
    joined_out, joined_rank = adapted(mixer_low, joined_weight, joined_left, joined_right)

    def block_places(first_row, width_now):
        return first_row + lax.broadcasted_iota(jnp.int32, (row_count, width_now), 1)

    places = block_places(lax.axis_index("seq") * slot_count, slot_count)
    segment, offsets = document_info(doc_lengths, places)
    split_heads = joined_out.reshape(row_count, slot_count, 3, HEADS, HEAD_DIM)
    query_heads = rotate(split_heads[:, :, 0], offsets, 1.0).astype(jnp.bfloat16)
    key_heads = rotate(split_heads[:, :, 1], offsets, 1.0).astype(jnp.bfloat16)
    value_heads = split_heads[:, :, 2].astype(jnp.bfloat16)

    def allowed_pairs(query_places, query_segment, key_places, key_segment):
        same = query_segment[:, :, None] == key_segment[:, None, :]
        return (same & (key_places[:, None, :] <= query_places[:, :, None]))[:, None]

    def block_scores(query_part, key_part, allowed):
        scores = (
            jnp.einsum("rqhd,rkhd->rhqk", query_part, key_part, preferred_element_type=jnp.float32)
            * 0.125
        )
        return jnp.where(allowed, scores, NEGATIVE)

    initial = (
        jnp.full((row_count, HEADS, slot_count), NEGATIVE, jnp.float32),
        jnp.zeros((row_count, HEADS, slot_count), jnp.float32),
        jnp.zeros((row_count, slot_count, HEADS, HEAD_DIM), jnp.float32),
    )
    key_part = lax.all_gather(key_heads, "seq", axis=1, tiled=True)
    value_part = lax.all_gather(value_heads, "seq", axis=1, tiled=True)
    key_count = key_part.shape[1]
    key_places = block_places(jnp.int32(0), key_count)
    key_segment, ignored = document_info(doc_lengths, key_places)
    allowed = allowed_pairs(places, segment, key_places, key_segment)

    def attend(current):
        row_max, row_sum, weighted = current
        scores = block_scores(query_heads, key_part, allowed)
        new_max = jnp.maximum(row_max, jnp.max(scores, axis=-1))
        weights = jnp.where(allowed, jnp.exp(scores - new_max[..., None]), 0.0)
        row_sum = jnp.sum(weights, axis=-1)
        weighted = jnp.einsum(
            "rhqk,rkhd->rqhd",
            weights.astype(jnp.bfloat16),
            value_part,
            preferred_element_type=jnp.float32,
        )
        return (new_max, row_sum, weighted)

    row_max, row_sum, weighted = lax.cond(
        jnp.any(allowed), attend, lambda current: current, initial
    )
    log_total = row_max + jnp.log(row_sum)
    attention = weighted / jnp.transpose(row_sum, (0, 2, 1))[..., None]
    attended = attention.astype(jnp.bfloat16).reshape(tokens, D)
    projected, proj_rank = adapted(attended, proj_weight, proj_left, proj_right)
    expanded, expand_rank = adapted(feed_low, expand_weight, expand_left, expand_right)
    activated, gelu_pull = jax.vjp(partial(jax.nn.gelu, approximate=False), expanded)
    act_low = activated.astype(jnp.bfloat16)
    shrunk, shrink_rank = adapted(act_low, shrink_weight, shrink_left, shrink_right)
    output = (inputs + projected + shrunk).astype(jnp.bfloat16).reshape(row_count, slot_count, D)
    incoming = out_grad.reshape(tokens, D)
    grad_act, grad_shrink_left, grad_shrink_right = adapted_back(
        act_low, shrink_rank, incoming, shrink_weight, shrink_left, shrink_right
    )
    grad_expanded = gelu_pull(grad_act)[0].astype(jnp.bfloat16)
    grad_feed, grad_expand_left, grad_expand_right = adapted_back(
        feed_low, expand_rank, grad_expanded, expand_weight, expand_left, expand_right
    )
    grad_attended, grad_proj_left, grad_proj_right = adapted_back(
        attended, proj_rank, incoming, proj_weight, proj_left, proj_right
    )
    grad_heads = grad_attended.astype(jnp.bfloat16).reshape(row_count, slot_count, HEADS, HEAD_DIM)
    delta_rows = jnp.sum(grad_heads.astype(jnp.float32) * attention, axis=-1)
    delta_heads = jnp.transpose(delta_rows, (0, 2, 1))
    log_rows = jnp.transpose(log_total, (0, 2, 1))
    empty_heads = jnp.zeros((row_count, slot_count, HEADS, HEAD_DIM), jnp.float32)
    query_key_part = lax.all_gather(key_heads, "seq", axis=1, tiled=True)
    query_value_part = lax.all_gather(value_heads, "seq", axis=1, tiled=True)
    key_count = query_key_part.shape[1]
    key_places = block_places(jnp.int32(0), key_count)
    key_segment, ignored = document_info(doc_lengths, key_places)
    query_allowed = allowed_pairs(places, segment, key_places, key_segment)

    def query_accumulate(current):
        scores = block_scores(query_heads, query_key_part, query_allowed)
        probabilities = jnp.where(query_allowed, jnp.exp(scores - log_total[..., None]), 0.0)
        grad_probs = jnp.einsum(
            "rqhd,rkhd->rhqk", grad_heads, query_value_part, preferred_element_type=jnp.float32
        )
        grad_scores = (probabilities * (grad_probs - delta_heads[..., None])).astype(jnp.bfloat16)
        return 0.125 * jnp.einsum(
            "rhqk,rkhd->rqhd", grad_scores, query_key_part, preferred_element_type=jnp.float32
        )

    grad_query = lax.cond(
        jnp.any(query_allowed), query_accumulate, lambda current: current, empty_heads
    )
    log_whole, delta_whole = (
        lax.all_gather(log_rows.astype(jnp.bfloat16), "seq", axis=1, tiled=True).astype(
            log_rows.dtype
        ),
        lax.all_gather(delta_rows.astype(jnp.bfloat16), "seq", axis=1, tiled=True).astype(
            delta_rows.dtype
        ),
    )
    query_part = lax.all_gather(query_heads, "seq", axis=1, tiled=True)
    grad_part = lax.all_gather(grad_heads, "seq", axis=1, tiled=True)
    query_count = query_part.shape[1]
    query_places = block_places(jnp.int32(0), query_count)
    query_segment, ignored = document_info(doc_lengths, query_places)
    key_allowed = allowed_pairs(query_places, query_segment, places, segment)
    log_part = jnp.transpose(log_whole, (0, 2, 1))
    delta_part = jnp.transpose(delta_whole, (0, 2, 1))

    def key_accumulate(current):
        scores = block_scores(query_part, key_heads, key_allowed)
        probabilities = jnp.where(key_allowed, jnp.exp(scores - log_part[..., None]), 0.0)
        grad_value = jnp.einsum(
            "rhqk,rqhd->rkhd",
            probabilities.astype(jnp.bfloat16),
            grad_part,
            preferred_element_type=jnp.float32,
        )
        grad_probs = jnp.einsum(
            "rqhd,rkhd->rhqk", grad_part, value_heads, preferred_element_type=jnp.float32
        )
        grad_scores = (probabilities * (grad_probs - delta_part[..., None])).astype(jnp.bfloat16)
        grad_key = 0.125 * jnp.einsum(
            "rhqk,rqhd->rkhd", grad_scores, query_part, preferred_element_type=jnp.float32
        )
        return (grad_key, grad_value)

    grad_key, grad_value = lax.cond(
        jnp.any(key_allowed), key_accumulate, lambda current: current, (empty_heads, empty_heads)
    )
    grad_joined = jnp.stack(
        [rotate(grad_query, offsets, -1.0), rotate(grad_key, offsets, -1.0), grad_value], axis=2
    )
    grad_joined = grad_joined.reshape(tokens, 3 * D).astype(jnp.bfloat16)
    grad_mixer, grad_joined_left, grad_joined_right = adapted_back(
        mixer_low, joined_rank, grad_joined, joined_weight, joined_left, joined_right
    )
    grad_inputs_mix, grad_mixer_gain, grad_mixer_shift = mixer_pull(grad_mixer)
    grad_inputs_feed, grad_feed_gain, grad_feed_shift = feed_pull(grad_feed)
    input_grad = (
        (incoming.astype(jnp.float32) + grad_inputs_mix + grad_inputs_feed)
        .astype(jnp.bfloat16)
        .reshape(row_count, slot_count, D)
    )
    summed = lax.psum(
        (
            grad_joined_left,
            grad_joined_right,
            grad_proj_left,
            grad_proj_right,
            grad_expand_left,
            grad_expand_right,
            grad_shrink_left,
            grad_shrink_right,
            grad_mixer_gain,
            grad_mixer_shift,
            grad_feed_gain,
            grad_feed_shift,
        ),
        ("batch", "seq"),
    )
    return (output, input_grad) + tuple(summed)


def solution(mesh):
    return jax.shard_map(
        per_device,
        mesh=mesh,
        in_specs=(
            P("batch", "seq", None),
            P("batch", None),
            P("batch", "seq", None),
            P(),
            P(),
            P(),
            P(),
            P(),
            P(),
            P(),
            P(),
            P(),
            P(),
            P(),
            P(),
            P(),
            P(),
            P(),
            P(),
        ),
        out_specs=(
            P("batch", "seq", None),
            P("batch", "seq", None),
            P(),
            P(),
            P(),
            P(),
            P(),
            P(),
            P(),
            P(),
            P(),
            P(),
            P(),
            P(),
        ),
        check_vma=False,
    )
```

profile of v0, /device:TPU:0, one launch (start us, length us, event | category | flops | bytes accessed | tf_op | source)
XLA Modules:
  0.0 647.6 jit_solution(8669051708804617982)
XLA Ops:
  7.3 1.3 convert_reduce_fusion
  8.6 1.3 multiply_reduce_fusion.5
  10.5 1.4 add_convert_fusion.2
  12.0 1.4 convolution_convert_fusion.3
  13.4 4.6 fusion.125
  18.1 2.2 fusion.74
  20.3 3.5 copy.129
  23.8 5.2 reshape.185
  29.1 3.1 fusion.122
  32.4 1.8 copy_bitcast_fusion
  36.6 2.5 slice.119
  39.1 1.2 slice.121
  42.4 1.1 fusion.85
  43.5 2.0 copy.135
  45.5 2.0 reshape.189
  48.7 2.2 fusion.99
  52.2 1.4 convolution_convert_fusion.1
  53.7 5.9 fusion.126
  59.9 2.4 fusion.129
  62.3 11.7 %multiply_convert_fusion.12 = (bf16[256,4096]{1,0:T(8,128)(2,1)S(1)}, f32[256,4096]{1,0:T(8,128)S(1)}, f32[256,4096]{1,0:T(8,128)S(1)}) fusion(f32[256,4096]{1,0:T(8,128)S(1)} %fusion.126, bf16[256,128]{1,0:T(8,128)(2,1)S(1)} %convolution_convert_fusion.1, bf16[128,4096]{1,0:T(8,128)(2,1)S(1)} %copy-done.21), kind=kOutput, calls=%fused_computation.54 | convolution fusion | flops 338690048 | bytes 15794176 | tf_op jit(solution)/shard_map/dot_general | solution.py:41
  74.0 2.3 add_convert_fusion
  77.0 1.2 fusion.132
  80.6 2.5 slice_bitcast_fusion
  83.0 1.8 convolution_multiply_fusion.1
  84.8 2.1 fusion.133
  86.9 3.4 fusion.130
  90.3 24.2 %all-gather.6.cloned.1.call-done = bf16[2,1024,16,64]{1,3,2,0:T(8,128)(2,1)} async-done(((bf16[2,128,16,64]{1,3,2,0:T(8,128)(2,1)}), bf16[2,1024,16,64]{1,3,2,0:T(8,128)(2,1)}) %all-gather.6.cloned.1.call-update) | async-done | bytes 4194320 | tf_op jit(solution)/shard_map/all_gather | solution.py:135
  114.5 106.5 %all-gather.12.cloned.1.call-done = bf16[2,1024,1,16,64]{1,0,4,3,2:T(2,128)(2,1)} async-done(((bf16[2,128,1,16,64]{1,0,4,3,2:T(2,128)(2,1)}), bf16[2,1024,1,16,64]{1,0,4,3,2:T(2,128)(2,1)}) %all-gather.12.cloned.1.call-update) | async-done | bytes 4194320 | tf_op jit(solution)/shard_map/all_gather | solution.py:136
  221.0 24.8 %conditional.3 = (f32[2,16,128]{2,1,0:T(8,128)}, f32[2,16,128]{2,1,0:T(8,128)}, f32[2,16,128]{2,1,0:T(8,128)S(1)}, f32[2,128,16,64]{1,0,3,2:T(2,128)}) conditional(s32[]{:T(128)} %convert_element_type.121, () %tuple.48, (pred[2,1,128,1024]{3,2,0,1:T(8,128)(4,1)S(1)}, bf16[2,128,16,64]{1,3,2,0:T(8,128)(2,1)}, bf16[2,1024,16,64]{1,3,2,0:T(8,128)(2,1)}, ...), branch_computations={%region_7.8_spmd, %region_8.11_spmd} | conditional | flops 1128263680 | bytes 65405016 | solution.py:156
  221.9 5.2 fusion
  227.7 6.4 fusion.2
  234.9 7.9 %fusion.7 = f32[2,128,16,64]{1,3,2,0:T(8,128)} fusion(bf16[2,1024,16,64]{1,0,3,2:T(2,128)(2,1)} %get-tuple-element.198, f32[2,16,128,1024]{3,2,1,0:T(8,128)S(1)} %get-tuple-element.247, f32[2,16,128]{2,1,0:T(8,128)} %broadcast_maximum_fusion, pred[2,128,1024]{2,1,0:T(8,128)(4,1)} %bitcast.186), kind=kOutput, calls=%fused_computation.8 | convolution fusion | flops 557842432 | bytes 22298624 | tf_op jit(solution)/shard_map/cond/branch_1_fun/rhqk,rkhd->rqhd/dot_general | solution.py:148
  242.8 3.0 copy.144
  246.6 2.2 multiply_reduce_fusion.4
  249.5 1.3 convert_bitcast_fusion.2
  250.8 29.6 %conditional.4 = (f32[2,128,16,8]{1,3,2,0:T(8,128)S(1)}, f32[2,128,16,8]{1,3,2,0:T(8,128)S(1)}, bf16[2,128,16,48]{1,3,2,0:T(8,128)(2,1)}) conditional(s32[]{:T(128)} %convert_element_type.121, () %tuple.50, (pred[2,1,128,1024]{3,2,0,1:T(8,128)(4,1)}, bf16[2,128,16,64]{1,3,2,0:T(8,128)(2,1)}, bf16[2,1024,16,64]{1,3,2,0:T(8,128)(2,1)}, ...), branch_computations={%region_12.13_spmd, %region_13.14_spmd} | conditional | flops 1640235008 | bytes 50987088 | solution.py:202
  251.0 10.7 %fusion.123 = f32[2,16,128,1024]{3,2,1,0:T(8,128)} fusion(bf16[2,128,16,64]{1,3,2,0:T(8,128)(2,1)} %get-tuple-element.78, bf16[2,1024,16,64]{1,3,2,0:T(8,128)(2,1)} %get-tuple-element.79), kind=kOutput, calls=%fused_computation.183 | convolution fusion | flops 536870912 | bytes 21495808 | tf_op jit(solution)/shard_map/cond/branch_1_fun/rqhd,rkhd->rhqk/dot_general | solution.py:125
  261.8 15.8 %fusion.24 = f32[2,128,16,64]{1,3,2,0:T(8,128)} fusion(bf16[2,1024,16,64]{1,3,2,0:T(8,128)(2,1)} %get-tuple-element.79, f32[2,16,128,1024]{3,2,1,0:T(8,128)} %fusion.123, f32[2,16,128]{2,1,0:T(8,128)S(1)} %copy.138, f32[2,16,128]{2,1,0:T(8,128)S(1)} %copy-done.60, pred[2,128,1024]{2,1,0:T(8,128)(4,1)S(1)} %bitcast.188, ...), kind=kOutput, calls=%fused_computation.19 | convolution fusion | flops 1103364096 | bytes 27033600 | tf_op jit(solution)/shard_map/cond/branch_1_fun/rhqk,rkhd->rqhd/dot_general | solution.py:198
  278.5 1.9 slice.117
  280.5 29.7 %all_gather.23 = bf16[2,1024,16]{1,2,0:T(8,128)(2,1)S(1)} all-gather(bf16[2,128,16]{1,2,0:T(8,128)(2,1)} %get-tuple-element.242), channel_id=1, replica_groups=mesh['batch'=4,'seq'=8] {'seq'}, dimensions={1}, use_global_device_ids=true | all-gather | bytes 73728 | tf_op jit(solution)/shard_map/all_gather | solution.py:206
  310.2 17.2 %all_gather.25 = bf16[2,1024,16]{1,0,2:T(2,128)(2,1)S(1)} all-gather(bf16[2,128,16]{1,0,2:T(2,128)(2,1)} %convert_element_type.140), channel_id=1, replica_groups=mesh['batch'=4,'seq'=8] {'seq'}, dimensions={1}, use_global_device_ids=true | all-gather | bytes 73728 | tf_op jit(solution)/shard_map/all_gather | solution.py:209
  328.8 77.6 %all-gather.10.cloned.1.call-done = bf16[2,1024,16,64]{1,0,3,2:T(2,128)(2,1)} async-done(((bf16[2,128,16,64]{1,0,3,2:T(2,128)(2,1)}), bf16[2,1024,16,64]{1,0,3,2:T(2,128)(2,1)}) %all-gather.10.cloned.1.call-update) | async-done | bytes 4194320 | tf_op jit(solution)/shard_map/all_gather | solution.py:214
  406.4 30.2 %conditional.5 = (f32[2,128,16,8]{1,3,2,0:T(8,128)S(1)}, f32[2,128,16,8]{1,3,2,0:T(8,128)S(1)}, bf16[2,128,16,48]{1,3,2,0:T(8,128)(2,1)S(1)}, bf16[2,128,1,16,64]{1,4,3,0,2:T(8,128)(2,1)S(1)}) conditional(s32[]{:T(128)} %convert_element_type.137, () %tuple.52, (pred[2,1,1024,128]{3,2,0,1:T(8,128)(4,1)}, bf16[2,1024,16,64]{1,3,2,0:T(8,128)(2,1)}, ...), branch_computations={%region_15.16_spmd, %region_16.17_spmd} | conditional | flops 2198339584 | bytes 109969584 | solution.py:240
  406.7 4.4 fusion.124
  411.2 13.5 %multiply_convert_fusion.15 = bf16[2,16,1024,128]{3,2,1,0:T(8,128)(2,1)S(1)} fusion(f32[2,16,1024,128]{3,2,1,0:T(8,128)S(1)} %fusion.124, f32[2,16,1024]{2,1,0:T(8,128)S(1)} %copy.141, f32[2,16,1024]{2,1,0:T(8,128)S(1)} %copy-done.51, pred[2,1024,128]{2,1,0:T(8,128)(4,1)S(1)} %bitcast.191, ...), kind=kOutput, calls=%fused_computation.25.clone.clone.clone.clone.clone.clone.1 | convolution fusion | flops 566231040 | bytes 30408704 | tf_op jit(solution)/shard_map/cond/branch_1_fun/rqhd,rkhd->rhqk/dot_general | solution.py:231
  424.8 1.6 fusion.46
  426.5 9.9 %fusion.54 = bf16[2,128,1,16,64]{1,4,3,0,2:T(8,128)(2,1)S(1)} fusion(f32[2,16,1024,128]{3,2,1,0:T(8,128)S(1)} %fusion.124, f32[2,16,1024]{2,1,0:T(8,128)S(1)} %copy-done.51, pred[2,1024,128]{2,1,0:T(8,128)(4,1)S(1)} %bitcast.192, bf16[2,1024,16,64]{1,0,3,2:T(2,128)(2,1)} %get-tuple-element.210), kind=kOutput, calls=%fused_computation.38 | convolution fusion | flops 558104576 | bytes 21889024 | tf_op jit(solution)/shard_map/cond/branch_1_fun/rhqk,rqhd->rkhd/dot_general | solution.py:225
  437.7 1.1 maximum_bitcast_fusion
  439.1 1.6 copy.142
  441.4 1.9 convolution_multiply_fusion.3
  444.7 1.2 fusion.131
  447.9 1.5 convolution_add_fusion.1
  449.5 8.8 %fusion.127 = f32[256,1024]{1,0:T(8,128)} fusion(bf16[256,4096]{1,0:T(8,128)(2,1)} %copy-done.4, bf16[4096,1024]{1,0:T(8,128)(2,1)} %param.31), kind=kOutput, calls=%fused_computation.187 | convolution fusion | flops 2147483648 | bytes 11534336 | tf_op jit(solution)/shard_map/dot_general | solution.py:40
  458.3 4.9 fusion.78
  463.3 1.2 fusion.117
  464.5 1.5 multiply_reduce_fusion
  466.1 41.8 %all-reduce = (f32[1024]{0:T(1024)}, f32[1024]{0:T(1024)}, f32[1024]{0:T(1024)}, f32[1024]{0:T(1024)}) all-reduce(f32[1024]{0:T(1024)} %get-tuple-element.223, f32[1024]{0:T(1024)} %get-tuple-element.220, f32[1024]{0:T(1024)S(1)} %get-tuple-element.214, f32[1024]{0:T(1024)} %get-tuple-element.261), channel_id=1, replica_groups=mesh['batch'=4,'seq'=8] {'batch','seq'}, use_global_device_ids=true, to_apply=%region_30.31 | all-reduce | flops 4096 | bytes 32768 | tf_op jit(solution)/shard_map/psum | solution.py:257
  509.4 1.9 fusion.103
  512.8 1.5 add_convert_fusion.1
  514.3 115.6 %all-reduce.4.cloned.1.call-done = (f32[1024,128]{1,0:T(8,128)}, f32[128,3072]{1,0:T(8,128)}, f32[1024,128]{1,0:T(8,128)}, f32[128,1024]{1,0:T(8,128)}, f32[1024...) async-done(((f32[1024,128]{1,0:T(8,128)}, f32[128,3072]{1,0:T(8,128)}, f32[1024,128]{1,0:T(8,128)}, f32[128,1024]{1,0:T(8,128)}, ...) | async-done | bytes 8388624 | tf_op jit(solution)/shard_map/psum | solution.py:257
  629.9 2.0 copy.245
  631.9 2.7 copy.246
  637.0 1.3 copy.250
  638.4 1.3 copy.251
  (211 shorter events, 27.2 us)
Async XLA Ops:
  7.2 34.4 %copy-start = (bf16[1024,1024]{1,0:T(8,128)(2,1)S(1)}, bf16[1024,1024]{1,0:T(8,128)(2,1)}, u32[]{:S(2)}) copy-start(bf16[1024,1024]{1,0:T(8,128)(2,1)} %param.29) | copy-start | bytes 6291460
  7.2 107.3 %all-gather.6.cloned.1.call-start = ((), (), s32[]{:S(2)}) async-start(), calls=%async_computation | async-start | bytes 4718592 | tf_op jit(solution)/shard_map/all_gather | solution.py:135
  8.6 3.4 copy-start.58
  11.9 6.1 copy-start.12
  13.4 4.7 copy-start.32
  13.4 4.7 copy-start.30
  23.8 8.3 %copy-start.70 = (s32[2,8]{1,0:T(2,128)S(1)}, s32[2,8]{1,0:T(2,128)}, u32[]{:S(2)}) copy-start(s32[2,8]{1,0:T(2,128)} %param.26) | copy-start | bytes 196
  34.3 7.0 %copy-start.3 = (bf16[2,128,1024]{2,1,0:T(8,128)(2,1)S(1)}, bf16[2,128,1024]{2,1,0:T(8,128)(2,1)}, u32[]{:S(2)}) copy-start(bf16[2,128,1024]{2,1,0:T(8,128)(2,1)} %param.27) | copy-start | bytes 1572868
  34.3 7.0 %copy-start.26 = (bf16[128,1024]{1,0:T(8,128)(2,1)S(1)}, bf16[128,1024]{1,0:T(8,128)(2,1)}, u32[]{:S(2)}) copy-start(bf16[128,1024]{1,0:T(8,128)(2,1)} %param.35) | copy-start | bytes 786436
  36.6 184.5 %all-gather.12.cloned.1.call-start = ((), (), s32[]{:S(2)}) async-start(), calls=%async_computation.3 | async-start | bytes 4718592 | tf_op jit(solution)/shard_map/all_gather | solution.py:136
  39.1 289.7 %all-gather.8.cloned.1.call-start = ((), (), s32[]{:S(2)}) async-start(), calls=%async_computation.1 | async-start | bytes 4718592 | tf_op jit(solution)/shard_map/all_gather | solution.py:213
  41.2 365.1 %all-gather.10.cloned.1.call-start = ((), (), s32[]{:S(2)}) async-start(), calls=%async_computation.2 | async-start | bytes 4718592 | tf_op jit(solution)/shard_map/all_gather | solution.py:214
  47.6 582.4 %all-reduce.4.cloned.1.call-start = ((), (), s32[]{:S(2)}) async-start(), calls=%async_computation.4 | async-start | bytes 16777216 | tf_op jit(solution)/shard_map/psum | solution.py:257
  48.7 172.3 %copy-start.15 = (pred[2,1,128,1024]{3,2,0,1:T(8,128)(4,1)}, pred[2,1,128,1024]{3,2,0,1:T(8,128)(4,1)S(1)}, u32[]{:S(2)}) copy-start(pred[2,1,128,1024]{3,2,0,1:T(8,128)(4,1)S(1)} %get-tuple-element.272) | copy-start | bytes 786436
  52.2 7.6 %slice-start.2 = ((s8[8388608]{0:T(1024)(128)(4,1)}), s8[4194304]{0:T(1024)(128)(4,1)S(1)}, s32[]{:S(2)}) async-start(s8[8388608]{0:T(1024)(128)(4,1)} %bitcast.196), calls=%async_computation.7 | async-start | bytes 8388608
  53.6 5.9 copy-start.28
  53.6 6.2 slice-start.3
  62.3 11.7 %copy-start.22 = (bf16[4096,128]{1,0:T(8,128)(2,1)S(1)}, bf16[4096,128]{1,0:T(8,128)(2,1)}, u32[]{:S(2)}) copy-start(bf16[4096,128]{1,0:T(8,128)(2,1)} %param.38) | copy-start | bytes 3145732
  74.0 10.8 %copy-start.4 = (bf16[256,4096]{1,0:T(8,128)(2,1)}, bf16[256,4096]{1,0:T(8,128)(2,1)S(1)}, u32[]{:S(2)}) copy-start(bf16[256,4096]{1,0:T(8,128)(2,1)S(1)} %get-tuple-element.244) | copy-start | bytes 6291460
  78.2 8.7 %slice-start = ((s8[8388608]{0:T(1024)(128)(4,1)}), s8[4194304]{0:T(1024)(128)(4,1)S(1)}, s32[]{:S(2)}) async-start(s8[8388608]{0:T(1024)(128)(4,1)} %bitcast.194), calls=%async_computation.5 | async-start | bytes 8388608
  83.0 3.9 slice-start.1
  221.9 5.8 copy-start.17
  248.8 194.8 %copy-start.11 = (bf16[2,128,16,64]{1,0,3,2:T(2,128)(2,1)}, bf16[2,128,16,64]{1,0,3,2:T(2,128)(2,1)S(1)}, u32[]{:S(2)}) copy-start(bf16[2,128,16,64]{1,0,3,2:T(2,128)(2,1)S(1)} %get-tuple-element.241) | copy-start | bytes 1572868
  251.0 10.7 %copy-start.18 = (pred[2,1,128,1024]{3,2,0,1:T(8,128)(4,1)S(1)}, pred[2,1,128,1024]{3,2,0,1:T(8,128)(4,1)}, u32[]{:S(2)}) copy-start(pred[2,1,128,1024]{3,2,0,1:T(8,128)(4,1)} %get-tuple-element.77) | copy-start | bytes 786436 | tf_op jit(solution)/shard_map/cond
  251.0 10.7 %copy-start.60 = (f32[2,16,128]{2,1,0:T(8,128)S(1)}, f32[2,16,128]{2,1,0:T(8,128)}, u32[]{:S(2)}) copy-start(f32[2,16,128]{2,1,0:T(8,128)} %get-tuple-element.80) | copy-start | bytes 49156 | tf_op jit(solution)/shard_map/cond
  280.5 125.9 %copy-start.40 = (f32[2,128,16,8]{1,3,2,0:T(8,128)}, f32[2,128,16,8]{1,3,2,0:T(8,128)S(1)}, u32[]{:S(2)}) copy-start(f32[2,128,16,8]{1,3,2,0:T(8,128)S(1)} %get-tuple-element.120) | copy-start | bytes 393220
  280.5 125.9 %copy-start.41 = (f32[2,128,16,8]{1,3,2,0:T(8,128)}, f32[2,128,16,8]{1,3,2,0:T(8,128)S(1)}, u32[]{:S(2)}) copy-start(f32[2,128,16,8]{1,3,2,0:T(8,128)S(1)} %get-tuple-element.121) | copy-start | bytes 393220
  406.4 30.3 %copy-start.53 = (f32[2,128,8]{1,2,0:T(8,128)S(1)}, f32[2,128,8]{1,2,0:T(8,128)}, u32[]{:S(2)}) copy-start(f32[2,128,8]{1,2,0:T(8,128)} %copy-done.52) | copy-start | bytes 24580
  406.4 30.3 %copy-start.57 = (f32[2,128,8]{1,2,0:T(8,128)S(1)}, f32[2,128,8]{1,2,0:T(8,128)}, u32[]{:S(2)}) copy-start(f32[2,128,8]{1,2,0:T(8,128)} %get-tuple-element.274) | copy-start | bytes 24580
  406.7 4.5 copy-start.47
  406.7 4.5 copy-start.42
  406.7 4.5 copy-start.48
  406.7 4.5 copy-start.51
  411.2 13.5 %copy-start.1 = (bf16[2,1024,16,64]{1,3,2,0:T(8,128)(2,1)S(1)}, bf16[2,1024,16,64]{1,3,2,0:T(8,128)(2,1)}, u32[]{:S(2)}) copy-start(bf16[2,1024,16,64]{1,3,2,0:T(8,128)(2,1)} %get-tuple-element.85) | copy-start | bytes 12582916 | tf_op jit(solution)/shard_map/cond
  437.7 3.1 copy-start.31
  438.9 2.5 copy-start.33
  439.1 4.2 copy-start.50
  440.7 5.2 copy-start.9
  440.8 2.9 copy-start.39
  440.8 4.0 copy-start.13
  449.4 15.1 %copy-start.5 = (f32[256,1024]{1,0:T(8,128)}, f32[256,1024]{1,0:T(8,128)S(1)}, u32[]{:S(2)}) copy-start(f32[256,1024]{1,0:T(8,128)S(1)} %convolution_add_fusion.1) | copy-start | bytes 3145732
  449.4 8.8 %copy-start.10 = (bf16[2,128,3,16,64]{1,0,4,3,2:T(2,128)(2,1)S(1)}, bf16[2,128,3,16,64]{1,0,4,3,2:T(2,128)(2,1)}, u32[]{:S(2)}) copy-start(bf16[2,128,3,16,64]{1,0,4,3,2:T(2,128)(2,1)} %copy-done.9) | copy-start | bytes 4718596
  458.2 4.9 copy-start.2
  458.2 5.0 copy-start.25
  458.2 5.0 copy-start.55
  458.3 5.0 copy-start.56
  458.3 5.0 copy-start.59
  458.3 6.2 copy-start.65
  458.3 6.2 copy-start.62
  463.2 48.1 %copy-start.27 = (bf16[128,1024]{1,0:T(8,128)(2,1)S(1)}, bf16[128,1024]{1,0:T(8,128)(2,1)}, u32[]{:S(2)}) copy-start(bf16[128,1024]{1,0:T(8,128)(2,1)} %param.35) | copy-start | bytes 786436
  464.5 47.1 %copy-start.35 = (bf16[256,128]{1,0:T(8,128)(2,1)S(1)}, bf16[256,128]{1,0:T(8,128)(2,1)}, u32[]{:S(2)}) copy-start(bf16[256,128]{1,0:T(8,128)(2,1)} %copy-done.34) | copy-start | bytes 196612
  507.9 3.7 copy-start.23
  507.9 3.7 copy-start.29
  509.4 3.4 copy-start.6
  509.4 3.4 copy-start.8
  509.4 3.4 copy-start.63
  509.4 3.4 copy-start.67
  509.4 3.4 copy-start.69
  629.9 4.7 copy-start.46
  629.9 5.5 copy-start.45
  629.9 6.3 copy-start.44
  629.9 7.1 %copy-start.20 = (f32[128,4096]{1,0:T(8,128)S(1)}, f32[128,4096]{1,0:T(8,128)}, u32[]{:S(2)}) copy-start(f32[128,4096]{1,0:T(8,128)} %get-tuple-element.314) | copy-start | bytes 6291460
  634.6 3.7 copy-start.19
  637.0 2.6 copy-start.43
  (16 other events, 17.8 us)
Sparse Core Ops, SparseCore 0:
  36.7 77.7 all-gather.5
  117.1 103.8 all-gather.11
  223.6 74.9 all-gather.7
  301.1 105.2 all-gather.9
  447.1 182.7 all-reduce.3
where the time goes:
time: 654 us; the launch traced here: 648 us
  waiting for transfers between devices  324 us (50%)
  matrix products  140 us (21%)
  blocking collectives  88.8 us (14%)
  local copies, waits for them, and re-layouts  47.2 us (7%)
  other arithmetic  29.8 us (5%)
  between operations  16.5 us (3%)
    psum x1, waiting for transfers between devices, per_device(): lax.psum((grad_joined_left, grad_joined_right, grad_proj_left, grad_proj_...  116 us
    all_gather x1, waiting for transfers between devices, per_device(): value_part = lax.all_gather(value_heads, 'seq', axis=1, tiled=True)  107 us
    all_gather x1, waiting for transfers between devices, per_device(): grad_part = lax.all_gather(grad_heads, 'seq', axis=1, tiled=True)  77.6 us
    psum x1, blocking collectives, per_device(): lax.psum((grad_joined_left, grad_joined_right, grad_proj_left, grad_proj_...  41.8 us
    all_gather x1, blocking collectives, per_device(): lax.all_gather(log_rows.astype(jnp.bfloat16), 'seq', axis=1, tiled=True)  29.7 us
    all_gather x1, waiting for transfers between devices, per_device(): key_part = lax.all_gather(key_heads, 'seq', axis=1, tiled=True)  24.2 us
    dot_general x4, matrix products, adapted(): result = jnp.dot(inputs, frozen, preferred_element_type=jnp.float32)  21.2 us
    dot_general x3, matrix products, block_scores(): jnp.einsum('rqhd,rkhd->rhqk', query_part, key_part, preferred_element_typ...  20.4 us
  transfers between devices with their start and end apart: 5, of which 4 were waited for; matrix products, arithmetic and copies ran while one was open for 21% of the time, Pallas kernels for 0%

commit v1 on v0

v1 whole, which is shorter than its diff:
```python
from functools import partial

import jax
import jax.numpy as jnp
from jax import lax
from jax.experimental import pallas as pl
from jax.experimental.pallas import tpu as pltpu
from jax.sharding import PartitionSpec as P

D = 1024
FF = 4096
HEADS = 16
HEAD_DIM = 64
ROT_DIM = 16
RANK = 128
PAIR = 128
PAIRS = 8

EPSILON = 1e-05
SCALING = 0.25
NEGATIVE = -1e30
BF = jnp.bfloat16
F32 = jnp.float32
MIB = 1024 * 1024

AT_EXPAND_LEFT = 0
AT_EXPAND_RIGHT = D
AT_SHRINK_LEFT = D + FF
AT_SHRINK_RIGHT = D + 2 * FF
FEED_ROWS = 2 * D + 2 * FF
AT_JOINED_LEFT = 0
AT_JOINED_RIGHT = D
AT_PROJ_LEFT = 4 * D
AT_PROJ_RIGHT = 5 * D
AT_NORMS = 6 * D
LATE_ROWS = 6 * D + 512


def nn(left, right):
    return lax.dot_general(left, right, (((1,), (0,)), ((), ())), preferred_element_type=F32)


def nt(left, right):
    return lax.dot_general(left, right, (((1,), (1,)), ((), ())), preferred_element_type=F32)


def tn(left, right):
    return lax.dot_general(left, right, (((0,), (0,)), ((), ())), preferred_element_type=F32)


def normalised(values):
    average = jnp.mean(values, axis=-1, keepdims=True)
    centred = values - average
    spread = jnp.mean(centred * centred, axis=-1, keepdims=True)
    scale = lax.rsqrt(spread + EPSILON)
    return centred * scale, scale


def turn(values, cosine, sine):
    lane = lax.broadcasted_iota(jnp.int32, values.shape, 1) % HEAD_DIM
    half = ROT_DIM // 2
    partner = jnp.where(lane < half, pltpu.roll(values, PAIR - half, 1), pltpu.roll(values, half, 1))
    return values * cosine + partner * sine


def project_kernel(
    x_ref, g_ref, wq_ref, wk_ref, wv_ref, wp_ref, lj_ref, rq_ref, rk_ref, rv_ref, lp_ref, rp_ref,
    gain_ref, shift_ref, cos_ref, sin_ref, msg_ref, low_ref, rank_ref, u_ref,
):
    @pl.when(pl.program_id(0) == 0)
    def _():
        hat, _ = normalised(x_ref[...].astype(F32))
        u_ref[...] = (hat * gain_ref[...] + shift_ref[...]).astype(BF)
        low_ref[...] = nn(u_ref[...], lj_ref[...]).astype(BF)
        rank_ref[...] = (SCALING * nt(g_ref[...], rp_ref[...])).astype(BF)

    u, low = u_ref[...], low_ref[...]
    cosine, sine = cos_ref[...], sin_ref[...]
    query = nn(u, wq_ref[...]) + SCALING * nn(low, rq_ref[...])
    key = nn(u, wk_ref[...]) + SCALING * nn(low, rk_ref[...])
    value = nn(u, wv_ref[...]) + SCALING * nn(low, rv_ref[...])
    grad = nt(g_ref[...], wp_ref[...]) + nt(rank_ref[...], lp_ref[...])
    rows, slots = msg_ref.shape[1], msg_ref.shape[3]
    for pair in range(msg_ref.shape[0]):
        columns = slice(pair * PAIR, (pair + 1) * PAIR)
        parts = (
            turn(query[:, columns], cosine, sine),
            turn(key[:, columns], cosine, sine),
            value[:, columns],
            grad[:, columns],
        )
        for place, part in enumerate(parts):
            part = part.astype(BF)
            for row in range(rows):
                msg_ref[pair, row, place] = part[row * slots : (row + 1) * slots]


def project(x, g, joined_weight, proj_weight, joined_left, joined_right, proj_left, proj_right,
            gain, shift, cosine, sine, rows):
    tokens = x.shape[0]
    slots = tokens // rows
    width = 256
    steps = D // width
    per = width // PAIR
    whole = lambda shape: pl.BlockSpec(shape, lambda j: (0,) * len(shape))
    column = lambda depth, first: pl.BlockSpec((depth, width), lambda j: (0, first + j))
    return pl.pallas_call(
        project_kernel,
        grid=(steps,),
        in_specs=[
            whole((tokens, D)), whole((tokens, D)),
            column(D, 0), column(D, steps), column(D, 2 * steps),
            pl.BlockSpec((width, D), lambda j: (j, 0)),
            whole((D, RANK)),
            column(RANK, 0), column(RANK, steps), column(RANK, 2 * steps),
            pl.BlockSpec((width, RANK), lambda j: (j, 0)),
            whole((RANK, D)),
            whole((1, D)), whole((1, D)),
            whole((tokens, PAIR)), whole((tokens, PAIR)),
        ],
        out_specs=[
            pl.BlockSpec((per, rows, 4, slots, PAIR), lambda j: (j, 0, 0, 0, 0)),
            whole((tokens, RANK)), whole((tokens, RANK)),
        ],
        out_shape=[
            jax.ShapeDtypeStruct((PAIRS, rows, 4, slots, PAIR), BF),
            jax.ShapeDtypeStruct((tokens, RANK), BF),
            jax.ShapeDtypeStruct((tokens, RANK), BF),
        ],
        scratch_shapes=[pltpu.VMEM((tokens, D), BF)],
        compiler_params=pltpu.CompilerParams(vmem_limit_bytes=24 * MIB),
        cost_estimate=pl.CostEstimate(flops=2 * tokens * D * 5 * D, bytes_accessed=12 * MIB, transcendentals=0),
        name="project",
    )(
        x, g, joined_weight, joined_weight, joined_weight, proj_weight, joined_left,
        joined_right, joined_right, joined_right, proj_left, proj_right, gain, shift, cosine, sine,
    )


def feed_kernel(
    x_ref, g_ref, we_ref, ws_ref, le_ref, re_ref, ls_ref, rs_ref, gain_ref, shift_ref,
    shrunk_ref, gfeed_ref, pack_ref, f_ref, lowe_ref, ranks_ref, lows_ref, ranke_ref,
):
    step = pl.program_id(0)
    width = we_ref.shape[1]

    @pl.when(step == 0)
    def _():
        hat, _ = normalised(x_ref[...].astype(F32))
        f_ref[...] = (hat * gain_ref[...] + shift_ref[...]).astype(BF)
        lowe_ref[...] = nn(f_ref[...], le_ref[...]).astype(BF)
        ranks_ref[...] = (SCALING * nt(g_ref[...], rs_ref[...])).astype(BF)
        lows_ref[...] = jnp.zeros_like(lows_ref)
        ranke_ref[...] = jnp.zeros_like(ranke_ref)
        shrunk_ref[...] = jnp.zeros_like(shrunk_ref)
        gfeed_ref[...] = jnp.zeros_like(gfeed_ref)

    g, f, ranks = g_ref[...], f_ref[...], ranks_ref[...]
    expanded = nn(f, we_ref[...]) + SCALING * nn(lowe_ref[...], re_ref[...])
    bell = 0.5 * (1.0 + lax.erf(expanded * 0.7071067811865476))
    act = (expanded * bell).astype(BF)
    slope = bell + expanded * (0.3989422804014327 * jnp.exp(-0.5 * expanded * expanded))
    lows_ref[...] += nn(act, ls_ref[...])
    shrunk_ref[...] += nn(act, ws_ref[...])
    grad_act = nt(g, ws_ref[...]) + nt(ranks, ls_ref[...])
    grad_expanded = (grad_act * slope).astype(BF)
    gfeed_ref[...] += nt(grad_expanded, we_ref[...])
    ranke_ref[...] += nt(grad_expanded, re_ref[...])
    grad_right = SCALING * tn(lowe_ref[...], grad_expanded)
    for block in range(width // RANK):
        at = pl.multiple_of(AT_EXPAND_RIGHT + step * width + block * RANK, RANK)
        pack_ref[pl.ds(at, RANK), :] = grad_right[:, block * RANK : (block + 1) * RANK].astype(BF)
    at = pl.multiple_of(AT_SHRINK_LEFT + step * width, RANK)
    pack_ref[pl.ds(at, width), :] = tn(act, ranks).astype(BF)

    @pl.when(step == pl.num_programs(0) - 1)
    def _():
        low = lows_ref[...].astype(BF)
        shrunk_ref[...] += SCALING * nn(low, rs_ref[...])
        grad_last = SCALING * tn(low, g)
        for block in range(D // RANK):
            at = AT_SHRINK_RIGHT + block * RANK
            pack_ref[at : at + RANK, :] = grad_last[:, block * RANK : (block + 1) * RANK].astype(BF)
        ranke = (SCALING * ranke_ref[...]).astype(BF)
        gfeed_ref[...] += nt(ranke, le_ref[...])
        pack_ref[AT_EXPAND_LEFT : AT_EXPAND_LEFT + D, :] = tn(f, ranke).astype(BF)


def feed(x, g, expand_weight, shrink_weight, expand_left, expand_right, shrink_left, shrink_right, gain, shift):
    tokens = x.shape[0]
    width = 512
    whole = lambda shape: pl.BlockSpec(shape, lambda j: (0,) * len(shape))
    return pl.pallas_call(
        feed_kernel,
        grid=(FF // width,),
        in_specs=[
            whole((tokens, D)), whole((tokens, D)),
            pl.BlockSpec((D, width), lambda j: (0, j)),
            pl.BlockSpec((width, D), lambda j: (j, 0)),
            whole((D, RANK)),
            pl.BlockSpec((RANK, width), lambda j: (0, j)),
            pl.BlockSpec((width, RANK), lambda j: (j, 0)),
            whole((RANK, D)), whole((1, D)), whole((1, D)),
        ],
        out_specs=[whole((tokens, D)), whole((tokens, D)), whole((FEED_ROWS, RANK))],
        out_shape=[
            jax.ShapeDtypeStruct((tokens, D), F32),
            jax.ShapeDtypeStruct((tokens, D), F32),
            jax.ShapeDtypeStruct((FEED_ROWS, RANK), BF),
        ],
        scratch_shapes=[
            pltpu.VMEM((tokens, D), BF),
            pltpu.VMEM((tokens, RANK), BF), pltpu.VMEM((tokens, RANK), BF),
            pltpu.VMEM((tokens, RANK), F32), pltpu.VMEM((tokens, RANK), F32),
        ],
        compiler_params=pltpu.CompilerParams(vmem_limit_bytes=36 * MIB),
        cost_estimate=pl.CostEstimate(flops=2 * tokens * D * FF * 5, bytes_accessed=24 * MIB, transcendentals=2 * tokens * FF),
        name="feed",
    )(x, g, expand_weight, shrink_weight, expand_left, expand_right, shrink_left, shrink_right, gain, shift)


def attend_kernel(msg_ref, start_ref, cos_ref, sin_ref, out_ref, vt_ref, kt_ref, dk_ref, dv_ref):
    count, _, _, slots, _ = msg_ref.shape
    length = count * slots
    keys = msg_ref[:, 0, 1].reshape(length, PAIR)
    values = msg_ref[:, 0, 2].reshape(length, PAIR)
    kt_ref[...] = keys.T
    vt_ref[...] = values.T
    dk_ref[...] = jnp.zeros_like(dk_ref)
    dv_ref[...] = jnp.zeros_like(dv_ref)
    first_head = lax.broadcasted_iota(jnp.int32, (slots, PAIR), 1) < HEAD_DIM
    none = jnp.zeros((slots, PAIR), BF)

    def both(part):
        return jnp.concatenate([jnp.where(first_head, part, none), jnp.where(first_head, none, part)], axis=0)

    for block in range(count):
        seen = (block + 1) * slots
        query = both(msg_ref[block, 0, 0] * BF(0.125))
        grad = both(msg_ref[block, 0, 3])
        query_t, grad_t = query.T, grad.T
        start = start_ref[0, :, block * slots : (block + 1) * slots]
        start = jnp.concatenate([start, start], axis=1)
        place = block * slots + lax.broadcasted_iota(jnp.int32, (1, slots), 1)
        place = jnp.concatenate([place, place], axis=1)
        scores = nn(keys[:seen], query_t)
        key_place = lax.broadcasted_iota(jnp.int32, scores.shape, 0)
        scores = jnp.where((key_place >= start) & (key_place <= place), scores, NEGATIVE)
        top = jnp.max(scores, axis=0, keepdims=True)
        weights = jnp.exp(scores - top)
        probabilities = weights * (1.0 / jnp.sum(weights, axis=0, keepdims=True))
        low = probabilities.astype(BF)
        out_t = nn(vt_ref[:, :seen], low)
        delta = jnp.sum(out_t * grad_t.astype(F32), axis=0, keepdims=True)
        grad_probs = nn(values[:seen], grad_t)
        grad_scores = (probabilities * (grad_probs - delta)).astype(BF)
        dv_ref[:seen] += nn(low, grad)
        dk_ref[:seen] += nn(grad_scores, query)
        query_grad_t = nn(kt_ref[:, :seen], grad_scores)

        def merge(both_t):
            return jnp.concatenate([both_t[:HEAD_DIM, :slots], both_t[HEAD_DIM:, slots:]], axis=0).T

        cosine = cos_ref[0, block * slots : (block + 1) * slots]
        sine = sin_ref[0, block * slots : (block + 1) * slots]
        out_ref[block, 0, 0] = merge(out_t).astype(BF)
        out_ref[block, 0, 1] = turn(0.125 * merge(query_grad_t), cosine, -sine).astype(BF)
    for block in range(count):
        here = slice(block * slots, (block + 1) * slots)
        out_ref[block, 0, 2] = turn(dk_ref[here], cos_ref[0, here], -sin_ref[0, here]).astype(BF)
        out_ref[block, 0, 3] = dv_ref[here].astype(BF)


def attend(message, starts, cosine, sine):
    count, rows, _, slots, _ = message.shape
    length = count * slots
    block = pl.BlockSpec((count, 1, 4, slots, PAIR), lambda r: (0, r, 0, 0, 0))
    table = pl.BlockSpec((1, length, PAIR), lambda r: (r, 0, 0))
    return pl.pallas_call(
        attend_kernel,
        grid=(rows,),
        in_specs=[block, pl.BlockSpec((1, 1, length), lambda r: (r, 0, 0)), table, table],
        out_specs=block,
        out_shape=jax.ShapeDtypeStruct(message.shape, BF),
        scratch_shapes=[
            pltpu.VMEM((PAIR, length), BF), pltpu.VMEM((PAIR, length), BF),
            pltpu.VMEM((length, PAIR), F32), pltpu.VMEM((length, PAIR), F32),
        ],
        compiler_params=pltpu.CompilerParams(vmem_limit_bytes=40 * MIB),
        cost_estimate=pl.CostEstimate(
            flops=rows * length * length * PAIR * 12, bytes_accessed=8 * MIB, transcendentals=rows * length * length
        ),
        name="attend",
    )(message, starts, cosine, sine)


def finish_kernel(
    msg_ref, x_ref, g_ref, shrunk_ref, gfeed_ref, wp_ref, lp_ref, rp_ref, rankp_ref,
    wj_ref, lj_ref, rj_ref, lowj_ref, mgain_ref, mshift_ref, fgain_ref,
    out_ref, igrad_ref, pack_ref,
):
    pairs, rows, _, slots, _ = msg_ref.shape
    tokens = rows * slots

    def gather(place):
        return jnp.concatenate([msg_ref[pair, :, place].reshape(tokens, PAIR) for pair in range(pairs)], axis=1)

    x = x_ref[...].astype(F32)
    g = g_ref[...]
    hat, scale = normalised(x)
    u = (hat * mgain_ref[...] + mshift_ref[...]).astype(BF)

    def put_right(first, matrix):
        for block in range(matrix.shape[1] // RANK):
            at = first + block * RANK
            pack_ref[at : at + RANK, :] = matrix[:, block * RANK : (block + 1) * RANK].astype(BF)

    joined = jnp.concatenate([gather(1), gather(2), gather(3)], axis=1)
    rank = (SCALING * nt(joined, rj_ref[...])).astype(BF)
    pack_ref[AT_JOINED_LEFT : AT_JOINED_LEFT + D, :] = tn(u, rank).astype(BF)
    put_right(AT_JOINED_RIGHT, SCALING * tn(lowj_ref[...], joined))
    grad_mixer = nt(joined, wj_ref[...]) + nt(rank, lj_ref[...])
    grad_feed = gfeed_ref[...]
    mixer_hat, feed_hat = grad_mixer * hat, grad_feed * hat
    sums = [jnp.sum(v, axis=0, keepdims=True) for v in (mixer_hat, grad_mixer, feed_hat, grad_feed)]
    pieces = [v[:, c * RANK : (c + 1) * RANK] for v in sums for c in range(D // RANK)]
    pack_ref[AT_NORMS : AT_NORMS + 32, :] = jnp.concatenate(pieces, axis=0).astype(BF)
    pack_ref[AT_NORMS + 32 :, :] = jnp.zeros((LATE_ROWS - AT_NORMS - 32, RANK), BF)
    pulled = grad_mixer * mgain_ref[...] + grad_feed * fgain_ref[...]
    along = jnp.mean(pulled * hat, axis=-1, keepdims=True)
    level = jnp.mean(pulled, axis=-1, keepdims=True)
    igrad_ref[...] = (g.astype(F32) + scale * (pulled - level - hat * along)).astype(BF)

    attended = gather(0)
    low = nn(attended, lp_ref[...]).astype(BF)
    projected = nn(attended, wp_ref[...]) + SCALING * nn(low, rp_ref[...])
    out_ref[...] = (x + projected + shrunk_ref[...]).astype(BF)
    pack_ref[AT_PROJ_LEFT : AT_PROJ_LEFT + D, :] = tn(attended, rankp_ref[...]).astype(BF)
    put_right(AT_PROJ_RIGHT, SCALING * tn(low, g))


def finish(message, x, g, shrunk, grad_feed, proj_weight, proj_left, proj_right, rank_proj,
           joined_weight, joined_left, joined_right, low_joined, mixer_gain, mixer_shift, feed_gain):
    tokens = x.shape[0]
    return pl.pallas_call(
        finish_kernel,
        out_shape=[
            jax.ShapeDtypeStruct((tokens, D), BF),
            jax.ShapeDtypeStruct((tokens, D), BF),
            jax.ShapeDtypeStruct((LATE_ROWS, RANK), BF),
        ],
        compiler_params=pltpu.CompilerParams(vmem_limit_bytes=40 * MIB),
        cost_estimate=pl.CostEstimate(flops=2 * tokens * D * 6 * D, bytes_accessed=16 * MIB, transcendentals=0),
        name="finish",
    )(message, x, g, shrunk, grad_feed, proj_weight, proj_left, proj_right, rank_proj,
      joined_weight, joined_left, joined_right, low_joined, mixer_gain, mixer_shift, feed_gain)


def swap(part, bit, size):
    return lax.ppermute(part, ("batch", "seq"), [(i, i ^ bit) for i in range(size)])


def add_low(left, right):
    return (left.astype(F32) + right.astype(F32)).astype(BF)


def summed(packed, order, size):
    me = lax.axis_index("batch") * lax.axis_size("seq") + lax.axis_index("seq")
    for bit in order:
        mine = jnp.where((me & bit) == 0, 0, 1)
        halves = packed.reshape(2, packed.shape[0] // 2, RANK)
        away = lax.dynamic_index_in_dim(halves, 1 - mine, 0, keepdims=False)
        keep = lax.dynamic_index_in_dim(halves, mine, 0, keepdims=False)
        packed = add_low(keep, swap(away, bit, size))
    for bit in reversed(order):
        other = swap(packed, bit, size)
        packed = jnp.where(
            (me & bit) == 0, jnp.concatenate([packed, other]), jnp.concatenate([other, packed])
        )
    return packed


def rows_of(packed, first, count):
    return packed[first : first + count].astype(F32)


def columns_of(packed, first, count):
    blocks = packed[first : first + count].reshape(count // RANK, RANK, RANK)
    return jnp.transpose(blocks, (1, 0, 2)).reshape(RANK, count).astype(F32)


def document_offsets(doc_lengths, places):
    endings = jnp.cumsum(doc_lengths, axis=1)
    passed = places[:, :, None] >= endings[:, None, :]
    begins = jnp.sum(jnp.where(passed, doc_lengths[:, None, :], 0), axis=2)
    return places - begins


def tables(offsets):
    half = ROT_DIM // 2
    frequency = 10000.0 ** (-2.0 * jnp.arange(half, dtype=F32) / ROT_DIM)
    lane = jnp.arange(PAIR) % HEAD_DIM
    per_lane = jnp.where(lane < ROT_DIM, frequency[lane % half], 0.0)
    sign = jnp.where(lane < half, -1.0, jnp.where(lane < ROT_DIM, 1.0, 0.0))
    angles = offsets.astype(F32)[..., None] * per_lane
    return jnp.cos(angles), jnp.sin(angles) * sign


def per_device(
    block_input, doc_lengths, out_grad, joined_weight, proj_weight, expand_weight, shrink_weight,
    joined_left, joined_right, proj_left, proj_right, expand_left, expand_right, shrink_left,
    shrink_right, mixer_gain, mixer_shift, feed_gain, feed_shift,
):
    rows, slots = block_input.shape[:2]
    tokens = rows * slots
    devices, batches = lax.axis_size("seq"), lax.axis_size("batch")
    size = devices * batches
    me = lax.axis_index("seq")
    length = devices * slots
    x = block_input.reshape(tokens, D)
    g = out_grad.reshape(tokens, D)
    mixer_gain, mixer_shift = mixer_gain.reshape(1, D), mixer_shift.reshape(1, D)
    feed_gain, feed_shift = feed_gain.reshape(1, D), feed_shift.reshape(1, D)

    places = me * slots + lax.broadcasted_iota(jnp.int32, (rows, slots), 1)
    cosine, sine = tables(document_offsets(doc_lengths, places))
    message, low_joined, rank_proj = project(
        x, g, joined_weight, proj_weight, joined_left, joined_right, proj_left, proj_right,
        mixer_gain, mixer_shift, cosine.reshape(tokens, PAIR), sine.reshape(tokens, PAIR), rows,
    )

    pair_parts = min(devices, PAIRS)
    row_parts = min(devices // pair_parts, rows)
    head_parts = devices // (pair_parts * row_parts)
    my_rows = rows // row_parts
    lanes = PAIR // head_parts

    def send(units):
        if row_parts * head_parts > 1:
            units = units.reshape(PAIRS, row_parts, my_rows, 4, slots, head_parts, lanes)
            units = jnp.transpose(units, (0, 1, 5, 2, 3, 4, 6))
        units = units.reshape(devices, PAIRS // pair_parts, my_rows, 4, slots, lanes)[:, 0]
        return lax.all_to_all(units, "seq", 0, 0, tiled=True)

    def send_back(units):
        units = lax.all_to_all(units[..., :lanes], "seq", 0, 0, tiled=True)
        if row_parts * head_parts > 1:
            units = units.reshape(PAIRS, row_parts, head_parts, my_rows, 4, slots, lanes)
            units = jnp.transpose(units, (0, 1, 3, 4, 5, 2, 6))
        return units.reshape(PAIRS, rows, 4, slots, PAIR)

    arrived = send(message)
    if lanes < PAIR:
        arrived = jnp.pad(arrived, ((0, 0),) * 4 + ((0, PAIR - lanes),))

    shrunk, grad_feed, feed_pack = feed(
        x, g, expand_weight, shrink_weight, expand_left, expand_right, shrink_left, shrink_right,
        feed_gain, feed_shift,
    )

    whole_places = lax.broadcasted_iota(jnp.int32, (rows, length), 1)
    whole_offsets = document_offsets(doc_lengths, whole_places)
    first_row = ((me // head_parts) % row_parts) * my_rows
    whole_offsets = lax.dynamic_slice_in_dim(whole_offsets, first_row, my_rows, 0)
    starts = (whole_places[:my_rows] - whole_offsets).reshape(my_rows, 1, length)
    whole_cosine, whole_sine = tables(whole_offsets)
    answer = attend(arrived, starts, whole_cosine, whole_sine)
    returned = send_back(answer)

    output, input_grad, late_pack = finish(
        returned, x, g, shrunk, grad_feed, proj_weight, proj_left, proj_right, rank_proj,
        joined_weight, joined_left, joined_right, low_joined, mixer_gain, mixer_shift, feed_gain,
    )

    def bits(first, count):
        return [first << step for step in range(count.bit_length() - 1)]

    order = bits(devices, batches) + bits(1, devices)
    feed_sum = summed(feed_pack, order, size)
    late_sum = summed(late_pack, order, size)
    norms = rows_of(late_sum, AT_NORMS, 32).reshape(4, D)
    return (
        output.reshape(rows, slots, D),
        input_grad.reshape(rows, slots, D),
        rows_of(late_sum, AT_JOINED_LEFT, D),
        columns_of(late_sum, AT_JOINED_RIGHT, 3 * D),
        rows_of(late_sum, AT_PROJ_LEFT, D),
        columns_of(late_sum, AT_PROJ_RIGHT, D),
        rows_of(feed_sum, AT_EXPAND_LEFT, D),
        columns_of(feed_sum, AT_EXPAND_RIGHT, FF),
        rows_of(feed_sum, AT_SHRINK_LEFT, FF),
        columns_of(feed_sum, AT_SHRINK_RIGHT, D),
        norms[0], norms[1], norms[2], norms[3],
    )


def solution(mesh):
    act = P("batch", "seq", None)
    return jax.shard_map(
        per_device,
        mesh=mesh,
        in_specs=(act, P("batch", None), act) + (P(),) * 16,
        out_specs=(act, act) + (P(),) * 12,
        check_vma=False,
    )
```

time: 654 us -> 264 us (0.40)
  waiting for transfers between devices: 324 us -> 94.7 us
  matrix products: 140 us -> 0 us
  blocking collectives: 88.8 us -> 0 us
  Pallas kernels: 0 us -> 50 us
  starting transfers between devices: 0.21 us -> 36.9 us
  between operations: 16.5 us -> 1.18 us
  other arithmetic: 29.8 us -> 36.7 us
    all_gather x4 -> x0, waiting for transfers between devices: 208 us -> none  [the longest x1 107 us: per_device(): value_part = lax.all_gather(value_heads, 'seq', axis=1, tiled=True)]
    dot_general x40 -> x0, matrix products: 140 us -> none  [the longest x4 21.2 us: adapted(): result = jnp.dot(inputs, frozen, preferred_element_type=jnp.float32)]
    psum x1 -> x0, waiting for transfers between devices: 116 us -> none  [per_device(): lax.psum((grad_joined_left, grad_joined_right, grad_proj_left, grad_proj_...]
    ppermute x0 -> x20, waiting for transfers between devices: none -> 81.1 us  [swap(): lax.ppermute(part, ('batch', 'seq'), [(i, i ^ bit) for i in range(size)])]
    pallas_call x0 -> x4, Pallas kernels: none -> 50 us  [the longest x1 18 us: feed(): pl.pallas_call(feed_kernel, grid=(FF // width,), in_specs=[whole((tokens,...]
    all_gather x2 -> x0, blocking collectives: 46.9 us -> none  [the longest x1 29.7 us: per_device(): lax.all_gather(log_rows.astype(jnp.bfloat16), 'seq', axis=1, tiled=True)]
    psum x1 -> x0, blocking collectives: 41.8 us -> none  [per_device(): lax.psum((grad_joined_left, grad_joined_right, grad_proj_left, grad_proj_...]
    ppermute x0 -> x20, starting transfers between devices: none -> 24.9 us  [swap(): lax.ppermute(part, ('batch', 'seq'), [(i, i ^ bit) for i in range(size)])]
  transfers between devices with their start and end apart: 5 -> 22, of which waited for: 4 -> 15; matrix products, arithmetic and copies ran while one was open for 21% -> 12% of each run, Pallas kernels for 0% -> 17%
where the time goes in v1:
time: 264 us; the launch traced here: 262 us
  waiting for transfers between devices  94.7 us (36%)
  Pallas kernels  50 us (19%)
  local copies, waits for them, and re-layouts  42.9 us (16%)
  starting transfers between devices  36.9 us (14%)
  other arithmetic  36.7 us (14%)
    ppermute x20, waiting for transfers between devices, swap(): lax.ppermute(part, ('batch', 'seq'), [(i, i ^ bit) for i in range(size)])  81.1 us
    unnamed x92, local copies, waits for them, and re-layouts  37.9 us
    ppermute x20, starting transfers between devices, swap(): lax.ppermute(part, ('batch', 'seq'), [(i, i ^ bit) for i in range(size)])  24.9 us
    pallas_call x1, Pallas kernels, feed(): pl.pallas_call(feed_kernel, grid=(FF // width,), in_specs=[whole((tokens,...  18 us
    pallas_call x1, Pallas kernels, attend(): pl.pallas_call(attend_kernel, grid=(rows,), in_specs=[block, pl.BlockSpec...  17 us
    all_to_all x1, waiting for transfers between devices, send(): return lax.all_to_all(units, 'seq', 0, 0, tiled=True)  13.7 us
    select_n x10, other arithmetic, summed(): jnp.where(me & bit == 0, jnp.concatenate([packed, other]), jnp.concatenat...  10.7 us
    pallas_call x1, Pallas kernels, finish(): pl.pallas_call(finish_kernel, out_shape=[jax.ShapeDtypeStruct((tokens, D)...  9.05 us
  transfers between devices with their start and end apart: 22, of which 15 were waited for; matrix products, arithmetic and copies ran while one was open for 12% of the time, Pallas kernels for 17%

profile of v1, /device:TPU:0, one launch (start us, length us, event | category | flops | bytes accessed | tf_op | source)
XLA Modules:
  0.0 262.4 jit_solution(1357721453056341133)
XLA Ops:
  2.9 5.2 %compare_select_fusion.9 = (f32[128]{0:T(128)S(1)}, f32[128]{0:T(128)S(1)}) fusion(f32[]{:T(128)} %bitcast.14, f32[]{:T(128)} %bitcast.13, f32[]{:T(128)} %bitcast.12, f32[]{:T(128)} %bitcast.11, f32[]{:T(128)} %bitcast.10, f32[]{:T(128)} %bitcast.9, f32[]{:T(128)} %bitcast.8, f32[]{:T(128)} %bitcast.7), kind=kLoop, calls=%fused_computation.75 | loop fusion | flops 5760 | bytes 1056 | tf_op jit(solution)/shard_map/jit(_where)/select_n | solution.py:404
  8.7 2.8 %copy-done = bf16[1024,3072]{1,0:T(8,128)(2,1)S(1)} copy-done((bf16[1024,3072]{1,0:T(8,128)(2,1)S(1)}, bf16[1024,3072]{1,0:T(8,128)(2,1)}, u32[]{:S(2)}) %copy-start) | copy-done | bytes 6291480
  11.5 1.1 copy-done.1
  12.6 1.6 copy-done.3
  14.2 1.0 copy-done.5
  15.3 1.0 copy-done.7
  17.2 0.9 copy-done.13
  20.5 6.0 %project.1 = (bf16[8,2,4,128,128]{4,3,2,1,0:T(8,128)(2,1)}, bf16[256,128]{1,0:T(8,128)(2,1)S(1)}, bf16[256,128]{1,0:T(8,128)(2,1)S(1)}) custom-call(bf16[256,1024]{1,0:T(8,128)(2,1)S(1)} %bitcast.131, bf16[256,1024]{1,0:T(8,128)(2,1)S(1)} %bitcast.134, bf16[1024,3072]{1,0:T(8,128)(2,1)S(1)} %copy-done, bf16[1024,3072]{1,0:T(8,128)(2,1)S(1)} %copy-done, ...), custom_call_target="tpu_custom_call" | custom-call | flops 2684354560 | bytes 12582912 | tf_op jit(solution)/shard_map/project/pallas_call | solution.py:107
  26.5 7.4 %all-to-all-start = ((bf16[8,2,4,128,128]{4,3,2,1,0:T(8,128)(2,1)}), bf16[8,2,4,128,128]{4,3,2,1,0:T(8,128)(2,1)}, u32[]{:S(2)}, u32[]{:S(2)}) async-start(bf16[8,2,4,128,128]{4,3,2,1,0:T(8,128)(2,1)} %get-tuple-element.23), calls=%async_computation | async-start | bytes 4194304 | tf_op jit(solution)/shard_map/all_to_all | solution.py:443
  34.0 1.0 copy-done.8
  35.0 3.4 %copy-done.28 = bf16[1024,4096]{1,0:T(8,128)(2,1)S(1)} copy-done((bf16[1024,4096]{1,0:T(8,128)(2,1)S(1)}, bf16[1024,4096]{1,0:T(8,128)(2,1)}, u32[]{:S(2)}) %copy-start.28) | copy-done | bytes 8388632
  38.4 1.2 copy-done.29
  39.6 1.2 copy-done.30
  41.8 18.0 %feed.1 = (f32[256,1024]{1,0:T(8,128)S(1)}, f32[256,1024]{1,0:T(8,128)S(1)}, bf16[10240,128]{1,0:T(8,128)(2,1)S(1)}) custom-call(bf16[256,1024]{1,0:T(8,128)(2,1)S(1)} %bitcast.132, bf16[256,1024]{1,0:T(8,128)(2,1)S(1)} %bitcast.135, bf16[1024,4096]{1,0:T(8,128)(2,1)S(1)} %copy-done.28, bf16[4096,1024]{1,0:T(8,128)(2,1)} %ws_ref.1, ...), custom_call_target="tpu_custom_call" | custom-call | flops 10737418240 | bytes 25165824 | tf_op jit(solution)/shard_map/feed/pallas_call | solution.py:193
  59.8 1.0 copy-done.19
  60.8 1.0 copy-done.21
  61.8 1.1 dynamic-slice_bitcast_fusion
  63.1 5.5 %fusion.3 = (f32[2,1024,128]{2,1,0:T(8,128)}, f32[2,1024,128]{2,1,0:T(8,128)}) fusion(f32[128]{0:T(128)S(1)} %copy-done.42, f32[128]{0:T(128)S(1)} %copy-done.44, f32[2,1024]{1,0:T(2,128)S(1)} %subtract_convert_fusion), kind=kLoop, calls=%fused_computation.16 | loop fusion | flops 524288 | bytes 2106368 | tf_op jit(solution)/shard_map/mul | solution.py:406
  68.6 13.7 %all-to-all-done.msg_ref = bf16[8,2,4,128,128]{4,3,2,1,0:T(8,128)(2,1)} async-done(((bf16[8,2,4,128,128]{4,3,2,1,0:T(8,128)(2,1)}), bf16[8,2,4,128,128]{4,3,2,1,0:T(8,128)(2,1)}, u32[]{:S(2)}, u32[]{:S(2)}) %all-to-all-start) | async-done | bytes 2097184 | tf_op jit(solution)/shard_map/all_to_all | solution.py:443
  82.3 1.2 copy-done.17
  83.5 1.2 copy-done.18
  84.7 17.0 %attend.1 = bf16[8,2,4,128,128]{4,3,2,1,0:T(8,128)(2,1)S(1)} custom-call(bf16[8,2,4,128,128]{4,3,2,1,0:T(8,128)(2,1)} %all-to-all-done.msg_ref, s32[2,1,1024]{2,1,0:T(1,128)S(1)} %reshape.254.start_ref, f32[2,1024,128]{2,1,0:T(8,128)S(1)} %copy-done.18, f32[2,1024,128]{2,1,0:T(8,128)S(1)} %copy-done.17), custom_call_target="tpu_custom_call" | custom-call | flops 3221225472 | bytes 8388608 | tf_op jit(solution)/shard_map/attend/pallas_call | solution.py:279
  101.7 1.3 copy-done.10
  103.1 4.6 %all-to-all-start.1 = ((bf16[8,2,4,128,128]{4,3,2,1,0:T(8,128)(2,1)}), bf16[8,2,4,128,128]{4,3,2,1,0:T(8,128)(2,1)}, u32[]{:S(2)}, u32[]{:S(2)}) async-start(bf16[8,2,4,128,128]{4,3,2,1,0:T(8,128)(2,1)} %copy-done.10), calls=%async_computation.1 | async-start | bytes 4194304 | tf_op jit(solution)/shard_map/all_to_all | solution.py:446
  107.6 1.7 fusion
  109.3 1.0 copy-done.35
  110.4 1.6 collective-permute-start.11
  112.0 13.9 %collective-permute-done.11 = bf16[2560,128]{1,0:T(8,128)(2,1)S(1)} collective-permute-done((bf16[2560,128]{1,0:T(8,128)(2,1)S(1)}, bf16[2560,128]{1,0:T(8,128)(2,1)S(1)}, u32[]{:S(2)}, u32[]{:S(2)}) %collective-permute-start.11) | collective-permute-done | bytes 655392 | tf_op jit(solution)/shard_map/ppermute | solution.py:360
  125.9 1.4 fusion.2
  128.9 1.7 collective-permute-start.12
  130.6 14.2 %collective-permute-done.12 = bf16[1280,128]{1,0:T(8,128)(2,1)} collective-permute-done((bf16[1280,128]{1,0:T(8,128)(2,1)}, bf16[1280,128]{1,0:T(8,128)(2,1)}, u32[]{:S(2)}, u32[]{:S(2)}) %collective-permute-start.12) | collective-permute-done | bytes 327712 | tf_op jit(solution)/shard_map/ppermute | solution.py:360
  144.8 1.2 fusion.5
  147.8 11.0 %collective-permute-done.13 = bf16[640,128]{1,0:T(8,128)(2,1)} collective-permute-done((bf16[640,128]{1,0:T(8,128)(2,1)}, bf16[640,128]{1,0:T(8,128)(2,1)}, u32[]{:S(2)}, u32[]{:S(2)}) %collective-permute-start.13) | collective-permute-done | bytes 163872 | tf_op jit(solution)/shard_map/ppermute | solution.py:360
  158.9 1.0 fusion.7
  161.3 1.0 copy-done.9
  165.1 1.2 copy-done.20
  166.4 1.2 copy-done.22
  167.6 9.1 %finish.1 = (bf16[256,1024]{1,0:T(8,128)(2,1)}, bf16[256,1024]{1,0:T(8,128)(2,1)}, bf16[6656,128]{1,0:T(8,128)(2,1)S(1)}) custom-call(bf16[8,2,4,128,128]{4,3,2,1,0:T(8,128)(2,1)} %all-to-all-done.1.msg_ref, bf16[256,1024]{1,0:T(8,128)(2,1)S(1)} %bitcast.133, bf16[256,1024]{1,0:T(8,128)(2,1)S(1)} %bitcast.136, f32[256,1024]{1,0:T(8,128)S(1)} %copy-done.20, ...), custom_call_target="tpu_custom_call" | custom-call | flops 3221225472 | bytes 16777216 | tf_op jit(solution)/shard_map/finish/pallas_call | solution.py:345
  178.5 3.0 %collective-permute-start.15 = (bf16[320,128]{1,0:T(8,128)(2,1)S(1)}, bf16[320,128]{1,0:T(8,128)(2,1)S(1)}, u32[]{:S(2)}, u32[]{:S(2)}) collective-permute-start(bf16[320,128]{1,0:T(8,128)(2,1)S(1)} %fusion.9), channel_id=1, source_target_pairs={{0,4},{1,5},{2,6},{3,7},{4,0},{5,1},{6,2},{7,3},{8,12},{9,13},{10,... | collective-permute-start | bytes 245768 | tf_op jit(solution)/shard_map/ppermute | solution.py:360
  181.5 3.3 %collective-permute-done.15 = bf16[320,128]{1,0:T(8,128)(2,1)S(1)} collective-permute-done((bf16[320,128]{1,0:T(8,128)(2,1)S(1)}, bf16[320,128]{1,0:T(8,128)(2,1)S(1)}, u32[]{:S(2)}, u32[]{:S(2)}) %collective-permute-start.15) | collective-permute-done | bytes 81952 | tf_op jit(solution)/shard_map/ppermute | solution.py:360
  184.8 1.6 collective-permute-start.16
  186.4 3.8 %collective-permute-done.16 = bf16[640,128]{1,0:T(8,128)(2,1)S(1)} collective-permute-done((bf16[640,128]{1,0:T(8,128)(2,1)S(1)}, bf16[640,128]{1,0:T(8,128)(2,1)S(1)}, u32[]{:S(2)}, u32[]{:S(2)}) %collective-permute-start.16) | collective-permute-done | bytes 163872 | tf_op jit(solution)/shard_map/ppermute | solution.py:360
  190.7 1.6 collective-permute-start.1
  192.2 5.2 %collective-permute-done.17 = bf16[1280,128]{1,0:T(8,128)(2,1)S(1)} collective-permute-done((bf16[1280,128]{1,0:T(8,128)(2,1)S(1)}, bf16[1280,128]{1,0:T(8,128)(2,1)S(1)}, u32[]{:S(2)}, u32[]{:S(2)}) %collective-permute-start.17) | collective-permute-done | bytes 327712 | tf_op jit(solution)/shard_map/ppermute | solution.py:360
  197.6 1.6 collective-permute-start.18
  199.2 3.8 %collective-permute-done.1 = bf16[1664,128]{1,0:T(8,128)(2,1)S(1)} collective-permute-done((bf16[1664,128]{1,0:T(8,128)(2,1)S(1)}, bf16[1664,128]{1,0:T(8,128)(2,1)S(1)}, u32[]{:S(2)}, u32[]{:S(2)}) %collective-permute-start.1) | collective-permute-done | bytes 426016 | tf_op jit(solution)/shard_map/ppermute | solution.py:360
  203.1 2.5 collective-permute-start.2
  205.7 8.1 %collective-permute-done.18 = bf16[2560,128]{1,0:T(8,128)(2,1)S(1)} collective-permute-done((bf16[2560,128]{1,0:T(8,128)(2,1)S(1)}, bf16[2560,128]{1,0:T(8,128)(2,1)S(1)}, u32[]{:S(2)}, u32[]{:S(2)}) %collective-permute-start.18) | collective-permute-done | bytes 655392 | tf_op jit(solution)/shard_map/ppermute | solution.py:360
  214.3 1.8 collective-permute-start.3
  216.1 3.6 %collective-permute-done.3 = bf16[416,128]{1,0:T(8,128)(2,1)S(1)} collective-permute-done((bf16[416,128]{1,0:T(8,128)(2,1)S(1)}, bf16[416,128]{1,0:T(8,128)(2,1)S(1)}, u32[]{:S(2)}, u32[]{:S(2)}) %collective-permute-start.3) | collective-permute-done | bytes 106528 | tf_op jit(solution)/shard_map/ppermute | solution.py:360
  219.8 2.4 collective-permute-start.4
  222.1 3.2 %collective-permute-done.4 = bf16[208,128]{1,0:T(8,128)(2,1)S(1)} collective-permute-done((bf16[208,128]{1,0:T(8,128)(2,1)S(1)}, bf16[208,128]{1,0:T(8,128)(2,1)S(1)}, u32[]{:S(2)}, u32[]{:S(2)}) %collective-permute-start.4) | collective-permute-done | bytes 53280 | tf_op jit(solution)/shard_map/ppermute | solution.py:360
  225.4 1.9 collective-permute-start.5
  227.3 3.2 %collective-permute-done.5 = bf16[208,128]{1,0:T(8,128)(2,1)S(1)} collective-permute-done((bf16[208,128]{1,0:T(8,128)(2,1)S(1)}, bf16[208,128]{1,0:T(8,128)(2,1)S(1)}, u32[]{:S(2)}, u32[]{:S(2)}) %collective-permute-start.5) | collective-permute-done | bytes 53280 | tf_op jit(solution)/shard_map/ppermute | solution.py:360
  230.5 1.3 collective-permute-start.6
  231.8 3.5 %collective-permute-done.6 = bf16[416,128]{1,0:T(8,128)(2,1)S(1)} collective-permute-done((bf16[416,128]{1,0:T(8,128)(2,1)S(1)}, bf16[416,128]{1,0:T(8,128)(2,1)S(1)}, u32[]{:S(2)}, u32[]{:S(2)}) %collective-permute-start.6) | collective-permute-done | bytes 106528 | tf_op jit(solution)/shard_map/ppermute | solution.py:360
  235.4 1.8 collective-permute-start.7
  237.2 9.1 %maximum_select_fusion = bf16[10240,128]{1,0:T(8,128)(2,1)S(1)} fusion(bf16[5120,128]{1,0:T(8,128)(2,1)S(1)} %collective-permute-done.19, bf16[5120,128]{1,0:T(8,128)(2,1)S(1)} %maximum_select_fusion.2, pred[]{:T(512)S(6)} %eq.17), kind=kLoop, calls=%fused_computation | loop fusion | flops 11796480 | bytes 5242881 | tf_op jit(solution)/shard_map/jit(_where)/select_n | solution.py:377
  246.4 1.5 collective-permute-start.8
  248.0 1.5 slice_convert_fusion
  251.4 3.2 %collective-permute-done.8 = bf16[1664,128]{1,0:T(8,128)(2,1)S(1)} collective-permute-done((bf16[1664,128]{1,0:T(8,128)(2,1)S(1)}, bf16[1664,128]{1,0:T(8,128)(2,1)S(1)}, u32[]{:S(2)}, u32[]{:S(2)}) %collective-permute-start.8) | collective-permute-done | bytes 426016 | tf_op jit(solution)/shard_map/ppermute | solution.py:360
  255.0 1.5 copy_bitcast_fusion
  257.8 1.2 fusion.16
  261.1 1.3 copy_bitcast_fusion.1
  (130 shorter events, 23.8 us)
Async XLA Ops:
  8.7 2.8 %copy-start = (bf16[1024,3072]{1,0:T(8,128)(2,1)S(1)}, bf16[1024,3072]{1,0:T(8,128)(2,1)}, u32[]{:S(2)}) copy-start(bf16[1024,3072]{1,0:T(8,128)(2,1)} %wj_ref.1) | copy-start | bytes 18874372
  11.5 1.1 copy-start.1
  12.6 1.6 copy-start.3
  14.2 1.0 copy-start.5
  15.3 1.0 copy-start.7
  16.3 0.9 copy-start.11
  17.2 0.9 copy-start.13
  18.2 0.9 copy-start.15
  19.1 0.7 copy-start.23
  26.5 7.4 %copy-start.6 = (bf16[2,128,1024]{2,1,0:T(8,128)(2,1)S(1)}, bf16[2,128,1024]{2,1,0:T(8,128)(2,1)}, u32[]{:S(2)}) copy-start(bf16[2,128,1024]{2,1,0:T(8,128)(2,1)} %param.19) | copy-start | bytes 1572868
  26.5 7.4 %copy-start.27 = (f32[1024]{0:T(1024)S(1)}, f32[1024]{0:T(1024)}, u32[]{:S(2)}) copy-start(f32[1024]{0:T(1024)} %param.36) | copy-start | bytes 12292
  26.5 7.4 %copy-start.31 = (bf16[1024,128]{1,0:T(8,128)(2,1)S(1)}, bf16[1024,128]{1,0:T(8,128)(2,1)}, u32[]{:S(2)}) copy-start(bf16[1024,128]{1,0:T(8,128)(2,1)} %le_ref.1) | copy-start | bytes 786436
  26.5 7.5 %copy-start.33 = (f32[1024]{0:T(1024)S(1)}, f32[1024]{0:T(1024)}, u32[]{:S(2)}) copy-start(f32[1024]{0:T(1024)} %param.37) | copy-start | bytes 12292
  26.5 55.8 %all-to-all-start = ((bf16[8,2,4,128,128]{4,3,2,1,0:T(8,128)(2,1)}), bf16[8,2,4,128,128]{4,3,2,1,0:T(8,128)(2,1)}, u32[]{:S(2)}, u32[]{:S(2)}) async-start(bf16[8,2,4,128,128]{4,3,2,1,0:T(8,128)(2,1)} %get-tuple-element.23), calls=%async_computation | async-start | bytes 4194304 | tf_op jit(solution)/shard_map/all_to_all | solution.py:443
  34.0 1.0 copy-start.8
  35.0 3.4 %copy-start.28 = (bf16[1024,4096]{1,0:T(8,128)(2,1)S(1)}, bf16[1024,4096]{1,0:T(8,128)(2,1)}, u32[]{:S(2)}) copy-start(bf16[1024,4096]{1,0:T(8,128)(2,1)} %we_ref.1) | copy-start | bytes 25165828
  38.4 1.2 copy-start.29
  39.6 1.2 copy-start.30
  40.9 0.9 copy-start.32
  59.8 1.0 copy-start.19
  60.8 1.0 copy-start.21
  61.8 1.2 copy-start.40
  61.8 1.3 copy-start.42
  61.8 1.3 copy-start.44
  62.9 44.7 %collective-permute-start.10 = (bf16[5120,128]{1,0:T(8,128)(2,1)}, bf16[5120,128]{1,0:T(8,128)(2,1)}, u32[]{:S(2)}, u32[]{:S(2)}) collective-permute-start(bf16[5120,128]{1,0:T(8,128)(2,1)} %dynamic-slice_bitcast_fusion), channel_id=1, source_target_pairs={{0,8},{1,9},{2,10},{3,11},{4,12},{5,13},{6,14},{7,15},{8,0},{9,1},... | collective-permute-start | bytes 3932168 | tf_op jit(solution)/shard_map/ppermute | solution.py:360
  82.3 1.2 copy-start.17
  83.5 1.2 copy-start.18
  101.7 1.3 copy-start.10
  103.1 58.2 %all-to-all-start.1 = ((bf16[8,2,4,128,128]{4,3,2,1,0:T(8,128)(2,1)}), bf16[8,2,4,128,128]{4,3,2,1,0:T(8,128)(2,1)}, u32[]{:S(2)}, u32[]{:S(2)}) async-start(bf16[8,2,4,128,128]{4,3,2,1,0:T(8,128)(2,1)} %copy-done.10), calls=%async_computation.1 | async-start | bytes 4194304 | tf_op jit(solution)/shard_map/all_to_all | solution.py:446
  109.3 1.1 copy-start.35
  110.4 15.5 %collective-permute-start.11 = (bf16[2560,128]{1,0:T(8,128)(2,1)S(1)}, bf16[2560,128]{1,0:T(8,128)(2,1)S(1)}, u32[]{:S(2)}, u32[]{:S(2)}) collective-permute-start(bf16[2560,128]{1,0:T(8,128)(2,1)S(1)} %dynamic-slice_bitcast_fusion.2), channel_id=1, source_target_pairs={{0,16},{1,17},{2,18},{3,19},{4,20},{5,21},{6,22},{7,23},{8,24},{9,... | collective-permute-start | bytes 1966088 | tf_op jit(solution)/shard_map/ppermute | solution.py:360
  125.9 35.3 %copy-start.4 = (bf16[1024,1024]{1,0:T(8,128)(2,1)S(1)}, bf16[1024,1024]{1,0:T(8,128)(2,1)}, u32[]{:S(2)}) copy-start(bf16[1024,1024]{1,0:T(8,128)(2,1)} %wp_ref.3) | copy-start | bytes 6291460
  127.3 0.8 copy-start.36
  127.3 33.9 %copy-start.2 = (bf16[128,3072]{1,0:T(8,128)(2,1)S(1)}, bf16[128,3072]{1,0:T(8,128)(2,1)}, u32[]{:S(2)}) copy-start(bf16[128,3072]{1,0:T(8,128)(2,1)} %rj_ref.1) | copy-start | bytes 2359300
  127.4 33.9 %copy-start.24 = (f32[1024]{0:T(1024)S(1)}, f32[1024]{0:T(1024)}, u32[]{:S(2)}) copy-start(f32[1024]{0:T(1024)} %param.34) | copy-start | bytes 12292
  127.4 33.9 %copy-start.26 = (f32[1024]{0:T(1024)S(1)}, f32[1024]{0:T(1024)}, u32[]{:S(2)}) copy-start(f32[1024]{0:T(1024)} %param.35) | copy-start | bytes 12292
  128.9 15.9 %collective-permute-start.12 = (bf16[1280,128]{1,0:T(8,128)(2,1)}, bf16[1280,128]{1,0:T(8,128)(2,1)}, u32[]{:S(2)}, u32[]{:S(2)}) collective-permute-start(bf16[1280,128]{1,0:T(8,128)(2,1)} %dynamic-slice_bitcast_fusion.4), channel_id=1, source_target_pairs={{0,1},{1,0},{2,3},{3,2},{4,5},{5,4},{6,7},{7,6},{8,9},{9,8},{10,11... | collective-permute-start | bytes 983048 | tf_op jit(solution)/shard_map/ppermute | solution.py:360
  146.0 0.7 copy-start.37
  147.4 11.4 %collective-permute-start.13 = (bf16[640,128]{1,0:T(8,128)(2,1)}, bf16[640,128]{1,0:T(8,128)(2,1)}, u32[]{:S(2)}, u32[]{:S(2)}) collective-permute-start(bf16[640,128]{1,0:T(8,128)(2,1)} %dynamic-slice_bitcast_fusion.6), channel_id=1, source_target_pairs={{0,2},{1,3},{2,0},{3,1},{4,6},{5,7},{6,4},{7,5},{8,10},{9,11},{10,... | collective-permute-start | bytes 491528 | tf_op jit(solution)/shard_map/ppermute | solution.py:360
  161.2 15.6 %collective-permute-start.14 = (bf16[320,128]{1,0:T(8,128)(2,1)}, bf16[320,128]{1,0:T(8,128)(2,1)}, u32[]{:S(2)}, u32[]{:S(2)}) collective-permute-start(bf16[320,128]{1,0:T(8,128)(2,1)} %dynamic-slice_bitcast_fusion.8), channel_id=1, source_target_pairs={{0,4},{1,5},{2,6},{3,7},{4,0},{5,1},{6,2},{7,3},{8,12},{9,13},{10,... | collective-permute-start | bytes 245768 | tf_op jit(solution)/shard_map/ppermute | solution.py:360
  161.2 1.0 copy-start.9
  162.3 0.9 copy-start.12
  163.2 0.9 copy-start.14
  164.2 0.9 copy-start.16
  165.1 1.2 copy-start.20
  166.4 1.2 copy-start.22
  176.6 0.9 copy-start.39
  176.7 13.7 %collective-permute-start = (bf16[3328,128]{1,0:T(8,128)(2,1)S(1)}, bf16[3328,128]{1,0:T(8,128)(2,1)S(1)}, u32[]{:S(2)}, u32[]{:S(2)}) collective-permute-start(bf16[3328,128]{1,0:T(8,128)(2,1)S(1)} %dynamic-slice_bitcast_fusion.1), channel_id=1, source_target_pairs={{0,8},{1,9},{2,10},{3,11},{4,12},{5,13},{6,14},{7,15},{8,0},{9,1},... | collective-permute-start | bytes 2555912 | tf_op jit(solution)/shard_map/ppermute | solution.py:360
  178.5 6.3 %collective-permute-start.15 = (bf16[320,128]{1,0:T(8,128)(2,1)S(1)}, bf16[320,128]{1,0:T(8,128)(2,1)S(1)}, u32[]{:S(2)}, u32[]{:S(2)}) collective-permute-start(bf16[320,128]{1,0:T(8,128)(2,1)S(1)} %fusion.9), channel_id=1, source_target_pairs={{0,4},{1,5},{2,6},{3,7},{4,0},{5,1},{6,2},{7,3},{8,12},{9,13},{10,... | collective-permute-start | bytes 245768 | tf_op jit(solution)/shard_map/ppermute | solution.py:360
  184.8 5.4 %collective-permute-start.16 = (bf16[640,128]{1,0:T(8,128)(2,1)S(1)}, bf16[640,128]{1,0:T(8,128)(2,1)S(1)}, u32[]{:S(2)}, u32[]{:S(2)}) collective-permute-start(bf16[640,128]{1,0:T(8,128)(2,1)S(1)} %maximum_select_fusion.8), channel_id=1, source_target_pairs={{0,2},{1,3},{2,0},{3,1},{4,6},{5,7},{6,4},{7,5},{8,10},{9,11},{10,... | collective-permute-start | bytes 491528 | tf_op jit(solution)/shard_map/ppermute | solution.py:360
  190.3 7.1 %collective-permute-start.17 = (bf16[1280,128]{1,0:T(8,128)(2,1)S(1)}, bf16[1280,128]{1,0:T(8,128)(2,1)S(1)}, u32[]{:S(2)}, u32[]{:S(2)}) collective-permute-start(bf16[1280,128]{1,0:T(8,128)(2,1)S(1)} %maximum_select_fusion.6), channel_id=1, source_target_pairs={{0,1},{1,0},{2,3},{3,2},{4,5},{5,4},{6,7},{7,6},{8,9},{9,8},{10,11... | collective-permute-start | bytes 983048 | tf_op jit(solution)/shard_map/ppermute | solution.py:360
  190.7 12.3 %collective-permute-start.1 = (bf16[1664,128]{1,0:T(8,128)(2,1)S(1)}, bf16[1664,128]{1,0:T(8,128)(2,1)S(1)}, u32[]{:S(2)}, u32[]{:S(2)}) collective-permute-start(bf16[1664,128]{1,0:T(8,128)(2,1)S(1)} %dynamic-slice_bitcast_fusion.3), channel_id=1, source_target_pairs={{0,16},{1,17},{2,18},{3,19},{4,20},{5,21},{6,22},{7,23},{8,24},{9,... | collective-permute-start | bytes 1277960 | tf_op jit(solution)/shard_map/ppermute | solution.py:360
  197.6 16.2 %collective-permute-start.18 = (bf16[2560,128]{1,0:T(8,128)(2,1)S(1)}, bf16[2560,128]{1,0:T(8,128)(2,1)S(1)}, u32[]{:S(2)}, u32[]{:S(2)}) collective-permute-start(bf16[2560,128]{1,0:T(8,128)(2,1)S(1)} %maximum_select_fusion.4), channel_id=1, source_target_pairs={{0,16},{1,17},{2,18},{3,19},{4,20},{5,21},{6,22},{7,23},{8,24},{9,... | collective-permute-start | bytes 1966088 | tf_op jit(solution)/shard_map/ppermute | solution.py:360
  203.1 11.1 %collective-permute-start.2 = (bf16[832,128]{1,0:T(8,128)(2,1)S(1)}, bf16[832,128]{1,0:T(8,128)(2,1)S(1)}, u32[]{:S(2)}, u32[]{:S(2)}) collective-permute-start(bf16[832,128]{1,0:T(8,128)(2,1)S(1)} %dynamic-slice_bitcast_fusion.5), channel_id=1, source_target_pairs={{0,1},{1,0},{2,3},{3,2},{4,5},{5,4},{6,7},{7,6},{8,9},{9,8},{10,11... | collective-permute-start | bytes 638984 | tf_op jit(solution)/shard_map/ppermute | solution.py:360
  214.1 23.0 %collective-permute-start.19 = (bf16[5120,128]{1,0:T(8,128)(2,1)S(1)}, bf16[5120,128]{1,0:T(8,128)(2,1)S(1)}, u32[]{:S(2)}, u32[]{:S(2)}) collective-permute-start(bf16[5120,128]{1,0:T(8,128)(2,1)S(1)} %maximum_select_fusion.2), channel_id=1, source_target_pairs={{0,8},{1,9},{2,10},{3,11},{4,12},{5,13},{6,14},{7,15},{8,0},{9,1},... | collective-permute-start | bytes 3932168 | tf_op jit(solution)/shard_map/ppermute | solution.py:360
  214.3 5.4 %collective-permute-start.3 = (bf16[416,128]{1,0:T(8,128)(2,1)S(1)}, bf16[416,128]{1,0:T(8,128)(2,1)S(1)}, u32[]{:S(2)}, u32[]{:S(2)}) collective-permute-start(bf16[416,128]{1,0:T(8,128)(2,1)S(1)} %dynamic-slice_bitcast_fusion.7), channel_id=1, source_target_pairs={{0,2},{1,3},{2,0},{3,1},{4,6},{5,7},{6,4},{7,5},{8,10},{9,11},{10,... | collective-permute-start | bytes 319496 | tf_op jit(solution)/shard_map/ppermute | solution.py:360
  219.8 5.6 %collective-permute-start.4 = (bf16[208,128]{1,0:T(8,128)(2,1)S(1)}, bf16[208,128]{1,0:T(8,128)(2,1)S(1)}, u32[]{:S(2)}, u32[]{:S(2)}) collective-permute-start(bf16[208,128]{1,0:T(8,128)(2,1)S(1)} %dynamic-slice_bitcast_fusion.9), channel_id=1, source_target_pairs={{0,4},{1,5},{2,6},{3,7},{4,0},{5,1},{6,2},{7,3},{8,12},{9,13},{10,... | collective-permute-start | bytes 159752 | tf_op jit(solution)/shard_map/ppermute | solution.py:360
  225.4 5.1 %collective-permute-start.5 = (bf16[208,128]{1,0:T(8,128)(2,1)S(1)}, bf16[208,128]{1,0:T(8,128)(2,1)S(1)}, u32[]{:S(2)}, u32[]{:S(2)}) collective-permute-start(bf16[208,128]{1,0:T(8,128)(2,1)S(1)} %fusion.11), channel_id=1, source_target_pairs={{0,4},{1,5},{2,6},{3,7},{4,0},{5,1},{6,2},{7,3},{8,12},{9,13},{10,... | collective-permute-start | bytes 159752 | tf_op jit(solution)/shard_map/ppermute | solution.py:360
  230.5 4.8 %collective-permute-start.6 = (bf16[416,128]{1,0:T(8,128)(2,1)S(1)}, bf16[416,128]{1,0:T(8,128)(2,1)S(1)}, u32[]{:S(2)}, u32[]{:S(2)}) collective-permute-start(bf16[416,128]{1,0:T(8,128)(2,1)S(1)} %maximum_select_fusion.9), channel_id=1, source_target_pairs={{0,2},{1,3},{2,0},{3,1},{4,6},{5,7},{6,4},{7,5},{8,10},{9,11},{10,... | collective-permute-start | bytes 319496 | tf_op jit(solution)/shard_map/ppermute | solution.py:360
  235.4 10.9 %collective-permute-start.7 = (bf16[832,128]{1,0:T(8,128)(2,1)S(1)}, bf16[832,128]{1,0:T(8,128)(2,1)S(1)}, u32[]{:S(2)}, u32[]{:S(2)}) collective-permute-start(bf16[832,128]{1,0:T(8,128)(2,1)S(1)} %maximum_select_fusion.7), channel_id=1, source_target_pairs={{0,1},{1,0},{2,3},{3,2},{4,5},{5,4},{6,7},{7,6},{8,9},{9,8},{10,11... | collective-permute-start | bytes 638984 | tf_op jit(solution)/shard_map/ppermute | solution.py:360
  246.4 8.2 %collective-permute-start.8 = (bf16[1664,128]{1,0:T(8,128)(2,1)S(1)}, bf16[1664,128]{1,0:T(8,128)(2,1)S(1)}, u32[]{:S(2)}, u32[]{:S(2)}) collective-permute-start(bf16[1664,128]{1,0:T(8,128)(2,1)S(1)} %maximum_select_fusion.5), channel_id=1, source_target_pairs={{0,16},{1,17},{2,18},{3,19},{4,20},{5,21},{6,22},{7,23},{8,24},{9,... | collective-permute-start | bytes 1277960 | tf_op jit(solution)/shard_map/ppermute | solution.py:360
  254.9 2.4 collective-permute-start.9
  257.8 1.6 copy-start.34
  260.0 1.1 slice-start
  (4 other events, 2.5 us)

commit v2 on v1

v2 whole, which is shorter than its diff:
```python
from functools import partial

import jax
import jax.numpy as jnp
from jax import lax
from jax.experimental import pallas as pl
from jax.experimental.pallas import tpu as pltpu
from jax.sharding import PartitionSpec as P

D = 1024
FF = 4096
HEADS = 16
HEAD_DIM = 64
ROT_DIM = 16
RANK = 128
PAIR = 128
PAIRS = 8

EPSILON = 1e-05
SCALING = 0.25
NEGATIVE = -1e30
BF = jnp.bfloat16
F32 = jnp.float32
MIB = 1024 * 1024
WIDE = 60 * MIB
LITTLE = pl.CostEstimate(flops=1, bytes_accessed=1, transcendentals=0)
MUCH = pl.CostEstimate(flops=2 * 10**11, bytes_accessed=1, transcendentals=0)

FEED_UNITS = {"expand_left": 0, "expand_right": 8, "shrink_left": 40, "shrink_right": 72}
FEED_ROWS = 80 * RANK
PROJ_UNITS = {"proj_left": 0, "proj_right": 8}
PROJ_ROWS = 16 * RANK
LATE_UNITS = {"joined_left": 0, "norms": 8}
LATE_ROWS = 9 * RANK


def nn(left, right):
    return lax.dot_general(left, right, (((1,), (0,)), ((), ())), preferred_element_type=F32)


def nt(left, right):
    return lax.dot_general(left, right, (((1,), (1,)), ((), ())), preferred_element_type=F32)


def tn(left, right):
    return lax.dot_general(left, right, (((0,), (0,)), ((), ())), preferred_element_type=F32)


def normalised(values):
    average = jnp.mean(values, axis=-1, keepdims=True)
    centred = values - average
    spread = jnp.mean(centred * centred, axis=-1, keepdims=True)
    scale = lax.rsqrt(spread + EPSILON)
    return centred * scale, scale


def turn(values, cosine, sine):
    lane = lax.broadcasted_iota(jnp.int32, values.shape, 1) % HEAD_DIM
    half = ROT_DIM // 2
    partner = jnp.where(lane < half, pltpu.roll(values, PAIR - half, 1), pltpu.roll(values, half, 1))
    return values * cosine + partner * sine


def document_starts(doc_ref, row, places):
    ending, begins = jnp.int32(0), jnp.zeros_like(places)
    for entry in range(doc_ref.shape[1]):
        ending = ending + doc_ref[row, entry]
        begins = begins + jnp.where(places >= ending, doc_ref[row, entry], 0)
    return begins


def turning(offsets):
    half = ROT_DIM // 2
    index = lax.broadcasted_iota(jnp.int32, (half, 1), 0)
    frequency = jnp.zeros((half, 1), F32)
    for j in range(half):
        frequency = jnp.where(index == j, 10000.0 ** (-2.0 * j / ROT_DIM), frequency)
    angles = offsets.astype(F32) * frequency
    lane = lax.broadcasted_iota(jnp.int32, (half, PAIR), 1) % HEAD_DIM
    here = (lane < ROT_DIM) & (lane % half == lax.broadcasted_iota(jnp.int32, (half, PAIR), 0))
    spread = jnp.where(here, 1.0, 0.0)
    signed = jnp.where(lane < half, -spread, spread)
    exact = partial(
        lax.dot_general, dimension_numbers=(((0,), (0,)), ((), ())),
        precision=lax.Precision.HIGHEST, preferred_element_type=F32,
    )
    cosine = exact(jnp.cos(angles), spread)
    still = lax.broadcasted_iota(jnp.int32, (1, PAIR), 1) % HEAD_DIM >= ROT_DIM
    return cosine + jnp.where(still, 1.0, 0.0), exact(jnp.sin(angles), signed)


def add_low(left, right):
    return (left.astype(F32) + right.astype(F32)).astype(BF)


def after(value, *others):
    return lax.optimization_barrier((value,) + others)[0] if others else value


class Packing:
    def __init__(self, rows, order, stride=None, first=0):
        self.rows, self.order, self.first = rows, order, first
        self.block = rows // 2 ** len(order)
        self.stride = stride or self.block
        self.piece = max(size for size in (16, 32, 64, 128) if self.block % size == 0 and first % size == 0 and self.stride % size == 0)

    def held(self, stride, first):
        return Packing(self.rows, self.order, stride, first)

    def bits(self, block):
        count = len(self.order)
        return [(block >> (count - 1 - step)) & 1 for step in range(count)]

    def place(self, bits):
        place = 0
        for bit, value in zip(self.order, bits):
            place = place * 2 + (value ^ (lax.shift_right_logical(device_number(), bit) & 1))
        return place

    def pieces(self, unit):
        per = self.block // self.piece
        for part in range(RANK // self.piece):
            piece = unit * (RANK // self.piece) + part
            row = self.place(self.bits(piece // per)) * self.stride + self.first + piece % per * self.piece
            yield part * self.piece, pl.multiple_of(row, 16)

    def put(self, ref, unit, value):
        for first, row in self.pieces(unit):
            ref[pl.ds(row, self.piece), :] = value[first : first + self.piece]

    def get(self, ref, unit):
        return jnp.concatenate([ref[pl.ds(row, self.piece), :] for _, row in self.pieces(unit)], axis=0)

    def put_rows(self, ref, unit, matrix):
        matrix = matrix.astype(BF)
        for step in range(matrix.shape[0] // RANK):
            self.put(ref, unit + step, matrix[step * RANK : (step + 1) * RANK])

    def put_columns(self, ref, unit, matrix):
        matrix = matrix.astype(BF)
        for step in range(matrix.shape[1] // RANK):
            self.put(ref, unit + step, matrix[:, step * RANK : (step + 1) * RANK])


class PairPacking(Packing):
    def __init__(self, order, own, pair_bits, stride=None, first=0):
        self.order, self.own, self.pair_bits = order, own, pair_bits
        self.block = -(-3 * RANK // (16 * 2 ** len(own))) * 16
        self.stride, self.first, self.piece = stride or self.block, first, 16
        self.rows = self.block * 2 ** len(own)

    def held(self, stride, first):
        return PairPacking(self.order, self.own, self.pair_bits, stride, first)

    def pieces(self, unit):
        part, pair = divmod(unit, PAIRS)
        for step in range(RANK // 16):
            row = part * RANK + step * 16
            block, inside = divmod(row, self.block)
            inner = dict(zip(self.own, [(block >> (len(self.own) - 1 - k)) & 1 for k in range(len(self.own))]))
            outer = {bit: (pair >> k) & 1 for k, bit in enumerate(self.pair_bits)}
            bits = [inner[bit] if bit in inner else outer[bit] for bit in self.order]
            at = self.place(bits) * self.stride + self.first + inside
            yield step * 16, pl.multiple_of(at, 16)

    def put_own(self, ref, part, value):
        for step in range(RANK // 16):
            block, inside = divmod(part * RANK + step * 16, self.block)
            place = 0
            for k, bit in enumerate(self.own):
                value_bit = (block >> (len(self.own) - 1 - k)) & 1
                place = place * 2 + (value_bit ^ (lax.shift_right_logical(device_number(), bit) & 1))
            at = pl.multiple_of(place * self.block + inside, 16)
            ref[pl.ds(at, 16), :] = value[step * 16 : (step + 1) * 16]


def device_number():
    return lax.axis_index("batch") * lax.axis_size("seq") + lax.axis_index("seq")


def halve(packed, bit, size, *hold):
    half = packed.shape[0] // 2
    return add_low(packed[:half], after(swap(packed[half:], 1 << bit, size), *hold))


def double(packed, bit, size, *hold):
    return jnp.concatenate([packed, after(swap(packed, 1 << bit, size), *hold)])


def join_kernel(*refs):
    *part_refs, out_ref = refs
    for place, part_ref in enumerate(part_refs):
        rows = part_ref.shape[0]
        out_ref[place * rows : (place + 1) * rows] = part_ref[...]


def join(parts):
    rows = sum(part.shape[0] for part in parts)
    return pl.pallas_call(
        join_kernel,
        out_shape=jax.ShapeDtypeStruct((rows, RANK), BF),
        compiler_params=pltpu.CompilerParams(vmem_limit_bytes=WIDE),
        cost_estimate=LITTLE,
        name="join",
    )(*parts)


def masks(pair):
    return [1 << pair[1], 1 << pair[0], (1 << pair[0]) | (1 << pair[1])]


def quarter(packed, pair, size, *hold):
    blocks = packed.reshape(4, packed.shape[0] // 4, RANK)
    others = [swap(blocks[k + 1], mask, size) for k, mask in enumerate(masks(pair))]
    return add_all(blocks[0], [after(other, *hold) for other in others])


def everyone(packed, pair, size, *hold):
    return [packed] + [after(swap(packed, mask, size), *hold) for mask in masks(pair)]


def add_all(first, others):
    total = first.astype(F32)
    for other in others:
        total = total + other.astype(F32)
    return total.astype(BF)


def project_kernel(
    x_ref, g_ref, wj_ref, wp_ref, lj_ref, rj_ref, lp_ref, rp_ref, gain_ref, shift_ref, doc_ref,
    msg_ref, low_ref, rank_ref, wj_here, wp_here, sems,
):
    rows, slots = msg_ref.shape[1], msg_ref.shape[3]
    third = lambda ref, part: ref.at[:, pl.ds(part * D, D)]
    copies = [pltpu.make_async_copy(wp_ref, wp_here, sems.at[3])] + [
        pltpu.make_async_copy(third(wj_ref, part), third(wj_here, part), sems.at[part]) for part in range(3)
    ]
    for copy in copies:
        copy.start()

    def put(place, matrix):
        matrix = matrix.astype(BF)
        for pair in range(PAIRS):
            for row in range(rows):
                msg_ref[pair, row, place] = matrix[row * slots : (row + 1) * slots, pair * PAIR : (pair + 1) * PAIR]

    g = g_ref[...]
    rank = (SCALING * nt(g, rp_ref[...])).astype(BF)
    rank_ref[...] = rank
    hat, _ = normalised(x_ref[...].astype(F32))
    u = (hat * gain_ref[...] + shift_ref[...]).astype(BF)
    low = nn(u, lj_ref[...]).astype(BF)
    low_ref[...] = low
    places = lax.axis_index("seq") * slots + lax.broadcasted_iota(jnp.int32, (1, slots), 1)
    turns = [turning(places - document_starts(doc_ref, row, places)) for row in range(rows)]
    cosine = jnp.concatenate([pair[0] for pair in turns], axis=0)
    sine = jnp.concatenate([pair[1] for pair in turns], axis=0)
    copies[0].wait()
    put(3, nt(g, wp_here[...]) + nt(rank, lp_ref[...]))
    for part in range(3):
        columns = slice(part * D, (part + 1) * D)
        copies[part + 1].wait()
        result = nn(u, wj_here[:, columns]) + SCALING * nn(low, rj_ref[:, columns])
        if part < 2:
            result = jnp.concatenate(
                [turn(result[:, k * PAIR : (k + 1) * PAIR], cosine, sine) for k in range(PAIRS)], axis=1
            )
        put(part, result)


def project(x, g, joined_weight, proj_weight, joined_left, joined_right, proj_left, proj_right,
            gain, shift, doc_lengths, rows):
    tokens = x.shape[0]
    held = pl.BlockSpec(memory_space=pltpu.VMEM)
    away = pl.BlockSpec(memory_space=pl.ANY)
    return pl.pallas_call(
        project_kernel,
        in_specs=[held, held, away, away] + [held] * 6 + [pl.BlockSpec(memory_space=pltpu.SMEM)],
        out_shape=[
            jax.ShapeDtypeStruct((PAIRS, rows, 4, tokens // rows, PAIR), BF),
            jax.ShapeDtypeStruct((tokens, RANK), BF),
            jax.ShapeDtypeStruct((tokens, RANK), BF),
        ],
        scratch_shapes=[
            pltpu.VMEM((D, 3 * D), BF), pltpu.VMEM((D, D), BF), pltpu.SemaphoreType.DMA((4,)),
        ],
        compiler_params=pltpu.CompilerParams(vmem_limit_bytes=WIDE),
        cost_estimate=LITTLE,
        name="project",
    )(x, g, joined_weight, proj_weight, joined_left, joined_right, proj_left, proj_right, gain, shift, doc_lengths)


def feed_kernel(
    packing, x_ref, g_ref, we_ref, ws_ref, le_ref, re_ref, ls_ref, rs_ref, gain_ref, shift_ref,
    shrunk_ref, gfeed_ref, pack_ref, f_ref, lowe_ref, ranks_ref, lows_ref, ranke_ref,
):
    step = pl.program_id(0)
    width = we_ref.shape[1]

    @pl.when(step == 0)
    def _():
        hat, _ = normalised(x_ref[...].astype(F32))
        f_ref[...] = (hat * gain_ref[...] + shift_ref[...]).astype(BF)
        lowe_ref[...] = nn(f_ref[...], le_ref[...]).astype(BF)
        ranks_ref[...] = (SCALING * nt(g_ref[...], rs_ref[...])).astype(BF)
        lows_ref[...] = jnp.zeros_like(lows_ref)
        ranke_ref[...] = jnp.zeros_like(ranke_ref)
        shrunk_ref[...] = jnp.zeros_like(shrunk_ref)
        gfeed_ref[...] = jnp.zeros_like(gfeed_ref)

    g, f, ranks = g_ref[...], f_ref[...], ranks_ref[...]
    expanded = nn(f, we_ref[...]) + SCALING * nn(lowe_ref[...], re_ref[...])
    bell = 0.5 * (1.0 + lax.erf(expanded * 0.7071067811865476))
    act = (expanded * bell).astype(BF)
    slope = bell + expanded * (0.3989422804014327 * jnp.exp(-0.5 * expanded * expanded))
    lows_ref[...] += nn(act, ls_ref[...])
    shrunk_ref[...] += nn(act, ws_ref[...])
    grad_act = nt(g, ws_ref[...]) + nt(ranks, ls_ref[...])
    grad_expanded = (grad_act * slope).astype(BF)
    gfeed_ref[...] += nt(grad_expanded, we_ref[...])
    ranke_ref[...] += nt(grad_expanded, re_ref[...])
    units = step * (width // RANK)
    packing.put_columns(pack_ref, FEED_UNITS["expand_right"] + units, SCALING * tn(lowe_ref[...], grad_expanded))
    packing.put_rows(pack_ref, FEED_UNITS["shrink_left"] + units, tn(act, ranks))

    @pl.when(step == pl.num_programs(0) - 1)
    def _():
        low = lows_ref[...].astype(BF)
        shrunk_ref[...] += SCALING * nn(low, rs_ref[...])
        packing.put_columns(pack_ref, FEED_UNITS["shrink_right"], SCALING * tn(low, g))
        ranke = (SCALING * ranke_ref[...]).astype(BF)
        gfeed_ref[...] += nt(ranke, le_ref[...])
        packing.put_rows(pack_ref, FEED_UNITS["expand_left"], tn(f, ranke))


def feed(x, g, expand_weight, shrink_weight, expand_left, expand_right, shrink_left, shrink_right, gain, shift, packing):
    tokens = x.shape[0]
    width = 512
    whole = lambda shape: pl.BlockSpec(shape, lambda j: (0,) * len(shape))
    return pl.pallas_call(
        partial(feed_kernel, packing),
        grid=(FF // width,),
        in_specs=[
            whole((tokens, D)), whole((tokens, D)),
            pl.BlockSpec((D, width), lambda j: (0, j)),
            pl.BlockSpec((width, D), lambda j: (j, 0)),
            whole((D, RANK)),
            pl.BlockSpec((RANK, width), lambda j: (0, j)),
            pl.BlockSpec((width, RANK), lambda j: (j, 0)),
            whole((RANK, D)), whole((1, D)), whole((1, D)),
        ],
        out_specs=[whole((tokens, D)), whole((tokens, D)), whole((FEED_ROWS, RANK))],
        out_shape=[
            jax.ShapeDtypeStruct((tokens, D), F32),
            jax.ShapeDtypeStruct((tokens, D), F32),
            jax.ShapeDtypeStruct((FEED_ROWS, RANK), BF),
        ],
        scratch_shapes=[
            pltpu.VMEM((tokens, D), BF),
            pltpu.VMEM((tokens, RANK), BF), pltpu.VMEM((tokens, RANK), BF),
            pltpu.VMEM((tokens, RANK), F32), pltpu.VMEM((tokens, RANK), F32),
        ],
        compiler_params=pltpu.CompilerParams(vmem_limit_bytes=WIDE),
        cost_estimate=LITTLE,
        name="feed",
    )(x, g, expand_weight, shrink_weight, expand_left, expand_right, shrink_left, shrink_right, gain, shift)


def attend_kernel(first_row, my_rows, row_parts, head_parts, msg_ref, doc_ref, *refs):
    out_ref, rest_ref, vt_ref, kt_ref, dk_ref, dv_ref, cos_ref, sin_ref = refs[-8:]
    count, _, _, slots, _ = msg_ref.shape
    length = count * slots
    row = first_row
    if row_parts > 1:
        row = row + (lax.axis_index("seq") // head_parts) % row_parts * my_rows
    places = lax.broadcasted_iota(jnp.int32, (1, length), 1)
    starts = document_starts(doc_ref, row, places)
    cos_ref[...], sin_ref[...] = turning(places - starts)
    keys = msg_ref[:, 0, 1].reshape(length, PAIR)
    values = msg_ref[:, 0, 2].reshape(length, PAIR)
    kt_ref[...] = keys.T
    vt_ref[...] = values.T
    dk_ref[...] = jnp.zeros_like(dk_ref)
    dv_ref[...] = jnp.zeros_like(dv_ref)
    first_head = lax.broadcasted_iota(jnp.int32, (slots, PAIR), 1) < HEAD_DIM
    none = jnp.zeros((slots, PAIR), BF)

    def both(part):
        return jnp.concatenate([jnp.where(first_head, part, none), jnp.where(first_head, none, part)], axis=0)

    def merge(both_t):
        return jnp.concatenate([both_t[:HEAD_DIM, :slots], both_t[HEAD_DIM:, slots:]], axis=0).T

    def front(block):
        here = slice(block * slots, (block + 1) * slots)
        seen = (block + 1) * slots
        query = both(msg_ref[block, 0, 0] * BF(0.125))
        grad = both(msg_ref[block, 0, 3])
        query_t, grad_t = query.T, grad.T
        start = jnp.concatenate([starts[:, here]] * 2, axis=1)
        place = jnp.concatenate([places[:, here]] * 2, axis=1)
        scores = nn(keys[:seen], query_t)
        key_place = lax.broadcasted_iota(jnp.int32, scores.shape, 0)
        allowed = key_place >= start
        if block:
            last = (key_place[-slots:] <= place) & allowed[-slots:]
            scores = jnp.concatenate(
                [jnp.where(allowed[:-slots], scores[:-slots], NEGATIVE), jnp.where(last, scores[-slots:], NEGATIVE)], axis=0
            )
        else:
            scores = jnp.where(allowed & (key_place <= place), scores, NEGATIVE)
        return scores, query, grad_t

    def back(block, scores, query, grad_t):
        here = slice(block * slots, (block + 1) * slots)
        seen = (block + 1) * slots
        top = jnp.max(scores, axis=0, keepdims=True)
        weights = jnp.exp(scores - top)
        inverse = 1.0 / jnp.sum(weights, axis=0, keepdims=True)
        low = weights.astype(BF)
        out_t = nn(vt_ref[:, :seen], low) * inverse
        scaled_t = grad_t.astype(F32) * inverse
        delta = jnp.sum(out_t * scaled_t, axis=0, keepdims=True)
        scaled_t = scaled_t.astype(BF)
        grad_probs = nn(values[:seen], scaled_t)
        grad_scores = (weights * (grad_probs - delta)).astype(BF)
        dv_ref[:seen] += nn(low, scaled_t.T)
        dk_ref[:seen] += nn(grad_scores, query)
        query_grad_t = nn(kt_ref[:, :seen], grad_scores)
        out_ref[block, 0] = merge(out_t).astype(BF)
        query_grad = turn(0.125 * merge(query_grad_t), cos_ref[here], -sin_ref[here])
        rest_ref[block, 0, 0] = query_grad.astype(BF)

    ready = front(0)
    for block in range(count):
        later = front(block + 1) if block + 1 < count else None
        back(block, *ready)
        ready = later
    for block in range(count):
        here = slice(block * slots, (block + 1) * slots)
        rest_ref[block, 0, 1] = turn(dk_ref[here], cos_ref[here], -sin_ref[here]).astype(BF)
        rest_ref[block, 0, 2] = dv_ref[here].astype(BF)


def attend(message, doc_lengths, row, earlier, row_parts, head_parts):
    count, rows, _, slots, _ = message.shape
    length = count * slots
    return pl.pallas_call(
        partial(attend_kernel, row, rows, row_parts, head_parts),
        grid=(1,),
        in_specs=[
            pl.BlockSpec((count, 1, 4, slots, PAIR), lambda r: (0, row, 0, 0, 0)),
            pl.BlockSpec(memory_space=pltpu.SMEM),
        ] + [pl.BlockSpec(memory_space=pl.ANY)] * len(earlier),
        out_specs=[
            pl.BlockSpec((count, 1, slots, PAIR), lambda r: (0, row, 0, 0)),
            pl.BlockSpec((count, 1, 3, slots, PAIR), lambda r: (0, row, 0, 0, 0)),
        ],
        out_shape=[
            jax.ShapeDtypeStruct((count, rows, slots, PAIR), BF),
            jax.ShapeDtypeStruct((count, rows, 3, slots, PAIR), BF),
        ],
        input_output_aliases={2 + k: k for k in range(len(earlier))},
        scratch_shapes=[
            pltpu.VMEM((PAIR, length), BF), pltpu.VMEM((PAIR, length), BF),
            pltpu.VMEM((length, PAIR), F32), pltpu.VMEM((length, PAIR), F32),
            pltpu.VMEM((length, PAIR), F32), pltpu.VMEM((length, PAIR), F32),
        ],
        compiler_params=pltpu.CompilerParams(vmem_limit_bytes=WIDE),
        cost_estimate=LITTLE if row else MUCH,
        name="attend",
    )(message, doc_lengths, *earlier)


def finish_proj_kernel(
    packing, att_ref, x_ref, g_ref, shrunk_ref, wp_ref, lp_ref, rp_ref, rankp_ref, out_ref, pack_ref,
):
    pairs, rows, slots, _ = att_ref.shape
    attended = jnp.concatenate([att_ref[pair].reshape(rows * slots, PAIR) for pair in range(pairs)], axis=1)
    low = nn(attended, lp_ref[...]).astype(BF)
    packing.put_rows(pack_ref, PROJ_UNITS["proj_left"], tn(attended, rankp_ref[...]))
    packing.put_columns(pack_ref, PROJ_UNITS["proj_right"], SCALING * tn(low, g_ref[...]))
    projected = nn(attended, wp_ref[...]) + SCALING * nn(low, rp_ref[...])
    out_ref[...] = (x_ref[...].astype(F32) + projected + shrunk_ref[...]).astype(BF)


def finish_proj(attended, x, g, shrunk, proj_weight, proj_left, proj_right, rank_proj, packing):
    tokens = x.shape[0]
    return pl.pallas_call(
        partial(finish_proj_kernel, packing),
        out_shape=[jax.ShapeDtypeStruct((tokens, D), BF), jax.ShapeDtypeStruct((PROJ_ROWS, RANK), BF)],
        compiler_params=pltpu.CompilerParams(vmem_limit_bytes=WIDE),
        cost_estimate=MUCH,
        name="finish_proj",
    )(attended, x, g, shrunk, proj_weight, proj_left, proj_right, rank_proj)


def gathered(msg_ref):
    pairs, rows, parts, slots, _ = msg_ref.shape
    return jnp.concatenate(
        [msg_ref[pair, :, part].reshape(rows * slots, PAIR) for part in range(parts) for pair in range(pairs)], axis=1
    )


def finish_kernel(
    packing, msg_ref, x_ref, g_ref, gfeed_ref, wj_ref, lj_ref, rj_ref,
    mgain_ref, mshift_ref, fgain_ref, igrad_ref, pack_ref, wj_here, sems,
):
    third = lambda ref, part: ref.at[:, pl.ds(part * D, D)]
    copies = [pltpu.make_async_copy(third(wj_ref, part), third(wj_here, part), sems.at[part]) for part in range(3)]
    for copy in copies:
        copy.start()
    x, g = x_ref[...].astype(F32), g_ref[...]
    hat, scale = normalised(x)
    joined = gathered(msg_ref)
    rank = (SCALING * nt(joined, rj_ref[...])).astype(BF)
    u = (hat * mgain_ref[...] + mshift_ref[...]).astype(BF)
    packing.put_rows(pack_ref, LATE_UNITS["joined_left"], tn(u, rank))
    grad_mixer = nt(rank, lj_ref[...])
    for part in range(3):
        columns = slice(part * D, (part + 1) * D)
        copies[part].wait()
        grad_mixer = grad_mixer + nt(joined[:, columns], wj_here[:, columns])
    grad_feed = gfeed_ref[...]
    mixer_hat, feed_hat = grad_mixer * hat, grad_feed * hat
    sums = [jnp.sum(v, axis=0, keepdims=True) for v in (mixer_hat, grad_mixer, feed_hat, grad_feed)]
    pieces = [v[:, c * RANK : (c + 1) * RANK] for v in sums for c in range(D // RANK)]
    norms = jnp.concatenate(pieces + [jnp.zeros((RANK - len(pieces), RANK), F32)], axis=0)
    packing.put_rows(pack_ref, LATE_UNITS["norms"], norms)
    pulled = grad_mixer * mgain_ref[...] + grad_feed * fgain_ref[...]
    along = jnp.mean(pulled * hat, axis=-1, keepdims=True)
    level = jnp.mean(pulled, axis=-1, keepdims=True)
    igrad_ref[...] = (g.astype(F32) + scale * (pulled - level - hat * along)).astype(BF)


def finish(message, x, g, grad_feed, joined_weight, joined_left, joined_right,
           mixer_gain, mixer_shift, feed_gain, packing):
    tokens = x.shape[0]
    held = pl.BlockSpec(memory_space=pltpu.VMEM)
    return pl.pallas_call(
        partial(finish_kernel, packing),
        in_specs=[held] * 4 + [pl.BlockSpec(memory_space=pl.ANY)] + [held] * 5,
        out_shape=[jax.ShapeDtypeStruct((tokens, D), BF), jax.ShapeDtypeStruct((LATE_ROWS, RANK), BF)],
        scratch_shapes=[pltpu.VMEM((D, 3 * D), BF), pltpu.SemaphoreType.DMA((3,))],
        compiler_params=pltpu.CompilerParams(vmem_limit_bytes=WIDE),
        cost_estimate=MUCH,
        name="finish",
    )(message, x, g, grad_feed, joined_weight, joined_left, joined_right,
      mixer_gain, mixer_shift, feed_gain)


def right_kernel(packing, head_parts, rest_ref, low_ref, pack_ref):
    count, rows, _, slots, _ = rest_ref.shape
    low = low_ref[...].reshape(count * rows * slots, RANK)
    if packing.rows > 3 * RANK:
        pack_ref[...] = jnp.zeros_like(pack_ref)
    for part in range(3):
        value = SCALING * tn(low, rest_ref[:, :, part].reshape(count * rows * slots, PAIR))
        if head_parts > 1:
            moved = pltpu.roll(value, HEAD_DIM, 1)
            value = jnp.where(lax.axis_index("seq") % head_parts == 0, value, moved)
        packing.put_own(pack_ref, part, value.astype(BF))


def right(rest, low, packing, head_parts):
    return pl.pallas_call(
        partial(right_kernel, packing, head_parts),
        out_shape=jax.ShapeDtypeStruct((packing.rows, RANK), BF),
        compiler_params=pltpu.CompilerParams(vmem_limit_bytes=WIDE),
        cost_estimate=MUCH,
        name="right",
    )(rest, low)


def swap(part, bit, size):
    return lax.ppermute(part, ("batch", "seq"), [(i, i ^ bit) for i in range(size)])


def unpack_kernel(units, count, *refs):
    part_refs, out_refs, (pack_ref, sems) = refs[:count], refs[count:-2], refs[-2:]
    copies, row = [], 0
    for place, part_ref in enumerate(part_refs):
        rows = part_ref.shape[0]
        copies.append(pltpu.make_async_copy(part_ref, pack_ref.at[pl.ds(row, rows)], sems.at[place]))
        row += rows
    for copy in copies:
        copy.start()
    for copy in copies:
        copy.wait()
    for (packing, unit, shape, kind), out_ref in zip(units, out_refs):
        if kind == "columns":
            for step in range(shape[1] // RANK):
                out_ref[:, step * RANK : (step + 1) * RANK] = packing.get(pack_ref, unit + step).astype(F32)
        elif kind == "rows":
            for step in range(shape[0] // RANK):
                out_ref[step * RANK : (step + 1) * RANK] = packing.get(pack_ref, unit + step).astype(F32)
        else:
            out_ref[...] = packing.get(pack_ref, unit)[kind * 8 : (kind + 1) * 8].astype(F32)


def unpack(parts, units):
    rows = sum(part.shape[0] for part in parts)
    return pl.pallas_call(
        partial(unpack_kernel, units, len(parts)),
        in_specs=[pl.BlockSpec(memory_space=pl.ANY)] * len(parts),
        out_shape=[jax.ShapeDtypeStruct(shape, F32) for _, _, shape, _ in units],
        scratch_shapes=[pltpu.VMEM((rows, RANK), BF), pltpu.SemaphoreType.DMA((len(parts),))],
        compiler_params=pltpu.CompilerParams(vmem_limit_bytes=WIDE),
        cost_estimate=LITTLE,
        name="unpack",
    )(*parts)


def per_device(
    block_input, doc_lengths, out_grad, joined_weight, proj_weight, expand_weight, shrink_weight,
    joined_left, joined_right, proj_left, proj_right, expand_left, expand_right, shrink_left,
    shrink_right, mixer_gain, mixer_shift, feed_gain, feed_shift,
):
    rows, slots = block_input.shape[:2]
    tokens = rows * slots
    devices, batches = lax.axis_size("seq"), lax.axis_size("batch")
    size = devices * batches
    me = lax.axis_index("seq")
    length = devices * slots
    x = block_input.reshape(tokens, D)
    g = out_grad.reshape(tokens, D)
    mixer_gain, mixer_shift = mixer_gain.reshape(1, D), mixer_shift.reshape(1, D)
    feed_gain, feed_shift = feed_gain.reshape(1, D), feed_shift.reshape(1, D)

    pair_parts = min(devices, PAIRS)
    row_parts = min(devices // pair_parts, rows)
    head_parts = devices // (pair_parts * row_parts)
    my_rows = rows // row_parts
    lanes = PAIR // head_parts

    def bits(first, count):
        return [first + step for step in range(count.bit_length() - 1)]

    seq_bits = bits(0, devices)
    order = bits(len(seq_bits), batches) + seq_bits
    shared = row_parts * head_parts
    own = order[: batches.bit_length() - 1] + bits(0, shared)
    feed_packing = Packing(FEED_ROWS, order)
    right_packing = PairPacking(order, own, seq_bits[shared.bit_length() - 1 :])
    proj_packing, late_packing = Packing(PROJ_ROWS, order[:3]), Packing(LATE_ROWS, order[:3])

    message, low_joined, rank_proj = project(
        x, g, joined_weight, proj_weight, joined_left, joined_right, proj_left, proj_right,
        mixer_gain, mixer_shift, doc_lengths, rows,
    )

    def send(units):
        if row_parts * head_parts > 1:
            units = units.reshape(PAIRS, row_parts, my_rows, 4, slots, head_parts, lanes)
            units = jnp.transpose(units, (0, 1, 5, 2, 3, 4, 6))
        units = units.reshape(devices, my_rows, 4, slots, lanes)
        return lax.all_to_all(units, "seq", 0, 0, tiled=True)

    def send_back(units):
        parts = units.shape[2] if units.ndim == 5 else 1
        units = lax.all_to_all(units[..., :lanes], "seq", 0, 0, tiled=True)
        if row_parts * head_parts > 1:
            units = units.reshape(PAIRS, row_parts, head_parts, my_rows, parts, slots, lanes)
            units = jnp.transpose(units, (0, 1, 3, 4, 5, 2, 6))
            units = units.reshape((PAIRS, rows, parts, slots, PAIR))
            units = units if parts > 1 else units[:, :, 0]
        return units

    arrived = send(message)
    if lanes < PAIR:
        arrived = jnp.pad(arrived, ((0, 0),) * 4 + ((0, PAIR - lanes),))

    shrunk, grad_feed, feed_pack = feed(
        after(x, message), g, expand_weight, shrink_weight, expand_left, expand_right, shrink_left, shrink_right,
        feed_gain, feed_shift, feed_packing,
    )

    part, steps = feed_pack, list(order)
    part = halve(part, steps.pop(0), size)
    low_all = after(jnp.broadcast_to(low_joined, (devices, tokens, RANK)), part)
    low_all = lax.all_to_all(after(low_all, arrived), "seq", 0, 0, tiled=True)
    answer = attend(arrived, doc_lengths, 0, (), row_parts, head_parts)
    part = halve(part, steps.pop(0), size, *answer)
    for row in range(1, my_rows):
        answer = attend(arrived, doc_lengths, row, answer, row_parts, head_parts)
    attended, rest = answer
    while len(steps) > 2:
        part = halve(part, steps.pop(0), size, *answer)
    attended = send_back(after(attended, part, low_all))

    low_all = low_all.reshape(devices, rows, slots, RANK)
    first_row = (me // head_parts) % row_parts * my_rows
    if row_parts > 1:
        low_all = lax.dynamic_slice_in_dim(low_all, first_row, my_rows, 1)
    right_part = right(rest, low_all, right_packing, head_parts)
    part = quarter(part, steps, size, right_part)
    for bit in own:
        right_part = halve(right_part, bit, size)
    stride = part.shape[0] + right_part.shape[0]
    early = jnp.concatenate([part, right_part])
    returned = send_back(after(rest, attended, early))

    output, proj_part = finish_proj(
        attended, x, g, shrunk, proj_weight, proj_left, proj_right, rank_proj, proj_packing
    )
    early = join(everyone(early, steps, size, output))
    early = double(early, order[-3], size)
    for bit in order[:2]:
        proj_part = halve(proj_part, bit, size)
    input_grad, late_part = finish(
        returned, after(x, early), g, grad_feed, joined_weight, joined_left, joined_right,
        mixer_gain, mixer_shift, feed_gain, late_packing,
    )
    proj_part = halve(proj_part, order[2], size, late_part)
    for bit in order[-4:0:-1]:
        early = double(early, bit, size, late_part)
    late_part = after(late_part, early)
    early = [early, swap(early, 1 << order[0], size)]
    feed_packing, right_packing = feed_packing.held(stride, 0), right_packing.held(stride, part.shape[0])
    early_grads = unpack(early, (
        (feed_packing, FEED_UNITS["expand_left"], (D, RANK), "rows"),
        (feed_packing, FEED_UNITS["expand_right"], (RANK, FF), "columns"),
        (feed_packing, FEED_UNITS["shrink_left"], (FF, RANK), "rows"),
        (feed_packing, FEED_UNITS["shrink_right"], (RANK, D), "columns"),
        (right_packing, 0, (RANK, 3 * D), "columns"),
    ))

    for bit in order[:3]:
        late_part = halve(late_part, bit, size)
    stride, first = proj_part.shape[0] + late_part.shape[0], late_part.shape[0]
    late = jnp.concatenate([late_part, proj_part])
    for bit in order[3:-2]:
        late = add_low(late, swap(late, 1 << bit, size))
    whole_late = everyone(late, order[-2:], size, *early_grads)
    late = add_all(whole_late[0], whole_late[1:])
    for bit in order[2:0:-1]:
        late = double(late, bit, size)
    late = [late, swap(late, 1 << order[0], size)]
    late_packing, proj_packing = late_packing.held(stride, 0), proj_packing.held(stride, first)
    late_grads = unpack(late, (
        (late_packing, LATE_UNITS["joined_left"], (D, RANK), "rows"),
        (proj_packing, PROJ_UNITS["proj_left"], (D, RANK), "rows"),
        (proj_packing, PROJ_UNITS["proj_right"], (RANK, D), "columns"),
    ) + tuple((late_packing, LATE_UNITS["norms"], (8, RANK), which) for which in range(4)))
    return (
        output.reshape(rows, slots, D), input_grad.reshape(rows, slots, D),
        late_grads[0], early_grads[4], late_grads[1], late_grads[2],
        early_grads[0], early_grads[1], early_grads[2], early_grads[3],
    ) + tuple(norm.reshape(D) for norm in late_grads[3:])


def solution(mesh):
    act = P("batch", "seq", None)
    return jax.shard_map(
        per_device,
        mesh=mesh,
        in_specs=(act, P("batch", None), act) + (P(),) * 16,
        out_specs=(act, act) + (P(),) * 12,
        check_vma=False,
    )
```

time: 264 us -> 220 us (0.83)
  local copies, waits for them, and re-layouts: 42.9 us -> 11.7 us
  other arithmetic: 36.7 us -> 8.82 us
  Pallas kernels: 50 us -> 72 us
  waiting for transfers between devices: 94.7 us -> 76.9 us
  starting transfers between devices: 36.9 us -> 48 us
    ppermute x20 -> x26, waiting for transfers between devices: 81.1 us -> 47.8 us  [swap(): lax.ppermute(part, ('batch', 'seq'), [(i, i ^ bit) for i in range(size)])]
    unnamed x92 -> x32, local copies, waits for them, and re-layouts: 37.9 us -> 5.12 us
    pallas_call x4 -> x10, Pallas kernels: 50 us -> 72 us  [the longest x1 21 us: feed(): pl.pallas_call(partial(feed_kernel, packing), grid=(FF // width,), in_spe...]
    select_n x11 -> x0, other arithmetic: 15.9 us -> none  [the longest x10 10.7 us: summed(): jnp.where(me & bit == 0, jnp.concatenate([packed, other]), jnp.concatenat...]
    mul x2 -> x0, other arithmetic: 6.07 us -> none  [tables(): return (jnp.cos(angles), jnp.sin(angles) * sign)]
    all_to_all x1, waiting for transfers between devices: 13.7 us -> 19.5 us  [send(): return lax.all_to_all(units, 'seq', 0, 0, tiled=True)]
    slice x2 -> x12, local copies, waits for them, and re-layouts: 0.09 us -> 5.73 us  [the longest x11 5.04 us: halve(): packed[half:]]
    all_to_all x1 -> x2, starting transfers between devices: 4.58 us -> 10.1 us  [send_back(): units = lax.all_to_all(units[..., :lanes], 'seq', 0, 0, tiled=True)]
  transfers between devices with their start and end apart: 22 -> 30, of which waited for: 15 -> 15; matrix products, arithmetic and copies ran while one was open for 12% -> 6% of each run, Pallas kernels for 17% -> 28%
where the time goes in v2:
time: 220 us; the launch traced here: 219 us
  waiting for transfers between devices  76.9 us (35%)
  Pallas kernels  72 us (33%)
  starting transfers between devices  48 us (22%)
  local copies, waits for them, and re-layouts  11.7 us (5%)
  other arithmetic  8.82 us (4%)
    ppermute x26, waiting for transfers between devices, swap(): lax.ppermute(part, ('batch', 'seq'), [(i, i ^ bit) for i in range(size)])  47.8 us
    ppermute x26, starting transfers between devices, swap(): lax.ppermute(part, ('batch', 'seq'), [(i, i ^ bit) for i in range(size)])  27 us
    pallas_call x1, Pallas kernels, feed(): pl.pallas_call(partial(feed_kernel, packing), grid=(FF // width,), in_spe...  21 us
    all_to_all x1, waiting for transfers between devices, send(): return lax.all_to_all(units, 'seq', 0, 0, tiled=True)  19.5 us
    pallas_call x2, Pallas kernels, attend(): pl.pallas_call(partial(attend_kernel, row, rows, row_parts, head_parts),...  15.7 us
    all_to_all x2, starting transfers between devices, send_back(): units = lax.all_to_all(units[..., :lanes], 'seq', 0, 0, tiled=True)  10.1 us
    pallas_call x1, Pallas kernels, finish(): pl.pallas_call(partial(finish_kernel, packing), in_specs=[held] * 4 + [pl...  9.25 us
    pallas_call x1, Pallas kernels, project(): pl.pallas_call(project_kernel, in_specs=[held, held, away, away] + [held]...  8.82 us
  transfers between devices with their start and end apart: 30, of which 15 were waited for; matrix products, arithmetic and copies ran while one was open for 6% of the time, Pallas kernels for 28%

profile of v2, /device:TPU:0, one launch (start us, length us, event | category | flops | bytes accessed | tf_op | source)
XLA Modules:
  0.0 218.7 jit_solution(9979518018671977252)
XLA Ops:
  0.6 8.8 %project.1 = (bf16[8,2,4,128,128]{4,3,2,1,0:T(8,128)(2,1)}, bf16[256,128]{1,0:T(8,128)(2,1)}, bf16[256,128]{1,0:T(8,128)(2,1)}) custom-call(bf16[256,1024]{1,0:T(8,128)(2,1)} %bitcast.13, bf16[256,1024]{1,0:T(8,128)(2,1)} %bitcast.17, bf16[1024,3072]{1,0:T(8,128)(2,1)} %wj_ref.3, bf16[1024,1024]{1,0:T(8,128)(2,1)} %wp_ref.3, bf16[1024,128]{1,0:T(8,128)(2,1)} %lj_ref.3, ...), custom_call_target="tpu_custom_call" | custom-call | flops 1 | bytes 1 | tf_op jit(solution)/shard_map/project/pallas_call | solution.py:276
  9.5 7.3 %all-to-all-start = ((bf16[8,2,4,128,128]{4,3,2,1,0:T(8,128)(2,1)}), bf16[8,2,4,128,128]{4,3,2,1,0:T(8,128)(2,1)S(1)}, u32[]{:S(2)}, u32[]{:S(2)}) async-start(bf16[8,2,4,128,128]{4,3,2,1,0:T(8,128)(2,1)} %get-tuple-element.60), calls=%async_computation | async-start | bytes 4194304 | tf_op jit(solution)/shard_map/all_to_all | solution.py:657
  16.8 21.0 %feed.1 = (f32[256,1024]{1,0:T(8,128)}, f32[256,1024]{1,0:T(8,128)}, bf16[10240,128]{1,0:T(8,128)(2,1)}) custom-call(bf16[256,1024]{1,0:T(8,128)(2,1)} %bitcast.14, bf16[256,1024]{1,0:T(8,128)(2,1)} %bitcast.18, bf16[1024,4096]{1,0:T(8,128)(2,1)} %we_ref.1, bf16[4096,1024]{1,0:T(8,128)(2,1)} %ws_ref.1, bf16[1024,128]{1,0:T(8,128)(2,1)} %le_ref.1, ...), custom_call_target="tpu_custom_call" | custom-call | flops 1 | bytes 1 | tf_op jit(solution)/shard_map/feed/pallas_call | solution.py:340
  37.8 1.6 slice.83
  39.4 3.0 %collective-permute-done = bf16[5120,128]{1,0:T(8,128)(2,1)S(1)} collective-permute-done((bf16[5120,128]{1,0:T(8,128)(2,1)S(1)}, bf16[5120,128]{1,0:T(8,128)(2,1)S(1)}, u32[]{:S(2)}, u32[]{:S(2)}) %collective-permute-start) | collective-permute-done | bytes 1310752 | tf_op jit(solution)/shard_map/ppermute | solution.py:576
  42.4 0.3 add_convert_fusion
  42.8 1.0 slice.109
  43.7 0.3 copy-done.2
  44.0 1.5 collective-permute-start.1
  45.5 19.5 %all-to-all-done.msg_ref = bf16[8,2,4,128,128]{4,3,2,1,0:T(8,128)(2,1)S(1)} async-done(((bf16[8,2,4,128,128]{4,3,2,1,0:T(8,128)(2,1)}), bf16[8,2,4,128,128]{4,3,2,1,0:T(8,128)(2,1)S(1)}, u32[]{:S(2)}, u32[]{:S(2)}) %all-to-all-start) | async-done | bytes 2097184 | tf_op jit(solution)/shard_map/all_to_all | solution.py:657
  65.0 1.3 copy-done
  66.3 7.9 %attend.2 = (bf16[8,2,128,128]{3,2,1,0:T(8,128)(2,1)}, bf16[8,2,3,128,128]{4,3,2,1,0:T(8,128)(2,1)}) custom-call(bf16[8,2,4,128,128]{4,3,2,1,0:T(8,128)(2,1)} %copy-done, s32[2,8]{1,0:T(2,128)} %doc_ref.5), custom_call_target="tpu_custom_call" | custom-call | flops 199999995904 | bytes 1 | tf_op jit(solution)/shard_map/attend/pallas_call | solution.py:448
  74.2 1.3 add_convert_fusion.1
  75.5 1.5 collective-permute-start.2
  77.1 0.9 broadcast_in_dim.3
  77.9 3.7 %all-to-all-start.1 = ((bf16[8,256,128]{2,1,0:T(8,128)(2,1)}), bf16[8,256,128]{2,1,0:T(8,128)(2,1)S(1)}, u32[]{:S(2)}, u32[]{:S(2)}) async-start(bf16[8,256,128]{2,1,0:T(8,128)(2,1)} %broadcast_in_dim.3), calls=%async_computation.1 | async-start | bytes 1048576 | tf_op jit(solution)/shard_map/all_to_all | solution.py:681
  81.7 7.8 %attend.3 = (bf16[8,2,128,128]{3,2,1,0:T(8,128)(2,1)}, bf16[8,2,3,128,128]{4,3,2,1,0:T(8,128)(2,1)}) custom-call(bf16[8,2,4,128,128]{4,3,2,1,0:T(8,128)(2,1)} %copy-done, s32[2,8]{1,0:T(2,128)} %doc_ref.5, bf16[8,2,128,128]{3,2,1,0:T(8,128)(2,1)} %get-tuple-element.61.refs_0_, ...), custom_call_target="tpu_custom_call", output_to_operand_aliasing={{0}: (2, {}), {1}: (3, {})} | custom-call | flops 1 | bytes 1 | tf_op jit(solution)/shard_map/attend/pallas_call | solution.py:448
  89.5 0.7 copy-done.10
  90.3 0.7 fusion
  91.0 3.6 %collective-permute-start.5 = (bf16[320,128]{1,0:T(8,128)(2,1)}, bf16[320,128]{1,0:T(8,128)(2,1)}, u32[]{:S(2)}, u32[]{:S(2)}) collective-permute-start(bf16[320,128]{1,0:T(8,128)(2,1)} %get-tuple-element.107), channel_id=1, source_target_pairs={{0,6},{1,7},{2,4},{3,5},{4,2},{5,3},{6,0},{7,1},{8,14},{9,15},{10,... | collective-permute-start | bytes 245768 | tf_op jit(solution)/shard_map/ppermute | solution.py:576
  94.6 0.7 collective-permute-start.3
  95.3 4.8 %all-to-all-done.1 = bf16[8,256,128]{2,1,0:T(8,128)(2,1)S(1)} async-done(((bf16[8,256,128]{2,1,0:T(8,128)(2,1)}), bf16[8,256,128]{2,1,0:T(8,128)(2,1)S(1)}, u32[]{:S(2)}, u32[]{:S(2)}) %all-to-all-start.1) | async-done | bytes 524320 | tf_op jit(solution)/shard_map/all_to_all | solution.py:681
  100.2 4.2 %all-to-all-start.2 = ((bf16[8,2,128,128]{3,2,1,0:T(8,128)(2,1)}), bf16[8,2,128,128]{3,2,1,0:T(8,128)(2,1)}, u32[]{:S(2)}, u32[]{:S(2)}) async-start(bf16[8,2,128,128]{3,2,1,0:T(8,128)(2,1)} %get-tuple-element.72), calls=%async_computation.2 | async-start | bytes 1048576 | tf_op jit(solution)/shard_map/all_to_all | solution.py:661
  104.4 2.8 %right.1 = bf16[384,128]{1,0:T(8,128)(2,1)} custom-call(bf16[8,2,3,128,128]{4,3,2,1,0:T(8,128)(2,1)} %get-tuple-element.79.rest_ref, bf16[8,2,128,128]{3,2,1,0:T(8,128)(2,1)} %bitcast.21), custom_call_target="tpu_custom_call" | custom-call | flops 199999995904 | bytes 1 | tf_op jit(solution)/shard_map/right/pallas_call | solution.py:566
  107.1 0.8 slice.117
  108.0 1.2 collective-permute-done.6
  109.2 0.8 add_convert_fusion.10
  110.0 1.6 collective-permute-start.7
  111.6 1.1 add_convert_fusion.7
  112.6 1.3 collective-permute-done.7
  113.9 0.7 pad_maximum_fusion.4.refs_0_
  114.6 2.8 %collective-permute-start.8 = (bf16[416,128]{1,0:T(8,128)(2,1)}, bf16[416,128]{1,0:T(8,128)(2,1)}, u32[]{:S(2)}, u32[]{:S(2)}) collective-permute-start(bf16[416,128]{1,0:T(8,128)(2,1)} %pad_maximum_fusion.4.refs_0_), channel_id=1, source_target_pairs={{0,4},{1,5},{2,6},{3,7},{4,0},{5,1},{6,2},{7,3},{8,12},{9,13},{10,... | collective-permute-start | bytes 319496 | tf_op jit(solution)/shard_map/ppermute | solution.py:576
  117.4 1.5 collective-permute-start.9
  119.0 5.9 %all-to-all-start.3 = ((bf16[8,2,3,128,128]{4,3,2,1,0:T(8,128)(2,1)}), bf16[8,2,3,128,128]{4,3,2,1,0:T(8,128)(2,1)}, u32[]{:S(2)}, u32[]{:S(2)}) async-start(bf16[8,2,3,128,128]{4,3,2,1,0:T(8,128)(2,1)} %get-tuple-element.79.rest_ref), calls=%async_computation.3 | async-start | bytes 3145728 | tf_op jit(solution)/shard_map/all_to_all | solution.py:661
  124.9 4.7 %finish_proj.1 = (bf16[256,1024]{1,0:T(8,128)(2,1)}, bf16[2048,128]{1,0:T(8,128)(2,1)}) custom-call(bf16[8,2,128,128]{3,2,1,0:T(8,128)(2,1)} %all-to-all-done.2.att_ref, bf16[256,1024]{1,0:T(8,128)(2,1)} %bitcast.15, bf16[256,1024]{1,0:T(8,128)(2,1)} %bitcast.19, f32[256,1024]{1,0:T(8,128)} %get-tuple-element.73.shrunk_ref, bf16[1024,1024]{1,0:T(8,128)(2,1)} %wp_ref.3, ...), custom_call_target="tpu_custom_call" | custom-call | flops 199999995904 | bytes 1 | tf_op jit(solution)/shard_map/finish_proj/pallas_call | solution.py:489
  129.6 1.8 join.1
  131.4 2.0 collective-permute-start.11
  133.5 1.7 slice.103
  135.1 16.9 %collective-permute-done.11 = bf16[1664,128]{1,0:T(8,128)(2,1)S(1)} collective-permute-done((bf16[1664,128]{1,0:T(8,128)(2,1)}, bf16[1664,128]{1,0:T(8,128)(2,1)S(1)}, u32[]{:S(2)}, u32[]{:S(2)}) %collective-permute-start.11) | collective-permute-done | bytes 426016 | tf_op jit(solution)/shard_map/ppermute | solution.py:576
  152.0 0.8 copy-done.7
  152.8 2.0 pad_maximum_fusion.1
  154.7 1.5 collective-permute-start.12
  156.2 4.7 %all-to-all-done.3.msg_ref = bf16[8,2,3,128,128]{4,3,2,1,0:T(8,128)(2,1)} async-done(((bf16[8,2,3,128,128]{4,3,2,1,0:T(8,128)(2,1)}), bf16[8,2,3,128,128]{4,3,2,1,0:T(8,128)(2,1)}, u32[]{:S(2)}, u32[]{:S(2)}) %all-to-all-start.3) | async-done | bytes 1572896 | tf_op jit(solution)/shard_map/all_to_all | solution.py:661
  161.0 9.3 %finish.1 = (bf16[256,1024]{1,0:T(8,128)(2,1)}, bf16[1152,128]{1,0:T(8,128)(2,1)}) custom-call(bf16[8,2,3,128,128]{4,3,2,1,0:T(8,128)(2,1)} %all-to-all-done.3.msg_ref, bf16[256,1024]{1,0:T(8,128)(2,1)} %bitcast.16, bf16[256,1024]{1,0:T(8,128)(2,1)} %bitcast.20, f32[256,1024]{1,0:T(8,128)} %get-tuple-element.84.gfeed_ref, bf16[1024,3072]{1,0:T(8,128)(2,1)} %wj_ref.3, ...), custom_call_target="tpu_custom_call" | custom-call | flops 199999995904 | bytes 1 | tf_op jit(solution)/shard_map/finish/pallas_call | solution.py:540
  170.2 3.8 %collective-permute-done.12 = bf16[3328,128]{1,0:T(8,128)(2,1)} collective-permute-done((bf16[3328,128]{1,0:T(8,128)(2,1)}, bf16[3328,128]{1,0:T(8,128)(2,1)}, u32[]{:S(2)}, u32[]{:S(2)}) %collective-permute-start.12) | collective-permute-done | bytes 852000 | tf_op jit(solution)/shard_map/ppermute | solution.py:576
  174.1 1.3 pad_maximum_fusion.refs_0_
  175.5 0.5 collective-permute-start.13
  176.1 1.0 add_convert_fusion.3
  177.1 1.6 collective-permute-start.17
  178.7 0.6 collective-permute-done.13
  179.3 1.6 collective-permute-start.14
  180.9 2.1 collective-permute-done.17
  183.2 4.3 %collective-permute-done.18 = bf16[256,128]{1,0:T(8,128)(2,1)S(1)} collective-permute-done((bf16[256,128]{1,0:T(8,128)(2,1)S(1)}, bf16[256,128]{1,0:T(8,128)(2,1)S(1)}, u32[]{:S(2)}, u32[]{:S(2)}) %collective-permute-start.18) | collective-permute-done | bytes 65568 | tf_op jit(solution)/shard_map/ppermute | solution.py:576
  187.6 3.9 %collective-permute-done.15 = bf16[144,128]{1,0:T(8,128)(2,1)S(1)} collective-permute-done((bf16[144,128]{1,0:T(8,128)(2,1)S(1)}, bf16[144,128]{1,0:T(8,128)(2,1)S(1)}, u32[]{:S(2)}, u32[]{:S(2)}) %collective-permute-start.15) | collective-permute-done | bytes 36896 | tf_op jit(solution)/shard_map/ppermute | solution.py:576
  191.5 3.7 %collective-permute-start.22 = (bf16[400,128]{1,0:T(8,128)(2,1)S(1)}, bf16[400,128]{1,0:T(8,128)(2,1)S(1)}, u32[]{:S(2)}, u32[]{:S(2)}) collective-permute-start(bf16[400,128]{1,0:T(8,128)(2,1)S(1)} %pad_maximum_fusion.5), channel_id=1, source_target_pairs={{0,6},{1,7},{2,4},{3,5},{4,2},{5,3},{6,0},{7,1},{8,14},{9,15},{10,... | collective-permute-start | bytes 307208 | tf_op jit(solution)/shard_map/ppermute | solution.py:576
  195.2 0.8 collective-permute-start.19
  196.0 1.2 copy-done.6
  197.2 5.5 %unpack.2 = (f32[1024,128]{1,0:T(8,128)}, f32[128,4096]{1,0:T(8,128)}, f32[4096,128]{1,0:T(8,128)}, f32[128,1024]{1,0:T(8,128)}, f32[128,3072]{1,0:T(8,128)}) custom-call(bf16[6656,128]{1,0:T(8,128)(2,1)} %copy-done.1, bf16[6656,128]{1,0:T(8,128)(2,1)} %copy-done.6), custom_call_target="tpu_custom_call" | custom-call | flops 1 | bytes 1 | tf_op jit(solution)/shard_map/unpack/pallas_call | solution.py:603
  202.9 4.6 %collective-permute-done.23 = bf16[400,128]{1,0:T(8,128)(2,1)S(1)} collective-permute-done((bf16[400,128]{1,0:T(8,128)(2,1)S(1)}, bf16[400,128]{1,0:T(8,128)(2,1)S(1)}, u32[]{:S(2)}, u32[]{:S(2)}) %collective-permute-start.23) | collective-permute-done | bytes 102432 | tf_op jit(solution)/shard_map/ppermute | solution.py:576
  207.5 1.6 collective-permute-start.24
  209.1 4.3 %collective-permute-done.24 = bf16[800,128]{1,0:T(8,128)(2,1)S(1)} collective-permute-done((bf16[800,128]{1,0:T(8,128)(2,1)S(1)}, bf16[800,128]{1,0:T(8,128)(2,1)S(1)}, u32[]{:S(2)}, u32[]{:S(2)}) %collective-permute-start.24) | collective-permute-done | bytes 204832 | tf_op jit(solution)/shard_map/ppermute | solution.py:576
  213.5 1.7 collective-permute-done.25.refs_1_
  215.2 0.8 copy-done.13
  216.0 2.5 %unpack.3 = (f32[1024,128]{1,0:T(8,128)}, f32[1024,128]{1,0:T(8,128)}, f32[128,1024]{1,0:T(8,128)}, f32[8,128]{1,0:T(8,128)}, f32[8,128]{1,0:T(8,128)}, /*index=5*/f32[8,128]{1,0:T(8,128)}, f32[8,128]{1,0:T(8,128)}) custom-call(bf16[1600,128]{1,0:T(8,128)(2,1)} %copy-done.9, bf16[1600,128]{1,0:T(8,128)(2,1)} %copy-done.13), custom_call_target="tpu_custom_call" | custom-call | flops 1 | bytes 1 | tf_op jit(solution)/shard_map/unpack/pallas_call | solution.py:603
  (70 shorter events, 1.1 us)
Async XLA Ops:
  9.5 55.5 %all-to-all-start = ((bf16[8,2,4,128,128]{4,3,2,1,0:T(8,128)(2,1)}), bf16[8,2,4,128,128]{4,3,2,1,0:T(8,128)(2,1)S(1)}, u32[]{:S(2)}, u32[]{:S(2)}) async-start(bf16[8,2,4,128,128]{4,3,2,1,0:T(8,128)(2,1)} %get-tuple-element.60), calls=%async_computation | async-start | bytes 4194304 | tf_op jit(solution)/shard_map/all_to_all | solution.py:657
  37.8 4.7 %copy-start.5 = (bf16[10240,128]{1,0:T(8,128)(2,1)S(1)}, bf16[10240,128]{1,0:T(8,128)(2,1)}, u32[]{:S(2)}) copy-start(bf16[10240,128]{1,0:T(8,128)(2,1)} %get-tuple-element.65) | copy-start | bytes 7864324
  39.3 3.1 %collective-permute-start = (bf16[5120,128]{1,0:T(8,128)(2,1)S(1)}, bf16[5120,128]{1,0:T(8,128)(2,1)S(1)}, u32[]{:S(2)}, u32[]{:S(2)}) collective-permute-start(bf16[5120,128]{1,0:T(8,128)(2,1)S(1)} %slice.83), channel_id=1, source_target_pairs={{0,8},{1,9},{2,10},{3,11},{4,12},{5,13},{6,14},{7,15},{8,0},{9,1},... | collective-permute-start | bytes 3932168 | tf_op jit(solution)/shard_map/ppermute | solution.py:576
  42.8 1.3 copy-start.2
  44.0 30.2 %collective-permute-start.1 = (bf16[2560,128]{1,0:T(8,128)(2,1)}, bf16[2560,128]{1,0:T(8,128)(2,1)}, u32[]{:S(2)}, u32[]{:S(2)}) collective-permute-start(bf16[2560,128]{1,0:T(8,128)(2,1)} %slice.109), channel_id=1, source_target_pairs={{0,16},{1,17},{2,18},{3,19},{4,20},{5,21},{6,22},{7,23},{8,24},{9,... | collective-permute-start | bytes 1966088 | tf_op jit(solution)/shard_map/ppermute | solution.py:576
  65.0 1.3 copy-start
  66.3 7.9 %copy-start.3 = (bf16[5120,128]{1,0:T(8,128)(2,1)S(1)}, bf16[5120,128]{1,0:T(8,128)(2,1)}, u32[]{:S(2)}) copy-start(bf16[5120,128]{1,0:T(8,128)(2,1)} %copy-done.2) | copy-start | bytes 3932164
  74.2 2.9 %copy-start.15 = (bf16[256,128]{1,0:T(8,128)(2,1)S(1)}, bf16[256,128]{1,0:T(8,128)(2,1)}, u32[]{:S(2)}) copy-start(bf16[256,128]{1,0:T(8,128)(2,1)} %get-tuple-element.69) | copy-start | bytes 196612
  75.5 13.9 %collective-permute-start.2 = (bf16[1280,128]{1,0:T(8,128)(2,1)S(1)}, bf16[1280,128]{1,0:T(8,128)(2,1)S(1)}, u32[]{:S(2)}, u32[]{:S(2)}) collective-permute-start(bf16[1280,128]{1,0:T(8,128)(2,1)S(1)} %slice.111), channel_id=1, source_target_pairs={{0,1},{1,0},{2,3},{3,2},{4,5},{5,4},{6,7},{7,6},{8,9},{9,8},{10,11... | collective-permute-start | bytes 983048 | tf_op jit(solution)/shard_map/ppermute | solution.py:576
  77.9 22.2 %all-to-all-start.1 = ((bf16[8,256,128]{2,1,0:T(8,128)(2,1)}), bf16[8,256,128]{2,1,0:T(8,128)(2,1)S(1)}, u32[]{:S(2)}, u32[]{:S(2)}) async-start(bf16[8,256,128]{2,1,0:T(8,128)(2,1)} %broadcast_in_dim.3), calls=%async_computation.1 | async-start | bytes 1048576 | tf_op jit(solution)/shard_map/all_to_all | solution.py:681
  89.5 0.7 copy-start.10
  91.0 17.0 %collective-permute-start.5 = (bf16[320,128]{1,0:T(8,128)(2,1)}, bf16[320,128]{1,0:T(8,128)(2,1)}, u32[]{:S(2)}, u32[]{:S(2)}) collective-permute-start(bf16[320,128]{1,0:T(8,128)(2,1)} %get-tuple-element.107), channel_id=1, source_target_pairs={{0,6},{1,7},{2,4},{3,5},{4,2},{5,3},{6,0},{7,1},{8,14},{9,15},{10,... | collective-permute-start | bytes 245768 | tf_op jit(solution)/shard_map/ppermute | solution.py:576
  94.6 13.4 %collective-permute-start.4 = (bf16[320,128]{1,0:T(8,128)(2,1)}, bf16[320,128]{1,0:T(8,128)(2,1)}, u32[]{:S(2)}, u32[]{:S(2)}) collective-permute-start(bf16[320,128]{1,0:T(8,128)(2,1)} %get-tuple-element.108), channel_id=1, source_target_pairs={{0,2},{1,3},{2,0},{3,1},{4,6},{5,7},{6,4},{7,5},{8,10},{9,11},{10,... | collective-permute-start | bytes 245768 | tf_op jit(solution)/shard_map/ppermute | solution.py:576
  94.6 13.4 %collective-permute-start.3 = (bf16[320,128]{1,0:T(8,128)(2,1)}, bf16[320,128]{1,0:T(8,128)(2,1)}, u32[]{:S(2)}, u32[]{:S(2)}) collective-permute-start(bf16[320,128]{1,0:T(8,128)(2,1)} %get-tuple-element.106), channel_id=1, source_target_pairs={{0,4},{1,5},{2,6},{3,7},{4,0},{5,1},{6,2},{7,3},{8,12},{9,13},{10,... | collective-permute-start | bytes 245768 | tf_op jit(solution)/shard_map/ppermute | solution.py:576
  100.2 4.2 %copy-start.12 = (bf16[8,256,128]{2,1,0:T(8,128)(2,1)}, bf16[8,256,128]{2,1,0:T(8,128)(2,1)S(1)}, u32[]{:S(2)}) copy-start(bf16[8,256,128]{2,1,0:T(8,128)(2,1)S(1)} %all-to-all-done.1) | copy-start | bytes 1572868
  100.2 18.8 %all-to-all-start.2 = ((bf16[8,2,128,128]{3,2,1,0:T(8,128)(2,1)}), bf16[8,2,128,128]{3,2,1,0:T(8,128)(2,1)}, u32[]{:S(2)}, u32[]{:S(2)}) async-start(bf16[8,2,128,128]{3,2,1,0:T(8,128)(2,1)} %get-tuple-element.72), calls=%async_computation.2 | async-start | bytes 1048576 | tf_op jit(solution)/shard_map/all_to_all | solution.py:661
  107.9 1.2 collective-permute-start.6
  110.0 3.9 %collective-permute-start.7 = (bf16[96,128]{1,0:T(8,128)(2,1)S(1)}, bf16[96,128]{1,0:T(8,128)(2,1)S(1)}, u32[]{:S(2)}, u32[]{:S(2)}) collective-permute-start(bf16[96,128]{1,0:T(8,128)(2,1)S(1)} %slice.119), channel_id=1, source_target_pairs={{0,16},{1,17},{2,18},{3,19},{4,20},{5,21},{6,22},{7,23},{8,24},{9,... | collective-permute-start | bytes 73736 | tf_op jit(solution)/shard_map/ppermute | solution.py:576
  114.6 15.0 %collective-permute-start.8 = (bf16[416,128]{1,0:T(8,128)(2,1)}, bf16[416,128]{1,0:T(8,128)(2,1)}, u32[]{:S(2)}, u32[]{:S(2)}) collective-permute-start(bf16[416,128]{1,0:T(8,128)(2,1)} %pad_maximum_fusion.4.refs_0_), channel_id=1, source_target_pairs={{0,4},{1,5},{2,6},{3,7},{4,0},{5,1},{6,2},{7,3},{8,12},{9,13},{10,... | collective-permute-start | bytes 319496 | tf_op jit(solution)/shard_map/ppermute | solution.py:576
  117.4 12.2 %collective-permute-start.9 = (bf16[416,128]{1,0:T(8,128)(2,1)}, bf16[416,128]{1,0:T(8,128)(2,1)}, u32[]{:S(2)}, u32[]{:S(2)}) collective-permute-start(bf16[416,128]{1,0:T(8,128)(2,1)} %pad_maximum_fusion.4.refs_0_), channel_id=1, source_target_pairs={{0,2},{1,3},{2,0},{3,1},{4,6},{5,7},{6,4},{7,5},{8,10},{9,11},{10,... | collective-permute-start | bytes 319496 | tf_op jit(solution)/shard_map/ppermute | solution.py:576
  118.8 10.7 %collective-permute-start.10 = (bf16[416,128]{1,0:T(8,128)(2,1)}, bf16[416,128]{1,0:T(8,128)(2,1)}, u32[]{:S(2)}, u32[]{:S(2)}) collective-permute-start(bf16[416,128]{1,0:T(8,128)(2,1)} %pad_maximum_fusion.4.refs_0_), channel_id=1, source_target_pairs={{0,6},{1,7},{2,4},{3,5},{4,2},{5,3},{6,0},{7,1},{8,14},{9,15},{10,... | collective-permute-start | bytes 319496 | tf_op jit(solution)/shard_map/ppermute | solution.py:576
  119.0 42.0 %all-to-all-start.3 = ((bf16[8,2,3,128,128]{4,3,2,1,0:T(8,128)(2,1)}), bf16[8,2,3,128,128]{4,3,2,1,0:T(8,128)(2,1)}, u32[]{:S(2)}, u32[]{:S(2)}) async-start(bf16[8,2,3,128,128]{4,3,2,1,0:T(8,128)(2,1)} %get-tuple-element.79.rest_ref), calls=%async_computation.3 | async-start | bytes 3145728 | tf_op jit(solution)/shard_map/all_to_all | solution.py:661
  131.4 20.6 %collective-permute-start.11 = (bf16[1664,128]{1,0:T(8,128)(2,1)}, bf16[1664,128]{1,0:T(8,128)(2,1)S(1)}, u32[]{:S(2)}, u32[]{:S(2)}) collective-permute-start(bf16[1664,128]{1,0:T(8,128)(2,1)} %join.1), channel_id=1, source_target_pairs={{0,1},{1,0},{2,3},{3,2},{4,5},{5,4},{6,7},{7,6},{8,9},{9,8},{10,11... | collective-permute-start | bytes 1277960 | tf_op jit(solution)/shard_map/ppermute | solution.py:576
  135.1 41.0 %collective-permute-start.16 = (bf16[1024,128]{1,0:T(8,128)(2,1)}, bf16[1024,128]{1,0:T(8,128)(2,1)}, u32[]{:S(2)}, u32[]{:S(2)}) collective-permute-start(bf16[1024,128]{1,0:T(8,128)(2,1)} %slice.103), channel_id=1, source_target_pairs={{0,8},{1,9},{2,10},{3,11},{4,12},{5,13},{6,14},{7,15},{8,0},{9,1},... | collective-permute-start | bytes 786440 | tf_op jit(solution)/shard_map/ppermute | solution.py:576
  152.0 0.8 copy-start.7
  154.7 19.3 %collective-permute-start.12 = (bf16[3328,128]{1,0:T(8,128)(2,1)}, bf16[3328,128]{1,0:T(8,128)(2,1)}, u32[]{:S(2)}, u32[]{:S(2)}) collective-permute-start(bf16[3328,128]{1,0:T(8,128)(2,1)} %pad_maximum_fusion.1), channel_id=1, source_target_pairs={{0,16},{1,17},{2,18},{3,19},{4,20},{5,21},{6,22},{7,23},{8,24},{9,... | collective-permute-start | bytes 2555912 | tf_op jit(solution)/shard_map/ppermute | solution.py:576
  160.9 13.1 %copy-start.4 = (bf16[1664,128]{1,0:T(8,128)(2,1)S(1)}, bf16[1664,128]{1,0:T(8,128)(2,1)}, u32[]{:S(2)}) copy-start(bf16[1664,128]{1,0:T(8,128)(2,1)} %join.1) | copy-start | bytes 1277956
  160.9 13.1 %copy-start.8 = (bf16[1664,128]{1,0:T(8,128)(2,1)S(1)}, bf16[1664,128]{1,0:T(8,128)(2,1)}, u32[]{:S(2)}) copy-start(bf16[1664,128]{1,0:T(8,128)(2,1)} %copy-done.7) | copy-start | bytes 1277956
  174.0 1.4 copy-start.14
  174.1 2.0 copy-start.11
  175.4 20.6 %copy-start.1 = (bf16[6656,128]{1,0:T(8,128)(2,1)}, bf16[6656,128]{1,0:T(8,128)(2,1)S(1)}, u32[]{:S(2)}) copy-start(bf16[6656,128]{1,0:T(8,128)(2,1)S(1)} %pad_maximum_fusion.refs_0_) | copy-start | bytes 5111812
  175.4 20.6 %collective-permute-start.20 = (bf16[6656,128]{1,0:T(8,128)(2,1)S(1)}, bf16[6656,128]{1,0:T(8,128)(2,1)S(1)}, u32[]{:S(2)}, u32[]{:S(2)}) collective-permute-start(bf16[6656,128]{1,0:T(8,128)(2,1)S(1)} %pad_maximum_fusion.refs_0_), channel_id=1, source_target_pairs={{0,8},{1,9},{2,10},{3,11},{4,12},{5,13},{6,14},{7,15},{8,0},{9,1},... | collective-permute-start | bytes 5111816 | tf_op jit(solution)/shard_map/ppermute | solution.py:576
  175.5 3.8 %collective-permute-start.13 = (bf16[576,128]{1,0:T(8,128)(2,1)S(1)}, bf16[576,128]{1,0:T(8,128)(2,1)S(1)}, u32[]{:S(2)}, u32[]{:S(2)}) collective-permute-start(bf16[576,128]{1,0:T(8,128)(2,1)S(1)} %slice.97), channel_id=1, source_target_pairs={{0,8},{1,9},{2,10},{3,11},{4,12},{5,13},{6,14},{7,15},{8,0},{9,1},... | collective-permute-start | bytes 442376 | tf_op jit(solution)/shard_map/ppermute | solution.py:576
  177.1 5.9 %collective-permute-start.17 = (bf16[512,128]{1,0:T(8,128)(2,1)S(1)}, bf16[512,128]{1,0:T(8,128)(2,1)S(1)}, u32[]{:S(2)}, u32[]{:S(2)}) collective-permute-start(bf16[512,128]{1,0:T(8,128)(2,1)S(1)} %slice.125), channel_id=1, source_target_pairs={{0,16},{1,17},{2,18},{3,19},{4,20},{5,21},{6,22},{7,23},{8,24},{9,... | collective-permute-start | bytes 393224 | tf_op jit(solution)/shard_map/ppermute | solution.py:576
  179.3 8.1 %collective-permute-start.14 = (bf16[288,128]{1,0:T(8,128)(2,1)S(1)}, bf16[288,128]{1,0:T(8,128)(2,1)S(1)}, u32[]{:S(2)}, u32[]{:S(2)}) collective-permute-start(bf16[288,128]{1,0:T(8,128)(2,1)S(1)} %slice.121), channel_id=1, source_target_pairs={{0,16},{1,17},{2,18},{3,19},{4,20},{5,21},{6,22},{7,23},{8,24},{9,... | collective-permute-start | bytes 221192 | tf_op jit(solution)/shard_map/ppermute | solution.py:576
  183.1 4.3 %collective-permute-start.18 = (bf16[256,128]{1,0:T(8,128)(2,1)S(1)}, bf16[256,128]{1,0:T(8,128)(2,1)S(1)}, u32[]{:S(2)}, u32[]{:S(2)}) collective-permute-start(bf16[256,128]{1,0:T(8,128)(2,1)S(1)} %slice.127), channel_id=1, source_target_pairs={{0,1},{1,0},{2,3},{3,2},{4,5},{5,4},{6,7},{7,6},{8,9},{9,8},{10,11... | collective-permute-start | bytes 196616 | tf_op jit(solution)/shard_map/ppermute | solution.py:576
  187.5 4.0 %collective-permute-start.15 = (bf16[144,128]{1,0:T(8,128)(2,1)S(1)}, bf16[144,128]{1,0:T(8,128)(2,1)S(1)}, u32[]{:S(2)}, u32[]{:S(2)}) collective-permute-start(bf16[144,128]{1,0:T(8,128)(2,1)S(1)} %slice.123), channel_id=1, source_target_pairs={{0,1},{1,0},{2,3},{3,2},{4,5},{5,4},{6,7},{7,6},{8,9},{9,8},{10,11... | collective-permute-start | bytes 110600 | tf_op jit(solution)/shard_map/ppermute | solution.py:576
  191.5 11.2 %collective-permute-start.22 = (bf16[400,128]{1,0:T(8,128)(2,1)S(1)}, bf16[400,128]{1,0:T(8,128)(2,1)S(1)}, u32[]{:S(2)}, u32[]{:S(2)}) collective-permute-start(bf16[400,128]{1,0:T(8,128)(2,1)S(1)} %pad_maximum_fusion.5), channel_id=1, source_target_pairs={{0,6},{1,7},{2,4},{3,5},{4,2},{5,3},{6,0},{7,1},{8,14},{9,15},{10,... | collective-permute-start | bytes 307208 | tf_op jit(solution)/shard_map/ppermute | solution.py:576
  195.2 7.5 %collective-permute-start.21 = (bf16[400,128]{1,0:T(8,128)(2,1)S(1)}, bf16[400,128]{1,0:T(8,128)(2,1)S(1)}, u32[]{:S(2)}, u32[]{:S(2)}) collective-permute-start(bf16[400,128]{1,0:T(8,128)(2,1)S(1)} %pad_maximum_fusion.5), channel_id=1, source_target_pairs={{0,2},{1,3},{2,0},{3,1},{4,6},{5,7},{6,4},{7,5},{8,10},{9,11},{10,... | collective-permute-start | bytes 307208 | tf_op jit(solution)/shard_map/ppermute | solution.py:576
  195.2 7.5 %collective-permute-start.19 = (bf16[400,128]{1,0:T(8,128)(2,1)S(1)}, bf16[400,128]{1,0:T(8,128)(2,1)S(1)}, u32[]{:S(2)}, u32[]{:S(2)}) collective-permute-start(bf16[400,128]{1,0:T(8,128)(2,1)S(1)} %pad_maximum_fusion.5), channel_id=1, source_target_pairs={{0,4},{1,5},{2,6},{3,7},{4,0},{5,1},{6,2},{7,3},{8,12},{9,13},{10,... | collective-permute-start | bytes 307208 | tf_op jit(solution)/shard_map/ppermute | solution.py:576
  196.0 1.2 copy-start.6
  202.8 4.7 %collective-permute-start.23 = (bf16[400,128]{1,0:T(8,128)(2,1)S(1)}, bf16[400,128]{1,0:T(8,128)(2,1)S(1)}, u32[]{:S(2)}, u32[]{:S(2)}) collective-permute-start(bf16[400,128]{1,0:T(8,128)(2,1)S(1)} %add_convert_fusion.6), channel_id=1, source_target_pairs={{0,1},{1,0},{2,3},{3,2},{4,5},{5,4},{6,7},{7,6},{8,9},{9,8},{10,11... | collective-permute-start | bytes 307208 | tf_op jit(solution)/shard_map/ppermute | solution.py:576
  207.5 5.8 %collective-permute-start.24 = (bf16[800,128]{1,0:T(8,128)(2,1)S(1)}, bf16[800,128]{1,0:T(8,128)(2,1)S(1)}, u32[]{:S(2)}, u32[]{:S(2)}) collective-permute-start(bf16[800,128]{1,0:T(8,128)(2,1)S(1)} %pad_maximum_fusion.3), channel_id=1, source_target_pairs={{0,16},{1,17},{2,18},{3,19},{4,20},{5,21},{6,22},{7,23},{8,24},{9,... | collective-permute-start | bytes 614408 | tf_op jit(solution)/shard_map/ppermute | solution.py:576
  213.4 1.8 copy-start.9
  213.4 1.8 collective-permute-start.25
  215.2 0.8 copy-start.13

commit v3 on v2

--- a/solution.py
+++ b/solution.py
@@ -22,7 +22,7 @@
 BF = jnp.bfloat16
 F32 = jnp.float32
 MIB = 1024 * 1024
-WIDE = 60 * MIB
+WIDE = 63 * MIB
 LITTLE = pl.CostEstimate(flops=1, bytes_accessed=1, transcendentals=0)
 MUCH = pl.CostEstimate(flops=2 * 10**11, bytes_accessed=1, transcendentals=0)
 
@@ -226,12 +226,22 @@
     return total.astype(BF)
 
 
+def fetch(pairs, sems):
+    copies = [pltpu.make_async_copy(away, here, sems.at[k]) for k, (away, here) in enumerate(pairs)]
+    for copy in copies:
+        copy.start()
+    return copies
+
+
+def third(ref, part):
+    return ref.at[:, pl.ds(part * D, D)]
+
+
 def project_kernel(
     x_ref, g_ref, wj_ref, wp_ref, lj_ref, rj_ref, lp_ref, rp_ref, gain_ref, shift_ref, doc_ref,
-    msg_ref, low_ref, rank_ref, wj_here, wp_here, sems,
+    msg_ref, lows_ref, rank_ref, wj_here, wp_here, sems,
 ):
     rows, slots = msg_ref.shape[1], msg_ref.shape[3]
-    third = lambda ref, part: ref.at[:, pl.ds(part * D, D)]
     copies = [pltpu.make_async_copy(wp_ref, wp_here, sems.at[3])] + [
         pltpu.make_async_copy(third(wj_ref, part), third(wj_here, part), sems.at[part]) for part in range(3)
     ]
@@ -250,7 +260,7 @@
     hat, _ = normalised(x_ref[...].astype(F32))
     u = (hat * gain_ref[...] + shift_ref[...]).astype(BF)
     low = nn(u, lj_ref[...]).astype(BF)
-    low_ref[...] = low
+    lows_ref[...] = jnp.broadcast_to(low, lows_ref.shape)
     places = lax.axis_index("seq") * slots + lax.broadcasted_iota(jnp.int32, (1, slots), 1)
     turns = [turning(places - document_starts(doc_ref, row, places)) for row in range(rows)]
     cosine = jnp.concatenate([pair[0] for pair in turns], axis=0)
@@ -269,7 +279,7 @@
 
 
 def project(x, g, joined_weight, proj_weight, joined_left, joined_right, proj_left, proj_right,
-            gain, shift, doc_lengths, rows):
+            gain, shift, doc_lengths, rows, devices):
     tokens = x.shape[0]
     held = pl.BlockSpec(memory_space=pltpu.VMEM)
     away = pl.BlockSpec(memory_space=pl.ANY)
@@ -278,7 +288,7 @@
         in_specs=[held, held, away, away] + [held] * 6 + [pl.BlockSpec(memory_space=pltpu.SMEM)],
         out_shape=[
             jax.ShapeDtypeStruct((PAIRS, rows, 4, tokens // rows, PAIR), BF),
-            jax.ShapeDtypeStruct((tokens, RANK), BF),
+            jax.ShapeDtypeStruct((devices, tokens, RANK), BF),
             jax.ShapeDtypeStruct((tokens, RANK), BF),
         ],
         scratch_shapes=[
@@ -503,24 +513,33 @@
 
 
 def finish_kernel(
-    packing, msg_ref, x_ref, g_ref, gfeed_ref, wj_ref, lj_ref, rj_ref,
-    mgain_ref, mshift_ref, fgain_ref, igrad_ref, pack_ref, wj_here, sems,
+    packing, x_away, msg_away, rj_away, wj_away, lj_away, gfeed_away, g_away,
+    mgain_ref, mshift_ref, fgain_ref, igrad_ref, pack_ref,
+    x_ref, msg_ref, rj_ref, wj_ref, lj_ref, gfeed_ref, g_ref, sems,
 ):
-    third = lambda ref, part: ref.at[:, pl.ds(part * D, D)]
-    copies = [pltpu.make_async_copy(third(wj_ref, part), third(wj_here, part), sems.at[part]) for part in range(3)]
-    for copy in copies:
-        copy.start()
-    x, g = x_ref[...].astype(F32), g_ref[...]
-    hat, scale = normalised(x)
+    x_in, msg_in, rj_in, w0_in, w1_in, w2_in, lj_in, gfeed_in, g_in = fetch([
+        (x_away, x_ref), (msg_away, msg_ref), (rj_away, rj_ref),
+    ] + [(third(wj_away, part), third(wj_ref, part)) for part in range(3)] + [
+        (lj_away, lj_ref), (gfeed_away, gfeed_ref), (g_away, g_ref),
+    ], sems)
+    x_in.wait()
+    hat, scale = normalised(x_ref[...].astype(F32))
+    u = (hat * mgain_ref[...] + mshift_ref[...]).astype(BF)
+    msg_in.wait()
+    rj_in.wait()
     joined = gathered(msg_ref)
     rank = (SCALING * nt(joined, rj_ref[...])).astype(BF)
-    u = (hat * mgain_ref[...] + mshift_ref[...]).astype(BF)
     packing.put_rows(pack_ref, LATE_UNITS["joined_left"], tn(u, rank))
-    grad_mixer = nt(rank, lj_ref[...])
-    for part in range(3):
+    grad_mixer = jnp.zeros(hat.shape, F32)
+    for part, wait in enumerate((w0_in, w1_in, w2_in)):
         columns = slice(part * D, (part + 1) * D)
-        copies[part].wait()
-        grad_mixer = grad_mixer + nt(joined[:, columns], wj_here[:, columns])
+        wait.wait()
+        grad_mixer = grad_mixer + nt(joined[:, columns], wj_ref[:, columns])
+    lj_in.wait()
+    grad_mixer = grad_mixer + nt(rank, lj_ref[...])
+    gfeed_in.wait()
+    g_in.wait()
+    g = g_ref[...]
     grad_feed = gfeed_ref[...]
     mixer_hat, feed_hat = grad_mixer * hat, grad_feed * hat
     sums = [jnp.sum(v, axis=0, keepdims=True) for v in (mixer_hat, grad_mixer, feed_hat, grad_feed)]
@@ -537,16 +556,16 @@
            mixer_gain, mixer_shift, feed_gain, packing):
     tokens = x.shape[0]
     held = pl.BlockSpec(memory_space=pltpu.VMEM)
+    loads = (x, message, joined_right, joined_weight, joined_left, grad_feed, g)
     return pl.pallas_call(
         partial(finish_kernel, packing),
-        in_specs=[held] * 4 + [pl.BlockSpec(memory_space=pl.ANY)] + [held] * 5,
+        in_specs=[pl.BlockSpec(memory_space=pl.ANY)] * len(loads) + [held] * 3,
         out_shape=[jax.ShapeDtypeStruct((tokens, D), BF), jax.ShapeDtypeStruct((LATE_ROWS, RANK), BF)],
-        scratch_shapes=[pltpu.VMEM((D, 3 * D), BF), pltpu.SemaphoreType.DMA((3,))],
+        scratch_shapes=[pltpu.VMEM(load.shape, load.dtype) for load in loads] + [pltpu.SemaphoreType.DMA((9,))],
         compiler_params=pltpu.CompilerParams(vmem_limit_bytes=WIDE),
         cost_estimate=MUCH,
         name="finish",
-    )(message, x, g, grad_feed, joined_weight, joined_left, joined_right,
-      mixer_gain, mixer_shift, feed_gain)
+    )(*loads, mixer_gain, mixer_shift, feed_gain)
 
 
 def right_kernel(packing, head_parts, rest_ref, low_ref, pack_ref):
@@ -577,34 +596,39 @@
 
 
 def unpack_kernel(units, count, *refs):
-    part_refs, out_refs, (pack_ref, sems) = refs[:count], refs[count:-2], refs[-2:]
-    copies, row = [], 0
-    for place, part_ref in enumerate(part_refs):
-        rows = part_ref.shape[0]
-        copies.append(pltpu.make_async_copy(part_ref, pack_ref.at[pl.ds(row, rows)], sems.at[place]))
-        row += rows
-    for copy in copies:
-        copy.start()
-    for copy in copies:
+    part_refs, out_refs, refs = refs[:count], refs[count : count + len(units)], refs[count + len(units) :]
+    value_refs, (pack_ref, sems, out_sems) = refs[:-3], refs[-3:]
+    rows = part_refs[0].shape[0]
+    for copy in fetch([(ref, pack_ref.at[pl.ds(k * rows, rows)]) for k, ref in enumerate(part_refs)], sems):
         copy.wait()
-    for (packing, unit, shape, kind), out_ref in zip(units, out_refs):
+    outs = []
+    for (packing, unit, shape, kind), out_ref, value_ref in zip(units, out_refs, value_refs):
         if kind == "columns":
             for step in range(shape[1] // RANK):
-                out_ref[:, step * RANK : (step + 1) * RANK] = packing.get(pack_ref, unit + step).astype(F32)
+                value_ref[:, step * RANK : (step + 1) * RANK] = packing.get(pack_ref, unit + step).astype(F32)
         elif kind == "rows":
             for step in range(shape[0] // RANK):
-                out_ref[step * RANK : (step + 1) * RANK] = packing.get(pack_ref, unit + step).astype(F32)
+                value_ref[step * RANK : (step + 1) * RANK] = packing.get(pack_ref, unit + step).astype(F32)
         else:
-            out_ref[...] = packing.get(pack_ref, unit)[kind * 8 : (kind + 1) * 8].astype(F32)
+            value_ref[...] = packing.get(pack_ref, unit)[kind * 8 : (kind + 1) * 8].astype(F32)
+        outs.append(pltpu.make_async_copy(value_ref, out_ref, out_sems.at[len(outs)]))
+        outs[-1].start()
+    for out in outs:
+        out.wait()
 
 
 def unpack(parts, units):
     rows = sum(part.shape[0] for part in parts)
+    away = pl.BlockSpec(memory_space=pl.ANY)
     return pl.pallas_call(
         partial(unpack_kernel, units, len(parts)),
-        in_specs=[pl.BlockSpec(memory_space=pl.ANY)] * len(parts),
+        in_specs=[away] * len(parts),
+        out_specs=[away] * len(units),
         out_shape=[jax.ShapeDtypeStruct(shape, F32) for _, _, shape, _ in units],
-        scratch_shapes=[pltpu.VMEM((rows, RANK), BF), pltpu.SemaphoreType.DMA((len(parts),))],
+        scratch_shapes=[pltpu.VMEM(shape, F32) for _, _, shape, _ in units] + [
+            pltpu.VMEM((rows, RANK), BF),
+            pltpu.SemaphoreType.DMA((len(parts),)), pltpu.SemaphoreType.DMA((len(units),)),
+        ],
         compiler_params=pltpu.CompilerParams(vmem_limit_bytes=WIDE),
         cost_estimate=LITTLE,
         name="unpack",
@@ -637,16 +661,18 @@
         return [first + step for step in range(count.bit_length() - 1)]
 
     seq_bits = bits(0, devices)
-    order = bits(len(seq_bits), batches) + seq_bits
+    batch_bits = bits(len(seq_bits), batches)
+    order = batch_bits[:1] + seq_bits[:1] + batch_bits[1:] + seq_bits[1:]
+    late_order = [order[0], order[2], order[1]]
     shared = row_parts * head_parts
-    own = order[: batches.bit_length() - 1] + bits(0, shared)
+    own = batch_bits + bits(0, shared)
     feed_packing = Packing(FEED_ROWS, order)
     right_packing = PairPacking(order, own, seq_bits[shared.bit_length() - 1 :])
-    proj_packing, late_packing = Packing(PROJ_ROWS, order[:3]), Packing(LATE_ROWS, order[:3])
-
-    message, low_joined, rank_proj = project(
+    proj_packing, late_packing = Packing(PROJ_ROWS, late_order), Packing(LATE_ROWS, late_order)
+
+    message, lows, rank_proj = project(
         x, g, joined_weight, proj_weight, joined_left, joined_right, proj_left, proj_right,
-        mixer_gain, mixer_shift, doc_lengths, rows,
+        mixer_gain, mixer_shift, doc_lengths, rows, devices,
     )
 
     def send(units):
@@ -677,8 +703,7 @@
 
     part, steps = feed_pack, list(order)
     part = halve(part, steps.pop(0), size)
-    low_all = after(jnp.broadcast_to(low_joined, (devices, tokens, RANK)), part)
-    low_all = lax.all_to_all(after(low_all, arrived), "seq", 0, 0, tiled=True)
+    low_all = lax.all_to_all(after(lows, arrived), "seq", 0, 0, tiled=True)
     answer = attend(arrived, doc_lengths, 0, (), row_parts, head_parts)
     part = halve(part, steps.pop(0), size, *answer)
     for row in range(1, my_rows):
@@ -705,13 +730,13 @@
     )
     early = join(everyone(early, steps, size, output))
     early = double(early, order[-3], size)
-    for bit in order[:2]:
+    for bit in late_order[:2]:
         proj_part = halve(proj_part, bit, size)
     input_grad, late_part = finish(
         returned, after(x, early), g, grad_feed, joined_weight, joined_left, joined_right,
         mixer_gain, mixer_shift, feed_gain, late_packing,
     )
-    proj_part = halve(proj_part, order[2], size, late_part)
+    proj_part = halve(proj_part, late_order[2], size, late_part)
     for bit in order[-4:0:-1]:
         early = double(early, bit, size, late_part)
     late_part = after(late_part, early)
@@ -725,7 +750,7 @@
         (right_packing, 0, (RANK, 3 * D), "columns"),
     ))
 
-    for bit in order[:3]:
+    for bit in late_order:
         late_part = halve(late_part, bit, size)
     stride, first = proj_part.shape[0] + late_part.shape[0], late_part.shape[0]
     late = jnp.concatenate([late_part, proj_part])
@@ -733,7 +758,7 @@
         late = add_low(late, swap(late, 1 << bit, size))
     whole_late = everyone(late, order[-2:], size, *early_grads)
     late = add_all(whole_late[0], whole_late[1:])
-    for bit in order[2:0:-1]:
+    for bit in late_order[:0:-1]:
         late = double(late, bit, size)
     late = [late, swap(late, 1 << order[0], size)]
     late_packing, proj_packing = late_packing.held(stride, 0), proj_packing.held(stride, first)

time: 220 us -> 213 us (0.968)
  waiting for transfers between devices: 76.9 us -> 71.6 us
    ppermute x26, waiting for transfers between devices: 47.8 us -> 37.6 us  [swap(): lax.ppermute(part, ('batch', 'seq'), [(i, i ^ bit) for i in range(size)])]
    all_to_all x2, waiting for transfers between devices: 4.73 us -> 14.9 us  [send_back(): units = lax.all_to_all(units[..., :lanes], 'seq', 0, 0, tiled=True)]
    all_to_all x1, waiting for transfers between devices: 4.84 us -> 0.68 us  [per_device(): low_all = lax.all_to_all(after(lows, arrived), 'seq', 0, 0, tiled=True)]
    unnamed x32 -> x22, local copies, waits for them, and re-layouts: 5.12 us -> 4.53 us
  transfers between devices with their start and end apart: 30 -> 30, of which waited for: 15 -> 15; matrix products, arithmetic and copies ran while one was open for 6% -> 7% of each run, Pallas kernels for 28% -> 28%
where the time goes in v3:
time: 213 us; the launch traced here: 212 us
  waiting for transfers between devices  71.6 us (34%)
  Pallas kernels  70.5 us (33%)
  starting transfers between devices  48.5 us (23%)
  local copies, waits for them, and re-layouts  10.2 us (5%)
  other arithmetic  9.96 us (5%)
    ppermute x26, waiting for transfers between devices, swap(): lax.ppermute(part, ('batch', 'seq'), [(i, i ^ bit) for i in range(size)])  37.6 us
    ppermute x26, starting transfers between devices, swap(): lax.ppermute(part, ('batch', 'seq'), [(i, i ^ bit) for i in range(size)])  25.8 us
    pallas_call x1, Pallas kernels, feed(): pl.pallas_call(partial(feed_kernel, packing), grid=(FF // width,), in_spe...  21 us
    all_to_all x1, waiting for transfers between devices, send(): return lax.all_to_all(units, 'seq', 0, 0, tiled=True)  18.4 us
    pallas_call x2, Pallas kernels, attend(): pl.pallas_call(partial(attend_kernel, row, rows, row_parts, head_parts),...  15.6 us
    all_to_all x2, waiting for transfers between devices, send_back(): units = lax.all_to_all(units[..., :lanes], 'seq', 0, 0, tiled=True)  14.9 us
    all_to_all x2, starting transfers between devices, send_back(): units = lax.all_to_all(units[..., :lanes], 'seq', 0, 0, tiled=True)  11 us
    pallas_call x1, Pallas kernels, project(): pl.pallas_call(project_kernel, in_specs=[held, held, away, away] + [held]...  8.82 us
  transfers between devices with their start and end apart: 30, of which 15 were waited for; matrix products, arithmetic and copies ran while one was open for 7% of the time, Pallas kernels for 28%

profile of v3, /device:TPU:0, one launch (start us, length us, event | category | flops | bytes accessed | tf_op | source)
XLA Modules:
  0.0 211.9 jit_solution(72167255266513621)
XLA Ops:
  0.6 8.8 %project.1 = (bf16[8,2,4,128,128]{4,3,2,1,0:T(8,128)(2,1)}, bf16[8,256,128]{2,1,0:T(8,128)(2,1)}, bf16[256,128]{1,0:T(8,128)(2,1)}) custom-call(bf16[256,1024]{1,0:T(8,128)(2,1)} %bitcast.13, bf16[256,1024]{1,0:T(8,128)(2,1)} %bitcast.17, bf16[1024,3072]{1,0:T(8,128)(2,1)} %wj_away.1, bf16[1024,1024]{1,0:T(8,128)(2,1)} %wp_ref.3, bf16[1024,128]{1,0:T(8,128)(2,1)} %lj_away.1, ...), custom_call_target="tpu_custom_call" | custom-call | flops 1 | bytes 1 | tf_op jit(solution)/shard_map/project/pallas_call | solution.py:286
  9.5 7.3 %all-to-all-start = ((bf16[8,2,4,128,128]{4,3,2,1,0:T(8,128)(2,1)}), bf16[8,2,4,128,128]{4,3,2,1,0:T(8,128)(2,1)}, u32[]{:S(2)}, u32[]{:S(2)}) async-start(bf16[8,2,4,128,128]{4,3,2,1,0:T(8,128)(2,1)} %get-tuple-element.59), calls=%async_computation | async-start | bytes 4194304 | tf_op jit(solution)/shard_map/all_to_all | solution.py:683
  16.8 21.0 %feed.1 = (f32[256,1024]{1,0:T(8,128)}, f32[256,1024]{1,0:T(8,128)}, bf16[10240,128]{1,0:T(8,128)(2,1)}) custom-call(bf16[256,1024]{1,0:T(8,128)(2,1)} %bitcast.14, bf16[256,1024]{1,0:T(8,128)(2,1)} %bitcast.18, bf16[1024,4096]{1,0:T(8,128)(2,1)} %we_ref.1, bf16[4096,1024]{1,0:T(8,128)(2,1)} %ws_ref.1, bf16[1024,128]{1,0:T(8,128)(2,1)} %le_ref.1, ...), custom_call_target="tpu_custom_call" | custom-call | flops 1 | bytes 1 | tf_op jit(solution)/shard_map/feed/pallas_call | solution.py:350
  37.8 1.6 slice.83
  39.4 3.0 %collective-permute-done = bf16[5120,128]{1,0:T(8,128)(2,1)S(1)} collective-permute-done((bf16[5120,128]{1,0:T(8,128)(2,1)S(1)}, bf16[5120,128]{1,0:T(8,128)(2,1)S(1)}, u32[]{:S(2)}, u32[]{:S(2)}) %collective-permute-start) | collective-permute-done | bytes 1310752 | tf_op jit(solution)/shard_map/ppermute | solution.py:595
  42.8 1.0 copy-done.1
  43.8 0.9 slice.109
  44.7 2.0 collective-permute-start.1
  46.7 18.4 %all-to-all-done.msg_ref = bf16[8,2,4,128,128]{4,3,2,1,0:T(8,128)(2,1)} async-done(((bf16[8,2,4,128,128]{4,3,2,1,0:T(8,128)(2,1)}), bf16[8,2,4,128,128]{4,3,2,1,0:T(8,128)(2,1)}, u32[]{:S(2)}, u32[]{:S(2)}) %all-to-all-start) | async-done | bytes 2097184 | tf_op jit(solution)/shard_map/all_to_all | solution.py:683
  65.2 7.8 %attend.2 = (bf16[8,2,128,128]{3,2,1,0:T(8,128)(2,1)}, bf16[8,2,3,128,128]{4,3,2,1,0:T(8,128)(2,1)}) custom-call(bf16[8,2,4,128,128]{4,3,2,1,0:T(8,128)(2,1)} %all-to-all-done.msg_ref, s32[2,8]{1,0:T(2,128)} %doc_ref.5), custom_call_target="tpu_custom_call" | custom-call | flops 199999995904 | bytes 1 | tf_op jit(solution)/shard_map/attend/pallas_call | solution.py:458
  72.9 1.5 add_convert_fusion.1
  74.4 1.6 collective-permute-start.2
  76.0 4.4 %all-to-all-start.1 = ((bf16[8,256,128]{2,1,0:T(8,128)(2,1)}), bf16[8,256,128]{2,1,0:T(8,128)(2,1)}, u32[]{:S(2)}, u32[]{:S(2)}) async-start(bf16[8,256,128]{2,1,0:T(8,128)(2,1)} %get-tuple-element.69), calls=%async_computation.1 | async-start | bytes 1048576 | tf_op jit(solution)/shard_map/all_to_all | solution.py:706
  80.4 7.8 %attend.3 = (bf16[8,2,128,128]{3,2,1,0:T(8,128)(2,1)}, bf16[8,2,3,128,128]{4,3,2,1,0:T(8,128)(2,1)}) custom-call(bf16[8,2,4,128,128]{4,3,2,1,0:T(8,128)(2,1)} %all-to-all-done.msg_ref, s32[2,8]{1,0:T(2,128)} %doc_ref.5, bf16[8,2,128,128]{3,2,1,0:T(8,128)(2,1)} %get-tuple-element.60.refs_0_, ...), custom_call_target="tpu_custom_call", output_to_operand_aliasing={{0}: (2, {}), {1}: (3, {})} | custom-call | flops 1 | bytes 1 | tf_op jit(solution)/shard_map/attend/pallas_call | solution.py:458
  88.1 1.1 add_convert_fusion.2
  89.2 0.7 copy-done.7
  89.9 0.7 fusion
  90.6 3.5 %collective-permute-start.5 = (bf16[320,128]{1,0:T(8,128)(2,1)}, bf16[320,128]{1,0:T(8,128)(2,1)}, u32[]{:S(2)}, u32[]{:S(2)}) collective-permute-start(bf16[320,128]{1,0:T(8,128)(2,1)} %get-tuple-element.105), channel_id=1, source_target_pairs={{0,6},{1,7},{2,4},{3,5},{4,2},{5,3},{6,0},{7,1},{8,14},{9,15},{10,... | collective-permute-start | bytes 245768 | tf_op jit(solution)/shard_map/ppermute | solution.py:595
  94.1 0.9 collective-permute-start.3
  95.0 0.7 all-to-all-done.1
  95.7 5.0 %all-to-all-start.2 = ((bf16[8,2,128,128]{3,2,1,0:T(8,128)(2,1)}), bf16[8,2,128,128]{3,2,1,0:T(8,128)(2,1)}, u32[]{:S(2)}, u32[]{:S(2)}) async-start(bf16[8,2,128,128]{3,2,1,0:T(8,128)(2,1)} %get-tuple-element.70), calls=%async_computation.2 | async-start | bytes 1048576 | tf_op jit(solution)/shard_map/all_to_all | solution.py:687
  100.7 2.8 %right.1 = bf16[384,128]{1,0:T(8,128)(2,1)} custom-call(bf16[8,2,3,128,128]{4,3,2,1,0:T(8,128)(2,1)} %get-tuple-element.81.rest_ref, bf16[8,2,128,128]{3,2,1,0:T(8,128)(2,1)} %bitcast.7.low_ref), custom_call_target="tpu_custom_call" | custom-call | flops 199999995904 | bytes 1 | tf_op jit(solution)/shard_map/right/pallas_call | solution.py:585
  103.5 0.8 slice.117
  104.3 1.2 collective-permute-done.6
  105.5 0.8 add_convert_fusion.10
  106.3 0.6 collective-permute-start.7
  106.9 1.1 add_convert_fusion.7
  108.0 2.2 %collective-permute-done.7 = bf16[96,128]{1,0:T(8,128)(2,1)S(1)} collective-permute-done((bf16[96,128]{1,0:T(8,128)(2,1)S(1)}, bf16[96,128]{1,0:T(8,128)(2,1)S(1)}, u32[]{:S(2)}, u32[]{:S(2)}) %collective-permute-start.7) | collective-permute-done | bytes 24608 | tf_op jit(solution)/shard_map/ppermute | solution.py:595
  110.2 0.7 pad_maximum_fusion.4.refs_0_
  110.9 2.9 %collective-permute-start.8 = (bf16[416,128]{1,0:T(8,128)(2,1)}, bf16[416,128]{1,0:T(8,128)(2,1)}, u32[]{:S(2)}, u32[]{:S(2)}) collective-permute-start(bf16[416,128]{1,0:T(8,128)(2,1)} %pad_maximum_fusion.4.refs_0_), channel_id=1, source_target_pairs={{0,4},{1,5},{2,6},{3,7},{4,0},{5,1},{6,2},{7,3},{8,12},{9,13},{10,... | collective-permute-start | bytes 319496 | tf_op jit(solution)/shard_map/ppermute | solution.py:595
  113.8 1.5 collective-permute-start.9
  115.3 6.0 %all-to-all-start.3 = ((bf16[8,2,3,128,128]{4,3,2,1,0:T(8,128)(2,1)}), bf16[8,2,3,128,128]{4,3,2,1,0:T(8,128)(2,1)}, u32[]{:S(2)}, u32[]{:S(2)}) async-start(bf16[8,2,3,128,128]{4,3,2,1,0:T(8,128)(2,1)} %get-tuple-element.81.rest_ref), calls=%async_computation.3 | async-start | bytes 3145728 | tf_op jit(solution)/shard_map/all_to_all | solution.py:687
  121.3 4.7 %finish_proj.1 = (bf16[256,1024]{1,0:T(8,128)(2,1)}, bf16[2048,128]{1,0:T(8,128)(2,1)}) custom-call(bf16[8,2,128,128]{3,2,1,0:T(8,128)(2,1)} %all-to-all-done.2.att_ref, bf16[256,1024]{1,0:T(8,128)(2,1)} %bitcast.15, bf16[256,1024]{1,0:T(8,128)(2,1)} %bitcast.19, f32[256,1024]{1,0:T(8,128)} %get-tuple-element.71.shrunk_ref, bf16[1024,1024]{1,0:T(8,128)(2,1)} %wp_ref.3, ...), custom_call_target="tpu_custom_call" | custom-call | flops 199999995904 | bytes 1 | tf_op jit(solution)/shard_map/finish_proj/pallas_call | solution.py:499
  126.0 1.8 join.1
  127.9 0.5 collective-permute-start.11
  128.4 1.7 slice.103
  130.1 8.0 %collective-permute-done.11 = bf16[1664,128]{1,0:T(8,128)(2,1)S(1)} collective-permute-done((bf16[1664,128]{1,0:T(8,128)(2,1)}, bf16[1664,128]{1,0:T(8,128)(2,1)S(1)}, u32[]{:S(2)}, u32[]{:S(2)}) %collective-permute-start.11) | collective-permute-done | bytes 426016 | tf_op jit(solution)/shard_map/ppermute | solution.py:595
  138.1 0.8 copy-done.4
  138.8 2.0 pad_maximum_fusion.1
  140.8 1.7 collective-permute-start.12
  142.5 14.9 %all-to-all-done.3.msg_away = bf16[8,2,3,128,128]{4,3,2,1,0:T(8,128)(2,1)} async-done(((bf16[8,2,3,128,128]{4,3,2,1,0:T(8,128)(2,1)}), bf16[8,2,3,128,128]{4,3,2,1,0:T(8,128)(2,1)}, u32[]{:S(2)}, u32[]{:S(2)}) %all-to-all-start.3) | async-done | bytes 1572896 | tf_op jit(solution)/shard_map/all_to_all | solution.py:687
  157.4 8.5 %finish.1 = (bf16[256,1024]{1,0:T(8,128)(2,1)}, bf16[1152,128]{1,0:T(8,128)(2,1)}) custom-call(bf16[256,1024]{1,0:T(8,128)(2,1)} %bitcast.16, bf16[8,2,3,128,128]{4,3,2,1,0:T(8,128)(2,1)} %all-to-all-done.3.msg_away, bf16[128,3072]{1,0:T(8,128)(2,1)} %rj_away.1, bf16[1024,3072]{1,0:T(8,128)(2,1)} %wj_away.1, bf16[1024,128]{1,0:T(8,128)(2,1)} %lj_away.1, ...), custom_call_target="tpu_custom_call" | custom-call | flops 199999995904 | bytes 1 | tf_op jit(solution)/shard_map/finish/pallas_call | solution.py:560
  166.0 1.3 pad_maximum_fusion.refs_0_
  167.3 1.2 copy-done
  168.6 0.6 collective-permute-start.13
  169.2 1.0 add_convert_fusion.3
  170.2 0.6 collective-permute-start.17
  170.8 1.2 collective-permute-done.13
  172.1 0.6 collective-permute-start.14
  172.7 3.6 %collective-permute-done.17 = bf16[512,128]{1,0:T(8,128)(2,1)S(1)} collective-permute-done((bf16[512,128]{1,0:T(8,128)(2,1)S(1)}, bf16[512,128]{1,0:T(8,128)(2,1)S(1)}, u32[]{:S(2)}, u32[]{:S(2)}) %collective-permute-start.17) | collective-permute-done | bytes 131104 | tf_op jit(solution)/shard_map/ppermute | solution.py:595
  176.3 1.4 collective-permute-start.18
  177.7 2.9 %collective-permute-done.18 = bf16[256,128]{1,0:T(8,128)(2,1)S(1)} collective-permute-done((bf16[256,128]{1,0:T(8,128)(2,1)S(1)}, bf16[256,128]{1,0:T(8,128)(2,1)S(1)}, u32[]{:S(2)}, u32[]{:S(2)}) %collective-permute-start.18) | collective-permute-done | bytes 65568 | tf_op jit(solution)/shard_map/ppermute | solution.py:595
  180.7 1.4 collective-permute-start.15
  182.1 2.6 %collective-permute-done.15 = bf16[144,128]{1,0:T(8,128)(2,1)S(1)} collective-permute-done((bf16[144,128]{1,0:T(8,128)(2,1)S(1)}, bf16[144,128]{1,0:T(8,128)(2,1)S(1)}, u32[]{:S(2)}, u32[]{:S(2)}) %collective-permute-start.15) | collective-permute-done | bytes 36896 | tf_op jit(solution)/shard_map/ppermute | solution.py:595
  184.8 3.0 %collective-permute-start.22 = (bf16[400,128]{1,0:T(8,128)(2,1)S(1)}, bf16[400,128]{1,0:T(8,128)(2,1)S(1)}, u32[]{:S(2)}, u32[]{:S(2)}) collective-permute-start(bf16[400,128]{1,0:T(8,128)(2,1)S(1)} %pad_maximum_fusion.5), channel_id=1, source_target_pairs={{0,6},{1,7},{2,4},{3,5},{4,2},{5,3},{6,0},{7,1},{8,14},{9,15},{10,... | collective-permute-start | bytes 307208 | tf_op jit(solution)/shard_map/ppermute | solution.py:595
  187.8 2.1 %collective-permute-start.21 = (bf16[400,128]{1,0:T(8,128)(2,1)S(1)}, bf16[400,128]{1,0:T(8,128)(2,1)S(1)}, u32[]{:S(2)}, u32[]{:S(2)}) collective-permute-start(bf16[400,128]{1,0:T(8,128)(2,1)S(1)} %pad_maximum_fusion.5), channel_id=1, source_target_pairs={{0,2},{1,3},{2,0},{3,1},{4,6},{5,7},{6,4},{7,5},{8,10},{9,11},{10,... | collective-permute-start | bytes 307208 | tf_op jit(solution)/shard_map/ppermute | solution.py:595
  190.0 5.0 %unpack.2 = (f32[1024,128]{1,0:T(8,128)}, f32[128,4096]{1,0:T(8,128)}, f32[4096,128]{1,0:T(8,128)}, f32[128,1024]{1,0:T(8,128)}, f32[128,3072]{1,0:T(8,128)}) custom-call(bf16[6656,128]{1,0:T(8,128)(2,1)} %copy-done, bf16[6656,128]{1,0:T(8,128)(2,1)} %collective-permute-done.20.refs_1_), custom_call_target="tpu_custom_call" | custom-call | flops 1 | bytes 1 | tf_op jit(solution)/shard_map/unpack/pallas_call | solution.py:623
  194.9 1.1 collective-permute-done.19
  196.2 4.6 %collective-permute-done.23 = bf16[400,128]{1,0:T(8,128)(2,1)S(1)} collective-permute-done((bf16[400,128]{1,0:T(8,128)(2,1)S(1)}, bf16[400,128]{1,0:T(8,128)(2,1)S(1)}, u32[]{:S(2)}, u32[]{:S(2)}) %collective-permute-start.23) | collective-permute-done | bytes 102432 | tf_op jit(solution)/shard_map/ppermute | solution.py:595
  200.8 0.6 collective-permute-start.24
  201.4 5.3 %collective-permute-done.24 = bf16[800,128]{1,0:T(8,128)(2,1)S(1)} collective-permute-done((bf16[800,128]{1,0:T(8,128)(2,1)S(1)}, bf16[800,128]{1,0:T(8,128)(2,1)S(1)}, u32[]{:S(2)}, u32[]{:S(2)}) %collective-permute-start.24) | collective-permute-done | bytes 204832 | tf_op jit(solution)/shard_map/ppermute | solution.py:595
  206.8 1.7 collective-permute-done.25.refs_1_
  208.5 0.8 copy-done.9
  209.3 2.4 %unpack.3 = (f32[1024,128]{1,0:T(8,128)}, f32[1024,128]{1,0:T(8,128)}, f32[128,1024]{1,0:T(8,128)}, f32[8,128]{1,0:T(8,128)}, f32[8,128]{1,0:T(8,128)}, /*index=5*/f32[8,128]{1,0:T(8,128)}, f32[8,128]{1,0:T(8,128)}) custom-call(bf16[1600,128]{1,0:T(8,128)(2,1)} %copy-done.6, bf16[1600,128]{1,0:T(8,128)(2,1)} %copy-done.9), custom_call_target="tpu_custom_call" | custom-call | flops 1 | bytes 1 | tf_op jit(solution)/shard_map/unpack/pallas_call | solution.py:623
  (59 shorter events, 1.0 us)
Async XLA Ops:
  9.5 55.7 %all-to-all-start = ((bf16[8,2,4,128,128]{4,3,2,1,0:T(8,128)(2,1)}), bf16[8,2,4,128,128]{4,3,2,1,0:T(8,128)(2,1)}, u32[]{:S(2)}, u32[]{:S(2)}) async-start(bf16[8,2,4,128,128]{4,3,2,1,0:T(8,128)(2,1)} %get-tuple-element.59), calls=%async_computation | async-start | bytes 4194304 | tf_op jit(solution)/shard_map/all_to_all | solution.py:683
  37.8 4.7 %copy-start.3 = (bf16[10240,128]{1,0:T(8,128)(2,1)S(1)}, bf16[10240,128]{1,0:T(8,128)(2,1)}, u32[]{:S(2)}) copy-start(bf16[10240,128]{1,0:T(8,128)(2,1)} %get-tuple-element.64) | copy-start | bytes 7864324
  39.3 3.1 %collective-permute-start = (bf16[5120,128]{1,0:T(8,128)(2,1)S(1)}, bf16[5120,128]{1,0:T(8,128)(2,1)S(1)}, u32[]{:S(2)}, u32[]{:S(2)}) collective-permute-start(bf16[5120,128]{1,0:T(8,128)(2,1)S(1)} %slice.83), channel_id=1, source_target_pairs={{0,8},{1,9},{2,10},{3,11},{4,12},{5,13},{6,14},{7,15},{8,0},{9,1},... | collective-permute-start | bytes 3932168 | tf_op jit(solution)/shard_map/ppermute | solution.py:595
  42.8 1.1 copy-start.1
  44.7 28.2 %collective-permute-start.1 = (bf16[2560,128]{1,0:T(8,128)(2,1)}, bf16[2560,128]{1,0:T(8,128)(2,1)}, u32[]{:S(2)}, u32[]{:S(2)}) collective-permute-start(bf16[2560,128]{1,0:T(8,128)(2,1)} %slice.109), channel_id=1, source_target_pairs={{0,1},{1,0},{2,3},{3,2},{4,5},{5,4},{6,7},{7,6},{8,9},{9,8},{10,11... | collective-permute-start | bytes 1966088 | tf_op jit(solution)/shard_map/ppermute | solution.py:595
  74.4 13.7 %collective-permute-start.2 = (bf16[1280,128]{1,0:T(8,128)(2,1)S(1)}, bf16[1280,128]{1,0:T(8,128)(2,1)}, u32[]{:S(2)}, u32[]{:S(2)}) collective-permute-start(bf16[1280,128]{1,0:T(8,128)(2,1)S(1)} %slice.111), channel_id=1, source_target_pairs={{0,16},{1,17},{2,18},{3,19},{4,20},{5,21},{6,22},{7,23},{8,24},{9,... | collective-permute-start | bytes 983048 | tf_op jit(solution)/shard_map/ppermute | solution.py:595
  76.0 19.7 %all-to-all-start.1 = ((bf16[8,256,128]{2,1,0:T(8,128)(2,1)}), bf16[8,256,128]{2,1,0:T(8,128)(2,1)}, u32[]{:S(2)}, u32[]{:S(2)}) async-start(bf16[8,256,128]{2,1,0:T(8,128)(2,1)} %get-tuple-element.69), calls=%async_computation.1 | async-start | bytes 1048576 | tf_op jit(solution)/shard_map/all_to_all | solution.py:706
  89.2 0.7 copy-start.7
  90.6 13.6 %collective-permute-start.5 = (bf16[320,128]{1,0:T(8,128)(2,1)}, bf16[320,128]{1,0:T(8,128)(2,1)}, u32[]{:S(2)}, u32[]{:S(2)}) collective-permute-start(bf16[320,128]{1,0:T(8,128)(2,1)} %get-tuple-element.105), channel_id=1, source_target_pairs={{0,6},{1,7},{2,4},{3,5},{4,2},{5,3},{6,0},{7,1},{8,14},{9,15},{10,... | collective-permute-start | bytes 245768 | tf_op jit(solution)/shard_map/ppermute | solution.py:595
  94.1 10.2 %collective-permute-start.4 = (bf16[320,128]{1,0:T(8,128)(2,1)}, bf16[320,128]{1,0:T(8,128)(2,1)}, u32[]{:S(2)}, u32[]{:S(2)}) collective-permute-start(bf16[320,128]{1,0:T(8,128)(2,1)} %get-tuple-element.106), channel_id=1, source_target_pairs={{0,2},{1,3},{2,0},{3,1},{4,6},{5,7},{6,4},{7,5},{8,10},{9,11},{10,... | collective-permute-start | bytes 245768 | tf_op jit(solution)/shard_map/ppermute | solution.py:595
  94.1 10.2 %collective-permute-start.3 = (bf16[320,128]{1,0:T(8,128)(2,1)}, bf16[320,128]{1,0:T(8,128)(2,1)}, u32[]{:S(2)}, u32[]{:S(2)}) collective-permute-start(bf16[320,128]{1,0:T(8,128)(2,1)} %get-tuple-element.104), channel_id=1, source_target_pairs={{0,4},{1,5},{2,6},{3,7},{4,0},{5,1},{6,2},{7,3},{8,12},{9,13},{10,... | collective-permute-start | bytes 245768 | tf_op jit(solution)/shard_map/ppermute | solution.py:595
  95.7 19.6 %all-to-all-start.2 = ((bf16[8,2,128,128]{3,2,1,0:T(8,128)(2,1)}), bf16[8,2,128,128]{3,2,1,0:T(8,128)(2,1)}, u32[]{:S(2)}, u32[]{:S(2)}) async-start(bf16[8,2,128,128]{3,2,1,0:T(8,128)(2,1)} %get-tuple-element.70), calls=%async_computation.2 | async-start | bytes 1048576 | tf_op jit(solution)/shard_map/all_to_all | solution.py:687
  104.3 1.2 collective-permute-start.6
  106.3 3.9 %collective-permute-start.7 = (bf16[96,128]{1,0:T(8,128)(2,1)S(1)}, bf16[96,128]{1,0:T(8,128)(2,1)S(1)}, u32[]{:S(2)}, u32[]{:S(2)}) collective-permute-start(bf16[96,128]{1,0:T(8,128)(2,1)S(1)} %slice.119), channel_id=1, source_target_pairs={{0,16},{1,17},{2,18},{3,19},{4,20},{5,21},{6,22},{7,23},{8,24},{9,... | collective-permute-start | bytes 73736 | tf_op jit(solution)/shard_map/ppermute | solution.py:595
  110.9 15.1 %collective-permute-start.8 = (bf16[416,128]{1,0:T(8,128)(2,1)}, bf16[416,128]{1,0:T(8,128)(2,1)}, u32[]{:S(2)}, u32[]{:S(2)}) collective-permute-start(bf16[416,128]{1,0:T(8,128)(2,1)} %pad_maximum_fusion.4.refs_0_), channel_id=1, source_target_pairs={{0,4},{1,5},{2,6},{3,7},{4,0},{5,1},{6,2},{7,3},{8,12},{9,13},{10,... | collective-permute-start | bytes 319496 | tf_op jit(solution)/shard_map/ppermute | solution.py:595
  113.8 12.2 %collective-permute-start.9 = (bf16[416,128]{1,0:T(8,128)(2,1)}, bf16[416,128]{1,0:T(8,128)(2,1)}, u32[]{:S(2)}, u32[]{:S(2)}) collective-permute-start(bf16[416,128]{1,0:T(8,128)(2,1)} %pad_maximum_fusion.4.refs_0_), channel_id=1, source_target_pairs={{0,2},{1,3},{2,0},{3,1},{4,6},{5,7},{6,4},{7,5},{8,10},{9,11},{10,... | collective-permute-start | bytes 319496 | tf_op jit(solution)/shard_map/ppermute | solution.py:595
  115.3 10.7 %collective-permute-start.10 = (bf16[416,128]{1,0:T(8,128)(2,1)}, bf16[416,128]{1,0:T(8,128)(2,1)}, u32[]{:S(2)}, u32[]{:S(2)}) collective-permute-start(bf16[416,128]{1,0:T(8,128)(2,1)} %pad_maximum_fusion.4.refs_0_), channel_id=1, source_target_pairs={{0,6},{1,7},{2,4},{3,5},{4,2},{5,3},{6,0},{7,1},{8,14},{9,15},{10,... | collective-permute-start | bytes 319496 | tf_op jit(solution)/shard_map/ppermute | solution.py:595
  115.3 42.1 %all-to-all-start.3 = ((bf16[8,2,3,128,128]{4,3,2,1,0:T(8,128)(2,1)}), bf16[8,2,3,128,128]{4,3,2,1,0:T(8,128)(2,1)}, u32[]{:S(2)}, u32[]{:S(2)}) async-start(bf16[8,2,3,128,128]{4,3,2,1,0:T(8,128)(2,1)} %get-tuple-element.81.rest_ref), calls=%async_computation.3 | async-start | bytes 3145728 | tf_op jit(solution)/shard_map/all_to_all | solution.py:687
  127.9 10.2 %collective-permute-start.11 = (bf16[1664,128]{1,0:T(8,128)(2,1)}, bf16[1664,128]{1,0:T(8,128)(2,1)S(1)}, u32[]{:S(2)}, u32[]{:S(2)}) collective-permute-start(bf16[1664,128]{1,0:T(8,128)(2,1)} %join.1), channel_id=1, source_target_pairs={{0,16},{1,17},{2,18},{3,19},{4,20},{5,21},{6,22},{7,23},{8,24},{9,... | collective-permute-start | bytes 1277960 | tf_op jit(solution)/shard_map/ppermute | solution.py:595
  130.1 39.1 %collective-permute-start.16 = (bf16[1024,128]{1,0:T(8,128)(2,1)}, bf16[1024,128]{1,0:T(8,128)(2,1)}, u32[]{:S(2)}, u32[]{:S(2)}) collective-permute-start(bf16[1024,128]{1,0:T(8,128)(2,1)} %slice.103), channel_id=1, source_target_pairs={{0,8},{1,9},{2,10},{3,11},{4,12},{5,13},{6,14},{7,15},{8,0},{9,1},... | collective-permute-start | bytes 786440 | tf_op jit(solution)/shard_map/ppermute | solution.py:595
  138.1 0.8 copy-start.4
  140.8 25.1 %collective-permute-start.12 = (bf16[3328,128]{1,0:T(8,128)(2,1)}, bf16[3328,128]{1,0:T(8,128)(2,1)}, u32[]{:S(2)}, u32[]{:S(2)}) collective-permute-start(bf16[3328,128]{1,0:T(8,128)(2,1)} %pad_maximum_fusion.1), channel_id=1, source_target_pairs={{0,1},{1,0},{2,3},{3,2},{4,5},{5,4},{6,7},{7,6},{8,9},{9,8},{10,11... | collective-permute-start | bytes 2555912 | tf_op jit(solution)/shard_map/ppermute | solution.py:595
  157.4 8.5 %copy-start.2 = (bf16[1664,128]{1,0:T(8,128)(2,1)S(1)}, bf16[1664,128]{1,0:T(8,128)(2,1)}, u32[]{:S(2)}) copy-start(bf16[1664,128]{1,0:T(8,128)(2,1)} %join.1) | copy-start | bytes 1277956
  157.4 8.5 %copy-start.5 = (bf16[1664,128]{1,0:T(8,128)(2,1)S(1)}, bf16[1664,128]{1,0:T(8,128)(2,1)}, u32[]{:S(2)}) copy-start(bf16[1664,128]{1,0:T(8,128)(2,1)} %copy-done.4) | copy-start | bytes 1277956
  166.0 2.6 %copy-start.10 = (bf16[1152,128]{1,0:T(8,128)(2,1)S(1)}, bf16[1152,128]{1,0:T(8,128)(2,1)}, u32[]{:S(2)}) copy-start(bf16[1152,128]{1,0:T(8,128)(2,1)} %get-tuple-element.86) | copy-start | bytes 884740
  166.0 3.2 %copy-start.8 = (bf16[2048,128]{1,0:T(8,128)(2,1)S(1)}, bf16[2048,128]{1,0:T(8,128)(2,1)}, u32[]{:S(2)}) copy-start(bf16[2048,128]{1,0:T(8,128)(2,1)} %get-tuple-element.87) | copy-start | bytes 1572868
  167.3 1.2 copy-start
  168.6 21.4 %collective-permute-start.20 = (bf16[6656,128]{1,0:T(8,128)(2,1)S(1)}, bf16[6656,128]{1,0:T(8,128)(2,1)}, u32[]{:S(2)}, u32[]{:S(2)}) collective-permute-start(bf16[6656,128]{1,0:T(8,128)(2,1)S(1)} %pad_maximum_fusion.refs_0_), channel_id=1, source_target_pairs={{0,8},{1,9},{2,10},{3,11},{4,12},{5,13},{6,14},{7,15},{8,0},{9,1},... | collective-permute-start | bytes 5111816 | tf_op jit(solution)/shard_map/ppermute | solution.py:595
  168.6 3.4 %collective-permute-start.13 = (bf16[576,128]{1,0:T(8,128)(2,1)S(1)}, bf16[576,128]{1,0:T(8,128)(2,1)S(1)}, u32[]{:S(2)}, u32[]{:S(2)}) collective-permute-start(bf16[576,128]{1,0:T(8,128)(2,1)S(1)} %slice.97), channel_id=1, source_target_pairs={{0,8},{1,9},{2,10},{3,11},{4,12},{5,13},{6,14},{7,15},{8,0},{9,1},... | collective-permute-start | bytes 442376 | tf_op jit(solution)/shard_map/ppermute | solution.py:595
  170.2 6.1 %collective-permute-start.17 = (bf16[512,128]{1,0:T(8,128)(2,1)S(1)}, bf16[512,128]{1,0:T(8,128)(2,1)S(1)}, u32[]{:S(2)}, u32[]{:S(2)}) collective-permute-start(bf16[512,128]{1,0:T(8,128)(2,1)S(1)} %slice.125), channel_id=1, source_target_pairs={{0,16},{1,17},{2,18},{3,19},{4,20},{5,21},{6,22},{7,23},{8,24},{9,... | collective-permute-start | bytes 393224 | tf_op jit(solution)/shard_map/ppermute | solution.py:595
  172.1 8.6 %collective-permute-start.14 = (bf16[288,128]{1,0:T(8,128)(2,1)S(1)}, bf16[288,128]{1,0:T(8,128)(2,1)S(1)}, u32[]{:S(2)}, u32[]{:S(2)}) collective-permute-start(bf16[288,128]{1,0:T(8,128)(2,1)S(1)} %slice.121), channel_id=1, source_target_pairs={{0,16},{1,17},{2,18},{3,19},{4,20},{5,21},{6,22},{7,23},{8,24},{9,... | collective-permute-start | bytes 221192 | tf_op jit(solution)/shard_map/ppermute | solution.py:595
  176.3 4.3 %collective-permute-start.18 = (bf16[256,128]{1,0:T(8,128)(2,1)S(1)}, bf16[256,128]{1,0:T(8,128)(2,1)S(1)}, u32[]{:S(2)}, u32[]{:S(2)}) collective-permute-start(bf16[256,128]{1,0:T(8,128)(2,1)S(1)} %slice.127), channel_id=1, source_target_pairs={{0,1},{1,0},{2,3},{3,2},{4,5},{5,4},{6,7},{7,6},{8,9},{9,8},{10,11... | collective-permute-start | bytes 196616 | tf_op jit(solution)/shard_map/ppermute | solution.py:595
  180.7 4.0 %collective-permute-start.15 = (bf16[144,128]{1,0:T(8,128)(2,1)S(1)}, bf16[144,128]{1,0:T(8,128)(2,1)S(1)}, u32[]{:S(2)}, u32[]{:S(2)}) collective-permute-start(bf16[144,128]{1,0:T(8,128)(2,1)S(1)} %slice.123), channel_id=1, source_target_pairs={{0,1},{1,0},{2,3},{3,2},{4,5},{5,4},{6,7},{7,6},{8,9},{9,8},{10,11... | collective-permute-start | bytes 110600 | tf_op jit(solution)/shard_map/ppermute | solution.py:595
  184.8 10.2 %collective-permute-start.22 = (bf16[400,128]{1,0:T(8,128)(2,1)S(1)}, bf16[400,128]{1,0:T(8,128)(2,1)S(1)}, u32[]{:S(2)}, u32[]{:S(2)}) collective-permute-start(bf16[400,128]{1,0:T(8,128)(2,1)S(1)} %pad_maximum_fusion.5), channel_id=1, source_target_pairs={{0,6},{1,7},{2,4},{3,5},{4,2},{5,3},{6,0},{7,1},{8,14},{9,15},{10,... | collective-permute-start | bytes 307208 | tf_op jit(solution)/shard_map/ppermute | solution.py:595
  187.8 7.1 %collective-permute-start.21 = (bf16[400,128]{1,0:T(8,128)(2,1)S(1)}, bf16[400,128]{1,0:T(8,128)(2,1)S(1)}, u32[]{:S(2)}, u32[]{:S(2)}) collective-permute-start(bf16[400,128]{1,0:T(8,128)(2,1)S(1)} %pad_maximum_fusion.5), channel_id=1, source_target_pairs={{0,2},{1,3},{2,0},{3,1},{4,6},{5,7},{6,4},{7,5},{8,10},{9,11},{10,... | collective-permute-start | bytes 307208 | tf_op jit(solution)/shard_map/ppermute | solution.py:595
  189.9 6.1 %collective-permute-start.19 = (bf16[400,128]{1,0:T(8,128)(2,1)S(1)}, bf16[400,128]{1,0:T(8,128)(2,1)S(1)}, u32[]{:S(2)}, u32[]{:S(2)}) collective-permute-start(bf16[400,128]{1,0:T(8,128)(2,1)S(1)} %pad_maximum_fusion.5), channel_id=1, source_target_pairs={{0,4},{1,5},{2,6},{3,7},{4,0},{5,1},{6,2},{7,3},{8,12},{9,13},{10,... | collective-permute-start | bytes 307208 | tf_op jit(solution)/shard_map/ppermute | solution.py:595
  196.1 4.7 %collective-permute-start.23 = (bf16[400,128]{1,0:T(8,128)(2,1)S(1)}, bf16[400,128]{1,0:T(8,128)(2,1)S(1)}, u32[]{:S(2)}, u32[]{:S(2)}) collective-permute-start(bf16[400,128]{1,0:T(8,128)(2,1)S(1)} %add_convert_fusion.6), channel_id=1, source_target_pairs={{0,1},{1,0},{2,3},{3,2},{4,5},{5,4},{6,7},{7,6},{8,9},{9,8},{10,11... | collective-permute-start | bytes 307208 | tf_op jit(solution)/shard_map/ppermute | solution.py:595
  200.8 5.8 %collective-permute-start.24 = (bf16[800,128]{1,0:T(8,128)(2,1)S(1)}, bf16[800,128]{1,0:T(8,128)(2,1)S(1)}, u32[]{:S(2)}, u32[]{:S(2)}) collective-permute-start(bf16[800,128]{1,0:T(8,128)(2,1)S(1)} %pad_maximum_fusion.3), channel_id=1, source_target_pairs={{0,16},{1,17},{2,18},{3,19},{4,20},{5,21},{6,22},{7,23},{8,24},{9,... | collective-permute-start | bytes 614408 | tf_op jit(solution)/shard_map/ppermute | solution.py:595
  206.7 1.8 copy-start.6
  206.7 1.8 collective-permute-start.25
  208.5 0.8 copy-start.9

commit v4 on v3

--- a/solution.py
+++ b/solution.py
@@ -187,6 +187,11 @@
     return jnp.concatenate([packed, after(swap(packed, 1 << bit, size), *hold)])
 
 
+def last_two(packed, bit, last_bit, size):
+    parts = [packed, swap(packed, 1 << bit, size)]
+    return parts + [swap(part, 1 << last_bit, size) for part in parts]
+
+
 def join_kernel(*refs):
     *part_refs, out_ref = refs
     for place, part_ref in enumerate(part_refs):
@@ -209,8 +214,29 @@
     return [1 << pair[1], 1 << pair[0], (1 << pair[0]) | (1 << pair[1])]
 
 
-def quarter(packed, pair, size, *hold):
-    blocks = packed.reshape(4, packed.shape[0] // 4, RANK)
+def fold_kernel(keep_ref, other_ref, *block_refs):
+    rows = block_refs[0].shape[0]
+    for place, block_ref in enumerate(block_refs):
+        here = slice(place * rows, (place + 1) * rows)
+        block_ref[...] = (keep_ref[here].astype(F32) + other_ref[here].astype(F32)).astype(BF)
+
+
+def fold(packed, bit, size, *hold):
+    half = packed.shape[0] // 2
+    other = after(swap(packed[half:], 1 << bit, size), *hold)
+    return pl.pallas_call(
+        fold_kernel,
+        grid=(1,),
+        in_specs=[pl.BlockSpec((half, RANK), lambda j: (0, 0))] * 2,
+        out_specs=[pl.BlockSpec((half // 4, RANK), lambda j: (0, 0))] * 4,
+        out_shape=[jax.ShapeDtypeStruct((half // 4, RANK), BF)] * 4,
+        compiler_params=pltpu.CompilerParams(vmem_limit_bytes=WIDE),
+        cost_estimate=LITTLE,
+        name="fold",
+    )(packed, other)
+
+
+def quarter(blocks, pair, size, *hold):
     others = [swap(blocks[k + 1], mask, size) for k, mask in enumerate(masks(pair))]
     return add_all(blocks[0], [after(other, *hold) for other in others])
 
@@ -514,8 +540,8 @@
 
 def finish_kernel(
     packing, x_away, msg_away, rj_away, wj_away, lj_away, gfeed_away, g_away,
-    mgain_ref, mshift_ref, fgain_ref, igrad_ref, pack_ref,
-    x_ref, msg_ref, rj_ref, wj_ref, lj_ref, gfeed_ref, g_ref, sems,
+    mgain_ref, mshift_ref, fgain_ref, igrad_ref, keep_ref, give_ref,
+    x_ref, msg_ref, rj_ref, wj_ref, lj_ref, gfeed_ref, g_ref, pack_ref, sems,
 ):
     x_in, msg_in, rj_in, w0_in, w1_in, w2_in, lj_in, gfeed_in, g_in = fetch([
         (x_away, x_ref), (msg_away, msg_ref), (rj_away, rj_ref),
@@ -546,6 +572,8 @@
     pieces = [v[:, c * RANK : (c + 1) * RANK] for v in sums for c in range(D // RANK)]
     norms = jnp.concatenate(pieces + [jnp.zeros((RANK - len(pieces), RANK), F32)], axis=0)
     packing.put_rows(pack_ref, LATE_UNITS["norms"], norms)
+    keep_ref[...] = pack_ref[: LATE_ROWS // 2]
+    give_ref[...] = pack_ref[LATE_ROWS // 2 :]
     pulled = grad_mixer * mgain_ref[...] + grad_feed * fgain_ref[...]
     along = jnp.mean(pulled * hat, axis=-1, keepdims=True)
     level = jnp.mean(pulled, axis=-1, keepdims=True)
@@ -560,8 +588,10 @@
     return pl.pallas_call(
         partial(finish_kernel, packing),
         in_specs=[pl.BlockSpec(memory_space=pl.ANY)] * len(loads) + [held] * 3,
-        out_shape=[jax.ShapeDtypeStruct((tokens, D), BF), jax.ShapeDtypeStruct((LATE_ROWS, RANK), BF)],
-        scratch_shapes=[pltpu.VMEM(load.shape, load.dtype) for load in loads] + [pltpu.SemaphoreType.DMA((9,))],
+        out_shape=[jax.ShapeDtypeStruct((tokens, D), BF)] + [jax.ShapeDtypeStruct((LATE_ROWS // 2, RANK), BF)] * 2,
+        scratch_shapes=[pltpu.VMEM(load.shape, load.dtype) for load in loads] + [
+            pltpu.VMEM((LATE_ROWS, RANK), BF), pltpu.SemaphoreType.DMA((9,)),
+        ],
         compiler_params=pltpu.CompilerParams(vmem_limit_bytes=WIDE),
         cost_estimate=MUCH,
         name="finish",
@@ -709,9 +739,10 @@
     for row in range(1, my_rows):
         answer = attend(arrived, doc_lengths, row, answer, row_parts, head_parts)
     attended, rest = answer
-    while len(steps) > 2:
+    while len(steps) > 3:
         part = halve(part, steps.pop(0), size, *answer)
-    attended = send_back(after(attended, part, low_all))
+    part = fold(part, steps.pop(0), size, *answer)
+    attended = send_back(after(attended, low_all, *part))
 
     low_all = low_all.reshape(devices, rows, slots, RANK)
     first_row = (me // head_parts) % row_parts * my_rows
@@ -730,17 +761,16 @@
     )
     early = join(everyone(early, steps, size, output))
     early = double(early, order[-3], size)
-    for bit in late_order[:2]:
-        proj_part = halve(proj_part, bit, size)
-    input_grad, late_part = finish(
-        returned, after(x, early), g, grad_feed, joined_weight, joined_left, joined_right,
+    proj_part = quarter(jnp.split(proj_part, 4), late_order[:2], size)
+    input_grad, late_part, late_give = finish(
+        returned, after(x, early, proj_part), g, grad_feed, joined_weight, joined_left, joined_right,
         mixer_gain, mixer_shift, feed_gain, late_packing,
     )
-    proj_part = halve(proj_part, late_order[2], size, late_part)
-    for bit in order[-4:0:-1]:
-        early = double(early, bit, size, late_part)
-    late_part = after(late_part, early)
-    early = [early, swap(early, 1 << order[0], size)]
+    late_part = add_low(late_part, swap(late_give, 1 << late_order[0], size))
+    late_part = halve(late_part, late_order[1], size)
+    for bit in order[-4:1:-1]:
+        early = double(early, bit, size)
+    early = last_two(early, order[1], order[0], size)
     feed_packing, right_packing = feed_packing.held(stride, 0), right_packing.held(stride, part.shape[0])
     early_grads = unpack(early, (
         (feed_packing, FEED_UNITS["expand_left"], (D, RANK), "rows"),
@@ -750,17 +780,17 @@
         (right_packing, 0, (RANK, 3 * D), "columns"),
     ))
 
-    for bit in late_order:
-        late_part = halve(late_part, bit, size)
-    stride, first = proj_part.shape[0] + late_part.shape[0], late_part.shape[0]
-    late = jnp.concatenate([late_part, proj_part])
+    both = [part.reshape(2, part.shape[0] // 2, RANK) for part in (late_part, proj_part)]
+    first, stride = both[0].shape[1], both[0].shape[1] + both[1].shape[1]
+    given = swap(jnp.concatenate([part[1] for part in both]), 1 << late_order[2], size)
+    late = add_low(jnp.concatenate([part[0] for part in both]), given)
     for bit in order[3:-2]:
         late = add_low(late, swap(late, 1 << bit, size))
     whole_late = everyone(late, order[-2:], size, *early_grads)
     late = add_all(whole_late[0], whole_late[1:])
-    for bit in late_order[:0:-1]:
+    for bit in late_order[:1:-1]:
         late = double(late, bit, size)
-    late = [late, swap(late, 1 << order[0], size)]
+    late = last_two(late, late_order[1], late_order[0], size)
     late_packing, proj_packing = late_packing.held(stride, 0), proj_packing.held(stride, first)
     late_grads = unpack(late, (
         (late_packing, LATE_UNITS["joined_left"], (D, RANK), "rows"),

time: 213 us -> 206 us (0.967)
  waiting for transfers between devices: 71.6 us -> 63.9 us
  starting transfers between devices: 48.5 us -> 52.1 us
  local copies, waits for them, and re-layouts: 10.2 us -> 7.02 us
    all_to_all x2, waiting for transfers between devices: 14.9 us -> 9.39 us  [send_back(): units = lax.all_to_all(units[..., :lanes], 'seq', 0, 0, tiled=True)]
    ppermute x26 -> x28, starting transfers between devices: 25.8 us -> 28.7 us  [swap(): lax.ppermute(part, ('batch', 'seq'), [(i, i ^ bit) for i in range(size)])]
    convert_element_type x2 -> x3, other arithmetic: 1.11 us -> 3.7 us  [add_all(): return total.astype(BF)]
    concatenate x4 -> x2, other arithmetic: 3.34 us -> 0.98 us  [double(): return jnp.concatenate([packed, after(swap(packed, 1 << bit, size), *hold)])]
    slice x11 -> x5, local copies, waits for them, and re-layouts: 4.99 us -> 3.25 us  [halve(): packed[half:]]
    ppermute x26 -> x28, waiting for transfers between devices: 37.6 us -> 36 us  [swap(): lax.ppermute(part, ('batch', 'seq'), [(i, i ^ bit) for i in range(size)])]
    convert_element_type x11 -> x7, other arithmetic: 4.84 us -> 3.64 us  [add_low(): return (left.astype(F32) + right.astype(F32)).astype(BF)]
  transfers between devices with their start and end apart: 30 -> 32, of which waited for: 15 -> 14; matrix products, arithmetic and copies ran while one was open for 7% -> 6% of each run, Pallas kernels for 28% -> 30%
where the time goes in v4:
time: 206 us
  Pallas kernels  72.5 us (35%)
  waiting for transfers between devices  63.9 us (31%)
  starting transfers between devices  52.1 us (25%)
  other arithmetic  8.98 us (4%)
  local copies, waits for them, and re-layouts  7.02 us (3%)
    ppermute x28, waiting for transfers between devices, swap(): lax.ppermute(part, ('batch', 'seq'), [(i, i ^ bit) for i in range(size)])  36 us
    ppermute x28, starting transfers between devices, swap(): lax.ppermute(part, ('batch', 'seq'), [(i, i ^ bit) for i in range(size)])  28.7 us
    pallas_call x1, Pallas kernels, feed(): pl.pallas_call(partial(feed_kernel, packing), grid=(FF // width,), in_spe...  21 us
    all_to_all x1, waiting for transfers between devices, send(): return lax.all_to_all(units, 'seq', 0, 0, tiled=True)  18.5 us
    pallas_call x2, Pallas kernels, attend(): pl.pallas_call(partial(attend_kernel, row, rows, row_parts, head_parts),...  15.5 us
    all_to_all x2, starting transfers between devices, send_back(): units = lax.all_to_all(units[..., :lanes], 'seq', 0, 0, tiled=True)  11.7 us
    all_to_all x2, waiting for transfers between devices, send_back(): units = lax.all_to_all(units[..., :lanes], 'seq', 0, 0, tiled=True)  9.39 us
    pallas_call x1, Pallas kernels, project(): pl.pallas_call(project_kernel, in_specs=[held, held, away, away] + [held]...  8.82 us
  transfers between devices with their start and end apart: 32, of which 14 were waited for; matrix products, arithmetic and copies ran while one was open for 6% of the time, Pallas kernels for 30%

profile of v4, /device:TPU:0, one launch (start us, length us, event | category | flops | bytes accessed | tf_op | source)
XLA Modules:
  0.0 205.6 jit_solution(6713996184159629644)
XLA Ops:
  0.6 8.8 %project.1 = (bf16[8,2,4,128,128]{4,3,2,1,0:T(8,128)(2,1)}, bf16[8,256,128]{2,1,0:T(8,128)(2,1)}, bf16[256,128]{1,0:T(8,128)(2,1)}) custom-call(bf16[256,1024]{1,0:T(8,128)(2,1)} %bitcast.13, bf16[256,1024]{1,0:T(8,128)(2,1)} %bitcast.17, bf16[1024,3072]{1,0:T(8,128)(2,1)} %wj_away.1, bf16[1024,1024]{1,0:T(8,128)(2,1)} %wp_ref.3, bf16[1024,128]{1,0:T(8,128)(2,1)} %lj_away.1, ...), custom_call_target="tpu_custom_call" | custom-call | flops 1 | bytes 1 | tf_op jit(solution)/shard_map/project/pallas_call | solution.py:312
  9.5 7.3 %all-to-all-start = ((bf16[8,2,4,128,128]{4,3,2,1,0:T(8,128)(2,1)}), bf16[8,2,4,128,128]{4,3,2,1,0:T(8,128)(2,1)}, u32[]{:S(2)}, u32[]{:S(2)}) async-start(bf16[8,2,4,128,128]{4,3,2,1,0:T(8,128)(2,1)} %get-tuple-element.61), calls=%async_computation | async-start | bytes 4194304 | tf_op jit(solution)/shard_map/all_to_all | solution.py:713
  16.8 21.0 %feed.1 = (f32[256,1024]{1,0:T(8,128)}, f32[256,1024]{1,0:T(8,128)}, bf16[10240,128]{1,0:T(8,128)(2,1)}) custom-call(bf16[256,1024]{1,0:T(8,128)(2,1)} %bitcast.14, bf16[256,1024]{1,0:T(8,128)(2,1)} %bitcast.18, bf16[1024,4096]{1,0:T(8,128)(2,1)} %we_ref.1, bf16[4096,1024]{1,0:T(8,128)(2,1)} %ws_ref.1, bf16[1024,128]{1,0:T(8,128)(2,1)} %le_ref.1, ...), custom_call_target="tpu_custom_call" | custom-call | flops 1 | bytes 1 | tf_op jit(solution)/shard_map/feed/pallas_call | solution.py:376
  37.7 1.6 slice.50
  39.4 3.0 %collective-permute-done = bf16[5120,128]{1,0:T(8,128)(2,1)S(1)} collective-permute-done((bf16[5120,128]{1,0:T(8,128)(2,1)S(1)}, bf16[5120,128]{1,0:T(8,128)(2,1)S(1)}, u32[]{:S(2)}, u32[]{:S(2)}) %collective-permute-start) | collective-permute-done | bytes 1310752 | tf_op jit(solution)/shard_map/ppermute | solution.py:625
  42.4 0.3 add_convert_fusion
  42.8 1.0 copy-done
  43.8 0.9 slice.65
  44.7 2.0 collective-permute-start.1
  46.7 18.5 %all-to-all-done.msg_ref = bf16[8,2,4,128,128]{4,3,2,1,0:T(8,128)(2,1)} async-done(((bf16[8,2,4,128,128]{4,3,2,1,0:T(8,128)(2,1)}), bf16[8,2,4,128,128]{4,3,2,1,0:T(8,128)(2,1)}, u32[]{:S(2)}, u32[]{:S(2)}) %all-to-all-start) | async-done | bytes 2097184 | tf_op jit(solution)/shard_map/all_to_all | solution.py:713
  65.2 7.8 %attend.2 = (bf16[8,2,128,128]{3,2,1,0:T(8,128)(2,1)}, bf16[8,2,3,128,128]{4,3,2,1,0:T(8,128)(2,1)}) custom-call(bf16[8,2,4,128,128]{4,3,2,1,0:T(8,128)(2,1)} %all-to-all-done.msg_ref, s32[2,8]{1,0:T(2,128)} %doc_ref.5), custom_call_target="tpu_custom_call" | custom-call | flops 199999995904 | bytes 1 | tf_op jit(solution)/shard_map/attend/pallas_call | solution.py:484
  72.9 4.4 %all-to-all-start.1 = ((bf16[8,256,128]{2,1,0:T(8,128)(2,1)}), bf16[8,256,128]{2,1,0:T(8,128)(2,1)}, u32[]{:S(2)}, u32[]{:S(2)}) async-start(bf16[8,256,128]{2,1,0:T(8,128)(2,1)} %get-tuple-element.66), calls=%async_computation.1 | async-start | bytes 1048576 | tf_op jit(solution)/shard_map/all_to_all | solution.py:736
  77.3 1.5 add_convert_fusion.1.keep_ref
  78.8 1.6 collective-permute-start.2
  80.4 7.8 %attend.3 = (bf16[8,2,128,128]{3,2,1,0:T(8,128)(2,1)}, bf16[8,2,3,128,128]{4,3,2,1,0:T(8,128)(2,1)}) custom-call(bf16[8,2,4,128,128]{4,3,2,1,0:T(8,128)(2,1)} %all-to-all-done.msg_ref, s32[2,8]{1,0:T(2,128)} %doc_ref.5, bf16[8,2,128,128]{3,2,1,0:T(8,128)(2,1)} %get-tuple-element.62.refs_0_, ...), custom_call_target="tpu_custom_call", output_to_operand_aliasing={{0}: (2, {}), {1}: (3, {})} | custom-call | flops 1 | bytes 1 | tf_op jit(solution)/shard_map/attend/pallas_call | solution.py:484
  88.2 1.8 fold.1
  90.0 3.5 %collective-permute-start.5 = (bf16[320,128]{1,0:T(8,128)(2,1)}, bf16[320,128]{1,0:T(8,128)(2,1)}, u32[]{:S(2)}, u32[]{:S(2)}) collective-permute-start(bf16[320,128]{1,0:T(8,128)(2,1)} %get-tuple-element.75), channel_id=1, source_target_pairs={{0,6},{1,7},{2,4},{3,5},{4,2},{5,3},{6,0},{7,1},{8,14},{9,15},{10,... | collective-permute-start | bytes 245768 | tf_op jit(solution)/shard_map/ppermute | solution.py:625
  93.5 0.9 collective-permute-start.3
  94.4 5.7 %all-to-all-start.2 = ((bf16[8,2,128,128]{3,2,1,0:T(8,128)(2,1)}), bf16[8,2,128,128]{3,2,1,0:T(8,128)(2,1)}, u32[]{:S(2)}, u32[]{:S(2)}) async-start(bf16[8,2,128,128]{3,2,1,0:T(8,128)(2,1)} %get-tuple-element.76), calls=%async_computation.2 | async-start | bytes 1048576 | tf_op jit(solution)/shard_map/all_to_all | solution.py:717
  100.0 2.8 %right.1 = bf16[384,128]{1,0:T(8,128)(2,1)} custom-call(bf16[8,2,3,128,128]{4,3,2,1,0:T(8,128)(2,1)} %get-tuple-element.88.rest_ref, bf16[8,2,128,128]{3,2,1,0:T(8,128)(2,1)} %bitcast.7.low_ref), custom_call_target="tpu_custom_call" | custom-call | flops 199999995904 | bytes 1 | tf_op jit(solution)/shard_map/right/pallas_call | solution.py:615
  102.9 0.8 slice.68
  103.7 1.2 collective-permute-done.6
  104.9 0.8 add_convert_fusion.8
  105.7 1.0 collective-permute-start.7
  106.8 1.0 add_convert_fusion.6
  107.8 1.8 collective-permute-done.7
  109.6 0.7 pad_maximum_fusion.2.refs_0_
  110.3 2.9 %collective-permute-start.8 = (bf16[416,128]{1,0:T(8,128)(2,1)}, bf16[416,128]{1,0:T(8,128)(2,1)}, u32[]{:S(2)}, u32[]{:S(2)}) collective-permute-start(bf16[416,128]{1,0:T(8,128)(2,1)} %pad_maximum_fusion.2.refs_0_), channel_id=1, source_target_pairs={{0,4},{1,5},{2,6},{3,7},{4,0},{5,1},{6,2},{7,3},{8,12},{9,13},{10,... | collective-permute-start | bytes 319496 | tf_op jit(solution)/shard_map/ppermute | solution.py:625
  113.2 1.5 collective-permute-start.9
  114.7 6.0 %all-to-all-start.3 = ((bf16[8,2,3,128,128]{4,3,2,1,0:T(8,128)(2,1)}), bf16[8,2,3,128,128]{4,3,2,1,0:T(8,128)(2,1)}, u32[]{:S(2)}, u32[]{:S(2)}) async-start(bf16[8,2,3,128,128]{4,3,2,1,0:T(8,128)(2,1)} %get-tuple-element.88.rest_ref), calls=%async_computation.3 | async-start | bytes 3145728 | tf_op jit(solution)/shard_map/all_to_all | solution.py:717
  120.7 4.7 %finish_proj.1 = (bf16[256,1024]{1,0:T(8,128)(2,1)}, bf16[2048,128]{1,0:T(8,128)(2,1)}) custom-call(bf16[8,2,128,128]{3,2,1,0:T(8,128)(2,1)} %all-to-all-done.2.att_ref, bf16[256,1024]{1,0:T(8,128)(2,1)} %bitcast.15, bf16[256,1024]{1,0:T(8,128)(2,1)} %bitcast.19, f32[256,1024]{1,0:T(8,128)} %get-tuple-element.77.shrunk_ref, bf16[1024,1024]{1,0:T(8,128)(2,1)} %wp_ref.3, ...), custom_call_target="tpu_custom_call" | custom-call | flops 199999995904 | bytes 1 | tf_op jit(solution)/shard_map/finish_proj/pallas_call | solution.py:525
  125.4 1.8 join.1
  127.2 1.0 collective-permute-start.11
  128.2 1.1 fusion
  129.3 1.2 collective-permute-start.13
  130.5 1.0 collective-permute-start.12
  131.5 8.7 %collective-permute-done.14 = bf16[512,128]{1,0:T(8,128)(2,1)S(1)} collective-permute-done((bf16[512,128]{1,0:T(8,128)(2,1)S(1)}, bf16[512,128]{1,0:T(8,128)(2,1)S(1)}, u32[]{:S(2)}, u32[]{:S(2)}) %collective-permute-start.14) | collective-permute-done | bytes 131104 | tf_op jit(solution)/shard_map/ppermute | solution.py:625
  140.2 2.9 %collective-permute-done.12 = bf16[512,128]{1,0:T(8,128)(2,1)S(1)} collective-permute-done((bf16[512,128]{1,0:T(8,128)(2,1)S(1)}, bf16[512,128]{1,0:T(8,128)(2,1)S(1)}, u32[]{:S(2)}, u32[]{:S(2)}) %collective-permute-start.12) | collective-permute-done | bytes 131104 | tf_op jit(solution)/shard_map/ppermute | solution.py:625
  143.1 1.6 add_convert_fusion.3
  144.7 1.0 pad_maximum_fusion.refs_0_
  145.7 1.7 collective-permute-start.19
  147.4 9.4 %all-to-all-done.3.msg_away = bf16[8,2,3,128,128]{4,3,2,1,0:T(8,128)(2,1)} async-done(((bf16[8,2,3,128,128]{4,3,2,1,0:T(8,128)(2,1)}), bf16[8,2,3,128,128]{4,3,2,1,0:T(8,128)(2,1)}, u32[]{:S(2)}, u32[]{:S(2)}) %all-to-all-start.3) | async-done | bytes 1572896 | tf_op jit(solution)/shard_map/all_to_all | solution.py:717
  156.8 8.5 %finish.1 = (bf16[256,1024]{1,0:T(8,128)(2,1)}, bf16[576,128]{1,0:T(8,128)(2,1)}, bf16[576,128]{1,0:T(8,128)(2,1)}) custom-call(bf16[256,1024]{1,0:T(8,128)(2,1)} %bitcast.16, bf16[8,2,3,128,128]{4,3,2,1,0:T(8,128)(2,1)} %all-to-all-done.3.msg_away, bf16[128,3072]{1,0:T(8,128)(2,1)} %rj_away.1, bf16[1024,3072]{1,0:T(8,128)(2,1)} %wj_away.1, ...), custom_call_target="tpu_custom_call" | custom-call | flops 199999995904 | bytes 1 | tf_op jit(solution)/shard_map/finish/pallas_call | solution.py:588
  165.4 1.6 collective-permute-done.15
  167.0 1.0 add_convert_fusion.2
  168.0 1.3 collective-permute-start.16
  169.4 0.5 collective-permute-start.21
  169.9 2.5 %collective-permute-done.16 = bf16[288,128]{1,0:T(8,128)(2,1)S(1)} collective-permute-done((bf16[288,128]{1,0:T(8,128)(2,1)S(1)}, bf16[288,128]{1,0:T(8,128)(2,1)S(1)}, u32[]{:S(2)}, u32[]{:S(2)}) %collective-permute-start.16) | collective-permute-done | bytes 73760 | tf_op jit(solution)/shard_map/ppermute | solution.py:625
  172.4 1.4 collective-permute-start.17
  173.8 3.4 %collective-permute-done.17 = bf16[400,128]{1,0:T(8,128)(2,1)S(1)} collective-permute-done((bf16[400,128]{1,0:T(8,128)(2,1)S(1)}, bf16[400,128]{1,0:T(8,128)(2,1)S(1)}, u32[]{:S(2)}, u32[]{:S(2)}) %collective-permute-start.17) | collective-permute-done | bytes 102432 | tf_op jit(solution)/shard_map/ppermute | solution.py:625
  177.2 3.0 %collective-permute-start.23 = (bf16[400,128]{1,0:T(8,128)(2,1)S(1)}, bf16[400,128]{1,0:T(8,128)(2,1)}, u32[]{:S(2)}, u32[]{:S(2)}) collective-permute-start(bf16[400,128]{1,0:T(8,128)(2,1)S(1)} %add_convert_fusion.5), channel_id=1, source_target_pairs={{0,6},{1,7},{2,4},{3,5},{4,2},{5,3},{6,0},{7,1},{8,14},{9,15},{10,... | collective-permute-start | bytes 307208 | tf_op jit(solution)/shard_map/ppermute | solution.py:625
  180.2 0.2 collective-permute-start.22
  180.5 1.2 collective-permute-start.18
  181.7 0.9 copy-done.4
  182.6 4.9 %unpack.2 = (f32[1024,128]{1,0:T(8,128)}, f32[128,4096]{1,0:T(8,128)}, f32[4096,128]{1,0:T(8,128)}, f32[128,1024]{1,0:T(8,128)}, f32[128,3072]{1,0:T(8,128)}) custom-call(bf16[3328,128]{1,0:T(8,128)(2,1)} %pad_maximum_fusion.refs_0_, bf16[3328,128]{1,0:T(8,128)(2,1)} %collective-permute-done.19.refs_1_, bf16[3328,128]{1,0:T(8,128)(2,1)} %copy-done.4, ...), custom_call_target="tpu_custom_call" | custom-call | flops 1 | bytes 1 | tf_op jit(solution)/shard_map/unpack/pallas_call | solution.py:653
  187.5 0.9 collective-permute-done.18
  188.4 1.0 add_convert_fusion.4
  189.5 1.5 collective-permute-start.24
  191.0 3.4 %collective-permute-done.24 = bf16[400,128]{1,0:T(8,128)(2,1)S(1)} collective-permute-done((bf16[400,128]{1,0:T(8,128)(2,1)S(1)}, bf16[400,128]{1,0:T(8,128)(2,1)S(1)}, u32[]{:S(2)}, u32[]{:S(2)}) %collective-permute-start.24) | collective-permute-done | bytes 102432 | tf_op jit(solution)/shard_map/ppermute | solution.py:625
  194.4 1.1 collective-permute-start.25
  195.6 5.1 %collective-permute-done.25.refs_1_ = bf16[800,128]{1,0:T(8,128)(2,1)S(1)} collective-permute-done((bf16[800,128]{1,0:T(8,128)(2,1)S(1)}, bf16[800,128]{1,0:T(8,128)(2,1)S(1)}, u32[]{:S(2)}, u32[]{:S(2)}) %collective-permute-start.25) | collective-permute-done | bytes 204832 | tf_op jit(solution)/shard_map/ppermute | solution.py:625
  200.7 1.4 collective-permute-done.27.refs_3_
  202.1 0.7 copy-done.9
  202.8 2.5 %unpack.3 = (f32[1024,128]{1,0:T(8,128)}, f32[1024,128]{1,0:T(8,128)}, f32[128,1024]{1,0:T(8,128)}, f32[8,128]{1,0:T(8,128)}, f32[8,128]{1,0:T(8,128)}, /*index=5*/f32[8,128]{1,0:T(8,128)}, f32[8,128]{1,0:T(8,128)}) custom-call(bf16[800,128]{1,0:T(8,128)(2,1)} %copy-done.5, bf16[800,128]{1,0:T(8,128)(2,1)} %copy-done.7, bf16[800,128]{1,0:T(8,128)(2,1)} %copy-done.8, ...), custom_call_target="tpu_custom_call" | custom-call | flops 1 | bytes 1 | tf_op jit(solution)/shard_map/unpack/pallas_call | solution.py:653
  (56 shorter events, 0.5 us)
Async XLA Ops:
  9.5 55.7 %all-to-all-start = ((bf16[8,2,4,128,128]{4,3,2,1,0:T(8,128)(2,1)}), bf16[8,2,4,128,128]{4,3,2,1,0:T(8,128)(2,1)}, u32[]{:S(2)}, u32[]{:S(2)}) async-start(bf16[8,2,4,128,128]{4,3,2,1,0:T(8,128)(2,1)} %get-tuple-element.61), calls=%async_computation | async-start | bytes 4194304 | tf_op jit(solution)/shard_map/all_to_all | solution.py:713
  37.7 4.7 %copy-start.2 = (bf16[10240,128]{1,0:T(8,128)(2,1)S(1)}, bf16[10240,128]{1,0:T(8,128)(2,1)}, u32[]{:S(2)}) copy-start(bf16[10240,128]{1,0:T(8,128)(2,1)} %get-tuple-element.68) | copy-start | bytes 7864324
  39.3 3.1 %collective-permute-start = (bf16[5120,128]{1,0:T(8,128)(2,1)S(1)}, bf16[5120,128]{1,0:T(8,128)(2,1)S(1)}, u32[]{:S(2)}, u32[]{:S(2)}) collective-permute-start(bf16[5120,128]{1,0:T(8,128)(2,1)S(1)} %slice.50), channel_id=1, source_target_pairs={{0,8},{1,9},{2,10},{3,11},{4,12},{5,13},{6,14},{7,15},{8,0},{9,1},... | collective-permute-start | bytes 3932168 | tf_op jit(solution)/shard_map/ppermute | solution.py:625
  42.7 1.1 copy-start
  44.7 28.3 %collective-permute-start.1 = (bf16[2560,128]{1,0:T(8,128)(2,1)}, bf16[2560,128]{1,0:T(8,128)(2,1)}, u32[]{:S(2)}, u32[]{:S(2)}) collective-permute-start(bf16[2560,128]{1,0:T(8,128)(2,1)} %slice.65), channel_id=1, source_target_pairs={{0,1},{1,0},{2,3},{3,2},{4,5},{5,4},{6,7},{7,6},{8,9},{9,8},{10,11... | collective-permute-start | bytes 1966088 | tf_op jit(solution)/shard_map/ppermute | solution.py:625
  72.9 21.4 %all-to-all-start.1 = ((bf16[8,256,128]{2,1,0:T(8,128)(2,1)}), bf16[8,256,128]{2,1,0:T(8,128)(2,1)}, u32[]{:S(2)}, u32[]{:S(2)}) async-start(bf16[8,256,128]{2,1,0:T(8,128)(2,1)} %get-tuple-element.66), calls=%async_computation.1 | async-start | bytes 1048576 | tf_op jit(solution)/shard_map/all_to_all | solution.py:736
  78.8 9.4 %copy-start.1 = (bf16[2560,128]{1,0:T(8,128)(2,1)}, bf16[2560,128]{1,0:T(8,128)(2,1)S(1)}, u32[]{:S(2)}) copy-start(bf16[2560,128]{1,0:T(8,128)(2,1)S(1)} %add_convert_fusion.1.keep_ref) | copy-start | bytes 1966084
  78.8 9.3 %collective-permute-start.2 = (bf16[1280,128]{1,0:T(8,128)(2,1)S(1)}, bf16[1280,128]{1,0:T(8,128)(2,1)}, u32[]{:S(2)}, u32[]{:S(2)}) collective-permute-start(bf16[1280,128]{1,0:T(8,128)(2,1)S(1)} %slice.66), channel_id=1, source_target_pairs={{0,16},{1,17},{2,18},{3,19},{4,20},{5,21},{6,22},{7,23},{8,24},{9,... | collective-permute-start | bytes 983048 | tf_op jit(solution)/shard_map/ppermute | solution.py:625
  90.0 13.7 %collective-permute-start.5 = (bf16[320,128]{1,0:T(8,128)(2,1)}, bf16[320,128]{1,0:T(8,128)(2,1)}, u32[]{:S(2)}, u32[]{:S(2)}) collective-permute-start(bf16[320,128]{1,0:T(8,128)(2,1)} %get-tuple-element.75), channel_id=1, source_target_pairs={{0,6},{1,7},{2,4},{3,5},{4,2},{5,3},{6,0},{7,1},{8,14},{9,15},{10,... | collective-permute-start | bytes 245768 | tf_op jit(solution)/shard_map/ppermute | solution.py:625
  93.5 10.2 %collective-permute-start.4 = (bf16[320,128]{1,0:T(8,128)(2,1)}, bf16[320,128]{1,0:T(8,128)(2,1)}, u32[]{:S(2)}, u32[]{:S(2)}) collective-permute-start(bf16[320,128]{1,0:T(8,128)(2,1)} %get-tuple-element.74), channel_id=1, source_target_pairs={{0,2},{1,3},{2,0},{3,1},{4,6},{5,7},{6,4},{7,5},{8,10},{9,11},{10,... | collective-permute-start | bytes 245768 | tf_op jit(solution)/shard_map/ppermute | solution.py:625
  93.5 10.2 %collective-permute-start.3 = (bf16[320,128]{1,0:T(8,128)(2,1)}, bf16[320,128]{1,0:T(8,128)(2,1)}, u32[]{:S(2)}, u32[]{:S(2)}) collective-permute-start(bf16[320,128]{1,0:T(8,128)(2,1)} %get-tuple-element.73), channel_id=1, source_target_pairs={{0,4},{1,5},{2,6},{3,7},{4,0},{5,1},{6,2},{7,3},{8,12},{9,13},{10,... | collective-permute-start | bytes 245768 | tf_op jit(solution)/shard_map/ppermute | solution.py:625
  94.4 20.3 %all-to-all-start.2 = ((bf16[8,2,128,128]{3,2,1,0:T(8,128)(2,1)}), bf16[8,2,128,128]{3,2,1,0:T(8,128)(2,1)}, u32[]{:S(2)}, u32[]{:S(2)}) async-start(bf16[8,2,128,128]{3,2,1,0:T(8,128)(2,1)} %get-tuple-element.76), calls=%async_computation.2 | async-start | bytes 1048576 | tf_op jit(solution)/shard_map/all_to_all | solution.py:717
  100.0 6.7 %copy-start.10 = (bf16[320,128]{1,0:T(8,128)(2,1)S(1)}, bf16[320,128]{1,0:T(8,128)(2,1)}, u32[]{:S(2)}) copy-start(bf16[320,128]{1,0:T(8,128)(2,1)} %get-tuple-element.72) | copy-start | bytes 245764
  103.7 1.2 collective-permute-start.6
  105.7 3.9 %collective-permute-start.7 = (bf16[96,128]{1,0:T(8,128)(2,1)S(1)}, bf16[96,128]{1,0:T(8,128)(2,1)S(1)}, u32[]{:S(2)}, u32[]{:S(2)}) collective-permute-start(bf16[96,128]{1,0:T(8,128)(2,1)S(1)} %slice.70), channel_id=1, source_target_pairs={{0,16},{1,17},{2,18},{3,19},{4,20},{5,21},{6,22},{7,23},{8,24},{9,... | collective-permute-start | bytes 73736 | tf_op jit(solution)/shard_map/ppermute | solution.py:625
  110.3 15.1 %collective-permute-start.8 = (bf16[416,128]{1,0:T(8,128)(2,1)}, bf16[416,128]{1,0:T(8,128)(2,1)}, u32[]{:S(2)}, u32[]{:S(2)}) collective-permute-start(bf16[416,128]{1,0:T(8,128)(2,1)} %pad_maximum_fusion.2.refs_0_), channel_id=1, source_target_pairs={{0,4},{1,5},{2,6},{3,7},{4,0},{5,1},{6,2},{7,3},{8,12},{9,13},{10,... | collective-permute-start | bytes 319496 | tf_op jit(solution)/shard_map/ppermute | solution.py:625
  113.2 12.2 %collective-permute-start.9 = (bf16[416,128]{1,0:T(8,128)(2,1)}, bf16[416,128]{1,0:T(8,128)(2,1)}, u32[]{:S(2)}, u32[]{:S(2)}) collective-permute-start(bf16[416,128]{1,0:T(8,128)(2,1)} %pad_maximum_fusion.2.refs_0_), channel_id=1, source_target_pairs={{0,2},{1,3},{2,0},{3,1},{4,6},{5,7},{6,4},{7,5},{8,10},{9,11},{10,... | collective-permute-start | bytes 319496 | tf_op jit(solution)/shard_map/ppermute | solution.py:625
  114.7 10.7 %collective-permute-start.10 = (bf16[416,128]{1,0:T(8,128)(2,1)}, bf16[416,128]{1,0:T(8,128)(2,1)}, u32[]{:S(2)}, u32[]{:S(2)}) collective-permute-start(bf16[416,128]{1,0:T(8,128)(2,1)} %pad_maximum_fusion.2.refs_0_), channel_id=1, source_target_pairs={{0,6},{1,7},{2,4},{3,5},{4,2},{5,3},{6,0},{7,1},{8,14},{9,15},{10,... | collective-permute-start | bytes 319496 | tf_op jit(solution)/shard_map/ppermute | solution.py:625
  114.7 42.2 %all-to-all-start.3 = ((bf16[8,2,3,128,128]{4,3,2,1,0:T(8,128)(2,1)}), bf16[8,2,3,128,128]{4,3,2,1,0:T(8,128)(2,1)}, u32[]{:S(2)}, u32[]{:S(2)}) async-start(bf16[8,2,3,128,128]{4,3,2,1,0:T(8,128)(2,1)} %get-tuple-element.88.rest_ref), calls=%async_computation.3 | async-start | bytes 3145728 | tf_op jit(solution)/shard_map/all_to_all | solution.py:717
  127.2 17.5 %copy-start.3 = (bf16[1664,128]{1,0:T(8,128)(2,1)S(1)}, bf16[1664,128]{1,0:T(8,128)(2,1)}, u32[]{:S(2)}) copy-start(bf16[1664,128]{1,0:T(8,128)(2,1)} %join.1) | copy-start | bytes 1277956
  127.2 17.5 %collective-permute-start.11 = (bf16[1664,128]{1,0:T(8,128)(2,1)}, bf16[1664,128]{1,0:T(8,128)(2,1)S(1)}, u32[]{:S(2)}, u32[]{:S(2)}) collective-permute-start(bf16[1664,128]{1,0:T(8,128)(2,1)} %join.1), channel_id=1, source_target_pairs={{0,16},{1,17},{2,18},{3,19},{4,20},{5,21},{6,22},{7,23},{8,24},{9,... | collective-permute-start | bytes 1277960 | tf_op jit(solution)/shard_map/ppermute | solution.py:625
  129.3 10.9 %collective-permute-start.14 = (bf16[512,128]{1,0:T(8,128)(2,1)S(1)}, bf16[512,128]{1,0:T(8,128)(2,1)S(1)}, u32[]{:S(2)}, u32[]{:S(2)}) collective-permute-start(bf16[512,128]{1,0:T(8,128)(2,1)S(1)} %get-tuple-element.109), channel_id=1, source_target_pairs={{0,24},{1,25},{2,26},{3,27},{4,28},{5,29},{6,30},{7,31},{8,16},{9,... | collective-permute-start | bytes 393224 | tf_op jit(solution)/shard_map/ppermute | solution.py:625
  129.3 10.8 %collective-permute-start.13 = (bf16[512,128]{1,0:T(8,128)(2,1)S(1)}, bf16[512,128]{1,0:T(8,128)(2,1)S(1)}, u32[]{:S(2)}, u32[]{:S(2)}) collective-permute-start(bf16[512,128]{1,0:T(8,128)(2,1)S(1)} %get-tuple-element.110), channel_id=1, source_target_pairs={{0,8},{1,9},{2,10},{3,11},{4,12},{5,13},{6,14},{7,15},{8,0},{9,1},... | collective-permute-start | bytes 393224 | tf_op jit(solution)/shard_map/ppermute | solution.py:625
  130.5 12.6 %collective-permute-start.12 = (bf16[512,128]{1,0:T(8,128)(2,1)S(1)}, bf16[512,128]{1,0:T(8,128)(2,1)S(1)}, u32[]{:S(2)}, u32[]{:S(2)}) collective-permute-start(bf16[512,128]{1,0:T(8,128)(2,1)S(1)} %get-tuple-element.108), channel_id=1, source_target_pairs={{0,16},{1,17},{2,18},{3,19},{4,20},{5,21},{6,22},{7,23},{8,24},{9,... | collective-permute-start | bytes 393224 | tf_op jit(solution)/shard_map/ppermute | solution.py:625
  145.7 23.7 %collective-permute-start.19 = (bf16[3328,128]{1,0:T(8,128)(2,1)}, bf16[3328,128]{1,0:T(8,128)(2,1)}, u32[]{:S(2)}, u32[]{:S(2)}) collective-permute-start(bf16[3328,128]{1,0:T(8,128)(2,1)} %pad_maximum_fusion.refs_0_), channel_id=1, source_target_pairs={{0,1},{1,0},{2,3},{3,2},{4,5},{5,4},{6,7},{7,6},{8,9},{9,8},{10,11... | collective-permute-start | bytes 2555912 | tf_op jit(solution)/shard_map/ppermute | solution.py:625
  156.8 12.4 %copy-start.6 = (bf16[512,128]{1,0:T(8,128)(2,1)S(1)}, bf16[512,128]{1,0:T(8,128)(2,1)}, u32[]{:S(2)}) copy-start(bf16[512,128]{1,0:T(8,128)(2,1)} %add_convert_fusion.3) | copy-start | bytes 393220
  165.3 1.6 collective-permute-start.15
  168.0 4.4 %collective-permute-start.16 = (bf16[288,128]{1,0:T(8,128)(2,1)S(1)}, bf16[288,128]{1,0:T(8,128)(2,1)S(1)}, u32[]{:S(2)}, u32[]{:S(2)}) collective-permute-start(bf16[288,128]{1,0:T(8,128)(2,1)S(1)} %slice.72), channel_id=1, source_target_pairs={{0,16},{1,17},{2,18},{3,19},{4,20},{5,21},{6,22},{7,23},{8,24},{9,... | collective-permute-start | bytes 221192 | tf_op jit(solution)/shard_map/ppermute | solution.py:625
  169.3 12.4 %collective-permute-start.20 = (bf16[3328,128]{1,0:T(8,128)(2,1)}, bf16[3328,128]{1,0:T(8,128)(2,1)S(1)}, u32[]{:S(2)}, u32[]{:S(2)}) collective-permute-start(bf16[3328,128]{1,0:T(8,128)(2,1)} %pad_maximum_fusion.refs_0_), channel_id=1, source_target_pairs={{0,8},{1,9},{2,10},{3,11},{4,12},{5,13},{6,14},{7,15},{8,0},{9,1},... | collective-permute-start | bytes 2555912 | tf_op jit(solution)/shard_map/ppermute | solution.py:625
  169.4 12.3 %collective-permute-start.21 = (bf16[3328,128]{1,0:T(8,128)(2,1)}, bf16[3328,128]{1,0:T(8,128)(2,1)}, u32[]{:S(2)}, u32[]{:S(2)}) collective-permute-start(bf16[3328,128]{1,0:T(8,128)(2,1)} %collective-permute-done.19.refs_1_), channel_id=1, source_target_pairs={{0,8},{1,9},{2,10},{3,11},{4,12},{5,13},{6,14},{7,15},{8,0},{9,1},... | collective-permute-start | bytes 2555912 | tf_op jit(solution)/shard_map/ppermute | solution.py:625
  172.4 4.7 %collective-permute-start.17 = (bf16[400,128]{1,0:T(8,128)(2,1)S(1)}, bf16[400,128]{1,0:T(8,128)(2,1)S(1)}, u32[]{:S(2)}, u32[]{:S(2)}) collective-permute-start(bf16[400,128]{1,0:T(8,128)(2,1)S(1)} %pad_maximum_fusion.3), channel_id=1, source_target_pairs={{0,1},{1,0},{2,3},{3,2},{4,5},{5,4},{6,7},{7,6},{8,9},{9,8},{10,11... | collective-permute-start | bytes 307208 | tf_op jit(solution)/shard_map/ppermute | solution.py:625
  177.2 10.3 %collective-permute-start.23 = (bf16[400,128]{1,0:T(8,128)(2,1)S(1)}, bf16[400,128]{1,0:T(8,128)(2,1)}, u32[]{:S(2)}, u32[]{:S(2)}) collective-permute-start(bf16[400,128]{1,0:T(8,128)(2,1)S(1)} %add_convert_fusion.5), channel_id=1, source_target_pairs={{0,6},{1,7},{2,4},{3,5},{4,2},{5,3},{6,0},{7,1},{8,14},{9,15},{10,... | collective-permute-start | bytes 307208 | tf_op jit(solution)/shard_map/ppermute | solution.py:625
  180.2 7.3 %collective-permute-start.22 = (bf16[400,128]{1,0:T(8,128)(2,1)S(1)}, bf16[400,128]{1,0:T(8,128)(2,1)}, u32[]{:S(2)}, u32[]{:S(2)}) collective-permute-start(bf16[400,128]{1,0:T(8,128)(2,1)S(1)} %add_convert_fusion.5), channel_id=1, source_target_pairs={{0,2},{1,3},{2,0},{3,1},{4,6},{5,7},{6,4},{7,5},{8,10},{9,11},{10,... | collective-permute-start | bytes 307208 | tf_op jit(solution)/shard_map/ppermute | solution.py:625
  180.5 8.0 %collective-permute-start.18 = (bf16[400,128]{1,0:T(8,128)(2,1)S(1)}, bf16[400,128]{1,0:T(8,128)(2,1)}, u32[]{:S(2)}, u32[]{:S(2)}) collective-permute-start(bf16[400,128]{1,0:T(8,128)(2,1)S(1)} %add_convert_fusion.5), channel_id=1, source_target_pairs={{0,4},{1,5},{2,6},{3,7},{4,0},{5,1},{6,2},{7,3},{8,12},{9,13},{10,... | collective-permute-start | bytes 307208 | tf_op jit(solution)/shard_map/ppermute | solution.py:625
  181.7 0.9 copy-start.4
  189.5 4.9 %collective-permute-start.24 = (bf16[400,128]{1,0:T(8,128)(2,1)S(1)}, bf16[400,128]{1,0:T(8,128)(2,1)S(1)}, u32[]{:S(2)}, u32[]{:S(2)}) collective-permute-start(bf16[400,128]{1,0:T(8,128)(2,1)S(1)} %add_convert_fusion.4), channel_id=1, source_target_pairs={{0,1},{1,0},{2,3},{3,2},{4,5},{5,4},{6,7},{7,6},{8,9},{9,8},{10,11... | collective-permute-start | bytes 307208 | tf_op jit(solution)/shard_map/ppermute | solution.py:625
  194.4 7.7 %copy-start.5 = (bf16[800,128]{1,0:T(8,128)(2,1)}, bf16[800,128]{1,0:T(8,128)(2,1)S(1)}, u32[]{:S(2)}) copy-start(bf16[800,128]{1,0:T(8,128)(2,1)S(1)} %pad_maximum_fusion.1.refs_0_) | copy-start | bytes 614404
  194.4 6.3 %collective-permute-start.25 = (bf16[800,128]{1,0:T(8,128)(2,1)S(1)}, bf16[800,128]{1,0:T(8,128)(2,1)S(1)}, u32[]{:S(2)}, u32[]{:S(2)}) collective-permute-start(bf16[800,128]{1,0:T(8,128)(2,1)S(1)} %pad_maximum_fusion.1.refs_0_), channel_id=1, source_target_pairs={{0,16},{1,17},{2,18},{3,19},{4,20},{5,21},{6,22},{7,23},{8,24},{9,... | collective-permute-start | bytes 614408 | tf_op jit(solution)/shard_map/ppermute | solution.py:625
  195.6 5.1 %collective-permute-start.26 = (bf16[800,128]{1,0:T(8,128)(2,1)S(1)}, bf16[800,128]{1,0:T(8,128)(2,1)S(1)}, u32[]{:S(2)}, u32[]{:S(2)}) collective-permute-start(bf16[800,128]{1,0:T(8,128)(2,1)S(1)} %pad_maximum_fusion.1.refs_0_), channel_id=1, source_target_pairs={{0,8},{1,9},{2,10},{3,11},{4,12},{5,13},{6,14},{7,15},{8,0},{9,1},... | collective-permute-start | bytes 614408 | tf_op jit(solution)/shard_map/ppermute | solution.py:625
  200.7 1.5 copy-start.7
  200.7 1.5 collective-permute-start.27
  200.7 1.5 copy-start.8
  202.1 0.7 copy-start.9
